TPU v7x, 256 devices: a whole 4x4x8 slice. The times are simulated.
256 devices in a mesh: dom: 64 (over z_hi, x, y), inner: 4 (over z_lo, core).
Axes of the slice: x: 4, y: 4, z: 8 (z_hi: 4, z_lo: 2; z = z_hi * 2 + z_lo), core: 2. Of those that a mesh axis runs over, the one named last changes fastest.
Arguments:
- features: bfloat16 [32768, 128], P(('dom', 'inner')), may hold values from -200 to 200
- adjacency: bfloat16 [32768, 32768], P(('dom', 'inner')), may hold values from 0 to 3, as said below
- tile_mask: int32 [256, 64], P(('dom', 'inner')), may hold values 0 or 1
- skip_owner: int32 [64], replicated, may hold values 0 or 1
- weight: bfloat16 [128, 256], replicated, may hold values from -0.5 to 0.5
- bias: float32 [256], replicated, may hold values from -3 to 3
- cotangent: bfloat16 [32768, 256], P(('dom', 'inner')), may hold values from -6 to 6
Outputs:
- activated: bfloat16 [32768, 256], P(('dom', 'inner'))
- grad_weight: float32 [128, 256], replicated
- grad_bias: float32 [256], replicated
Inputs may be any that keep to these rules, and one draw needn't show every extreme that they name: `adjacency`: edge weights are 0 or between 0.1 and 3; each row has some 32 nonzero entries on average, spread over all partitions.
All inputs are finite; a program needn't handle non-finite values. Where the computation divides by a largest or mean magnitude, that divisor is 1e-20 or more. No bound on the sum of `tile_mask` on one device may be relied on, other than what follows from the above.
Results may differ from a plain program's by a relative error of at most 0.0064.
Values may be sent and summed in bfloat16 or wider, within the bound.
No kernel may reach another device: no remote copies, remote signals or barrier semaphores. Data moves between devices by JAX's collectives and lax.ppermute only.
A program may use at most 64 MiB of HBM per device.

v0:
```python
import jax
import jax.numpy as jnp
from jax import lax
from jax.sharding import PartitionSpec as P


def silu_slope(values):
    sigma = jax.nn.sigmoid(values)
    return sigma * (1.0 + values * (1.0 - sigma))


def local(features, adjacency, tile_mask, skip_owner, weight, bias, cotangent):
    node_count = features.shape[0]
    part_nodes = node_count * lax.axis_size("inner")
    wide = features.astype(jnp.float32)
    shared = lax.pmax(jnp.max(jnp.abs(wide)), ("dom", "inner")) + 1e-06
    factor = 64.0 / shared
    scaled = (wide * factor).astype(jnp.bfloat16)
    live_tiles = tile_mask[0] * (1 - skip_owner)
    live_cols = jnp.repeat(live_tiles, part_nodes).astype(jnp.bfloat16)
    masked = adjacency * live_cols[None, :]
    degree = 1.0 + jnp.sum(masked.astype(jnp.float32), axis=1)
    summed = jnp.dot(
        masked,
        lax.all_gather(scaled, ("dom", "inner"), axis=0, tiled=True),
        preferred_element_type=jnp.float32,
    )
    mixed = ((summed + scaled.astype(jnp.float32)) / degree[:, None]).astype(jnp.bfloat16)
    pre = jnp.dot(mixed, weight, preferred_element_type=jnp.float32) + bias[None, :]
    activated = jax.nn.silu(pre).astype(jnp.bfloat16)
    delta = cotangent.astype(jnp.float32) * silu_slope(pre)
    delta_low = delta.astype(jnp.bfloat16)
    local_weight = lax.dot_general(
        mixed, delta_low, (((0,), (0,)), ((), ())), preferred_element_type=jnp.float32
    )
    local_bias = jnp.sum(delta, axis=0)
    grad_weight, grad_bias = lax.psum((local_weight, local_bias), ("dom", "inner"))
    return (activated, grad_weight, grad_bias)


def solution(mesh):
    return jax.shard_map(
        local,
        mesh=mesh,
        in_specs=(
            P(("dom", "inner"), None),
            P(("dom", "inner"), None),
            P(("dom", "inner"), None),
            P(),
            P(),
            P(),
            P(("dom", "inner"), None),
        ),
        out_specs=(P(("dom", "inner"), None), P(), P()),
        check_vma=False,
    )
```

profile of v0, /device:TPU:1, one launch (start us, length us, event | category | flops | bytes accessed | tf_op | source)
XLA Modules:
  0.0 763.8 jit_solution(16653864483207517237)
XLA Ops:
  7.2 0.0 copy-start
  7.2 0.0 all-gather.2.cloned.1.call-start
  7.2 1.4 fusion.12
  8.6 81.4 %pmax.7 = f32[]{:T(128)} all-reduce(f32[]{:T(128)} %fusion.12), channel_id=1, replica_groups=mesh['dom'=64,'inner'=4] {'dom','inner'}, use_global_device_ids=true, to_apply=%region_1.0 | all-reduce | flops 1 | bytes 8 | tf_op jit(solution)/shard_map/pmax | solution.py:16
  90.7 1.4 fusion.13
  92.1 0.0 copy-start.1
  92.1 0.0 all-gather.2.cloned.1.call-update
  92.1 0.0 all-reduce.2.cloned.1.call-start
  92.1 0.7 fusion.16
  92.8 0.1 broadcast_bitcast_fusion
  92.9 5.1 convert_reduce_fusion
  98.0 0.0 copy-start.2
  98.1 0.0 copy-start.3
  98.1 408.1 %all-gather.2.cloned.1.call-done = bf16[32768,128]{1,0:T(8,128)(2,1)} async-done(((bf16[128,128]{1,0:T(8,128)(2,1)}), bf16[32768,128]{1,0:T(8,128)(2,1)}) %all-gather.2.cloned.1.call-update) | async-done | bytes 8388624 | tf_op jit(solution)/shard_map/all_gather | solution.py:25
  506.2 0.0 copy-done.1
  506.2 8.1 %fusion.9 = bf16[128,128]{1,0:T(8,128)(2,1)S(1)} fusion(bf16[32768,128]{1,0:T(8,128)(2,1)} %all-gather.2.cloned.1.call-done, bf16[128,32768]{1,0:T(8,128)(2,1)} %param.8, bf16[32768]{0:T(1024)(128)(2,1)S(1)} %bitcast.12, bf16[128,128]{1,0:T(8,128)(2,1)S(1)} %copy-done.1, f32[128]{0:T(128)S(1)} %broadcast_add_fusion), kind=kOutput, calls=%fused_computation.7 | convolution fusion | flops 1078001664 | bytes 16908800 | tf_op jit(solution)/shard_map/dot_general | solution.py:23
  514.3 0.0 copy-done
  514.3 0.0 copy-done.2
  514.3 0.0 copy-done.3
  514.3 0.8 fusion.17
  515.2 0.8 fusion.14
  516.0 0.0 all-reduce.2.cloned.1.call-update
  516.0 76.0 %psum.15 = f32[256]{0:T(256)} all-reduce(f32[256]{0:T(256)S(1)} %get-tuple-element.3), channel_id=1, replica_groups=mesh['dom'=64,'inner'=4] {'dom','inner'}, use_global_device_ids=true, to_apply=%region_5.6 | all-reduce | flops 256 | bytes 2048 | tf_op jit(solution)/shard_map/psum | solution.py:37
  592.0 163.3 %all-reduce.2.cloned.1.call-done = f32[128,256]{1,0:T(8,128)} async-done(((f32[128,256]{1,0:T(8,128)}), f32[128,256]{1,0:T(8,128)}) %all-reduce.2.cloned.1.call-update) | async-done | bytes 131088 | tf_op jit(solution)/shard_map/psum | solution.py:37
  755.4 1.6 copy.12
  (2 shorter events, 0.0 us)
Async XLA Ops:
  7.2 507.1 %copy-start = (bf16[128,256]{1,0:T(8,128)(2,1)S(1)}, bf16[128,256]{1,0:T(8,128)(2,1)}, u32[]{:S(2)}) copy-start(bf16[128,256]{1,0:T(8,128)(2,1)} %param.11) | copy-start | bytes 196612
  7.2 499.0 %all-gather.2.cloned.1.call-start = ((), (), s32[]{:S(2)}) async-start(), calls=%async_computation | async-start | bytes 8421376 | tf_op jit(solution)/shard_map/all_gather | solution.py:25
  92.1 414.1 %copy-start.1 = (bf16[128,128]{1,0:T(8,128)(2,1)S(1)}, bf16[128,128]{1,0:T(8,128)(2,1)}, u32[]{:S(2)}) copy-start(bf16[128,128]{1,0:T(8,128)(2,1)} %fusion.13) | copy-start | bytes 98308
  92.1 663.3 %all-reduce.2.cloned.1.call-start = ((), (), s32[]{:S(2)}) async-start(), calls=%async_computation.1 | async-start | bytes 262144 | tf_op jit(solution)/shard_map/psum | solution.py:37
  98.0 416.3 %copy-start.2 = (bf16[128,256]{1,0:T(8,128)(2,1)S(1)}, bf16[128,256]{1,0:T(8,128)(2,1)}, u32[]{:S(2)}) copy-start(bf16[128,256]{1,0:T(8,128)(2,1)} %param.13) | copy-start | bytes 196612
  98.1 416.3 %copy-start.3 = (f32[256]{0:T(256)S(1)}, f32[256]{0:T(256)}, u32[]{:S(2)}) copy-start(f32[256]{0:T(256)} %param.12) | copy-start | bytes 3076
Sparse Core Ops, SparseCore 0:
  92.2 413.9 all-gather.1
  516.2 239.1 all-reduce.1
where the time goes:
time: 765 us; the launch traced here: 764 us
  waiting for transfers between devices  571 us (75%)
  blocking collectives  157 us (21%)
  between operations  14.8 us (2%)
  matrix products  9.79 us (1%)
  other arithmetic  8.55 us (1%)
    all_gather x1, waiting for transfers between devices, local(): lax.all_gather(scaled, ('dom', 'inner'), axis=0, tiled=True)  408 us
    psum x1, waiting for transfers between devices, local(): lax.psum((local_weight, local_bias), ('dom', 'inner'))  163 us
    pmax x1, blocking collectives, local(): shared = lax.pmax(jnp.max(jnp.abs(wide)), ('dom', 'inner')) + 1e-06  81.4 us
    psum x1, blocking collectives, local(): lax.psum((local_weight, local_bias), ('dom', 'inner'))  76 us
  transfers between devices with their start and end apart: 2, of which 2 were waited for; matrix products, arithmetic and copies ran while one was open for 1% of the time, Pallas kernels for 0%

commit v1 on v0

v1 whole, which is shorter than its diff:
```python
import jax
import jax.numpy as jnp
from jax import lax
from jax.experimental import pallas as pl
from jax.experimental.pallas import tpu as pltpu
from jax.sharding import Mesh, PartitionSpec as P

NAMES = ("zh", "x", "y", "zl", "core")
SIZES = (4, 4, 4, 2, 2)
XY = ("x", "y")
ZC = ("zh", "zl", "core")
SHIFTS = (0, 1, 3, 2)
PIECES = 8
PIECE = 4096
BLOCKS = PIECE // 128
VMEM_LIMIT = 60 * 1024 * 1024


def index_of(zh, x, y, zl, core):
    return (((zh * 4 + x) * 4 + y) * 2 + zl) * 2 + core


def coords():
    return [
        (zh, x, y, zl, core)
        for zh in range(4)
        for x in range(4)
        for y in range(4)
        for zl in range(2)
        for core in range(2)
    ]


def permute(array, move):
    return lax.ppermute(array, NAMES, [(index_of(*at), index_of(*move(*at))) for at in coords()])


def swap_cores(array):
    return permute(array, lambda zh, x, y, zl, core: (zh, x, y, zl, 1 - core))


def along_z(array, step):
    def move(zh, x, y, zl, core):
        z = zh * 2 + zl
        if core == 0:
            z = (z + step) % 8 if step < 4 else z
        else:
            z = (z - step) % 8
        return z // 2, x, y, z % 2, core

    return permute(array, move)


def along_xy(array, step, turned):
    def move(zh, x, y, zl, core):
        if (core == 0) != turned:
            return zh, (x + step) % 4, y, zl, core
        return zh, x, (y + step) % 4, zl, core

    return permute(array, move)


def block_table():
    zh, x, y, zl, core = (lax.axis_index(n) for n in NAMES)
    z = zh * 2 + zl
    place = lax.iota(jnp.int32, PIECES * BLOCKS)
    piece, within = place >> 5, place & 31

    def shift_of(slot):
        return jnp.where(slot == 2, 3, jnp.where(slot == 3, 2, slot))

    outer, half = shift_of(piece >> 1), piece & 1
    inner, hop, pair = shift_of(within >> 3), (within >> 1) & 3, within & 1
    plane = core ^ half
    first = plane == 0
    at_x = (x - jnp.where(first, inner, outer)) & 3
    at_y = (y - jnp.where(first, outer, inner)) & 3
    at_z = (z + jnp.where(first, -hop, jnp.where(hop == 0, 4, hop))) & 7
    return index_of(at_z >> 1, at_x, at_y, at_z & 1, pair ^ plane)


def order_kernel(table, tile_mask, skip_owner, adjacency, *outs):
    pieces, degree = outs[:PIECES], outs[PIECES]
    total = jnp.zeros((128, 128), jnp.float32)
    for number, out in enumerate(pieces):

        def one_block(block, total, number=number, out=out):
            source = table[number * BLOCKS + block]
            owner = source >> 2
            live = tile_mask[0, owner] * (1 - skip_owner[owner])
            values = adjacency[:, pl.ds(pl.multiple_of(source * 128, 128), 128)]
            values = values * jnp.full((1, 1), live.astype(jnp.float32)).astype(jnp.bfloat16)
            out[:, pl.ds(pl.multiple_of(block * 128, 128), 128)] = values
            return total + values.astype(jnp.float32)

        total = lax.fori_loop(0, BLOCKS, one_block, total)
    degree[...] = jnp.broadcast_to(1.0 + jnp.sum(total, axis=1, keepdims=True), (128, 128))


def order_adjacency(table, tile_mask, skip_owner, adjacency):
    smem = pl.BlockSpec(memory_space=pltpu.SMEM)
    vmem = pl.BlockSpec(memory_space=pltpu.VMEM)
    return pl.pallas_call(
        order_kernel,
        out_shape=[jax.ShapeDtypeStruct((128, PIECE), jnp.bfloat16)] * PIECES
        + [jax.ShapeDtypeStruct((128, 128), jnp.float32)],
        in_specs=[smem, smem, smem, vmem],
        out_specs=[vmem] * (PIECES + 1),
        compiler_params=pltpu.CompilerParams(vmem_limit_bytes=VMEM_LIMIT),
        cost_estimate=pl.CostEstimate(flops=2 * 128 * 32768, bytes_accessed=4 * 128 * 32768, transcendentals=0),
    )(table, tile_mask, skip_owner, adjacency)


def add_piece(adj, feat, total, largest):
    for start in range(0, PIECE, 512):
        rows = feat[start : start + 512, :]
        total = total + jnp.dot(adj[:, start : start + 512], rows, preferred_element_type=jnp.float32)
        largest = jnp.maximum(largest, jnp.max(jnp.abs(rows).reshape(32, 16, 128), axis=0))
    return total, largest


def piece_kernel(adj_a, adj_b, feat_a, feat_b, total_in, largest_in, total_out, largest_out):
    total, largest = add_piece(adj_a, feat_a, total_in[...], largest_in[...])
    total, largest = add_piece(adj_b, feat_b, total, largest)
    total_out[...] = total
    largest_out[...] = largest


def piece_step(adj_a, adj_b, feat_a, feat_b, total, largest):
    vmem = pl.BlockSpec(memory_space=pltpu.VMEM)
    return pl.pallas_call(
        piece_kernel,
        out_shape=[
            jax.ShapeDtypeStruct((128, 128), jnp.float32),
            jax.ShapeDtypeStruct((16, 128), jnp.bfloat16),
        ],
        in_specs=[vmem] * 6,
        out_specs=[vmem] * 2,
        compiler_params=pltpu.CompilerParams(vmem_limit_bytes=VMEM_LIMIT // 4),
        cost_estimate=pl.CostEstimate(
            flops=4 * 128 * PIECE * 128, bytes_accessed=8 * 128 * PIECE, transcendentals=0
        ),
    )(adj_a, adj_b, feat_a, feat_b, total, largest)


def last_kernel(
    adj_a, adj_b, feat_a, feat_b, total_in, largest_in, own, degree, weight, bias, cotangent, activated, grads
):
    total, largest = add_piece(adj_a, feat_a, total_in[...], largest_in[...])
    total, largest = add_piece(adj_b, feat_b, total, largest)
    factor = 64.0 / (jnp.max(largest.astype(jnp.float32)) + 1e-06)
    summed = (total + own[...].astype(jnp.float32)) * factor
    mixed = (summed / degree[...]).astype(jnp.bfloat16)
    pre = jnp.dot(mixed, weight[...], preferred_element_type=jnp.float32) + bias[...]
    sigma = jax.nn.sigmoid(pre)
    activated[...] = (pre * sigma).astype(jnp.bfloat16)
    delta = cotangent[...].astype(jnp.float32) * (sigma * (1.0 + pre * (1.0 - sigma)))
    grad_weight = lax.dot_general(
        mixed, delta.astype(jnp.bfloat16), (((0,), (0,)), ((), ())), preferred_element_type=jnp.float32
    )
    grad_bias = jnp.sum(delta, axis=0, keepdims=True)
    grads[:, :, :256] = grad_weight.reshape(16, 8, 256)
    row = lax.broadcasted_iota(jnp.int32, (8, 128), 0)
    side = jnp.where(row == 0, grad_bias[:, :128], jnp.where(row == 1, grad_bias[:, 128:], 0.0))
    grads[:, :, 256:] = jnp.broadcast_to(side[None], (16, 8, 128))


def last_step(*args):
    vmem = pl.BlockSpec(memory_space=pltpu.VMEM)
    return pl.pallas_call(
        last_kernel,
        out_shape=[
            jax.ShapeDtypeStruct((128, 256), jnp.bfloat16),
            jax.ShapeDtypeStruct((16, 8, 384), jnp.float32),
        ],
        in_specs=[vmem] * 11,
        out_specs=[vmem] * 2,
        compiler_params=pltpu.CompilerParams(vmem_limit_bytes=VMEM_LIMIT // 4),
        cost_estimate=pl.CostEstimate(
            flops=4 * 128 * PIECE * 128, bytes_accessed=8 * 128 * PIECE, transcendentals=32768
        ),
    )(*args)


def sum_kernel(parts, out):
    out[...] = jnp.broadcast_to(jnp.sum(parts[...], axis=0)[None], out.shape)


def sum_last_kernel(parts, weight_out, bias_out):
    total = jnp.sum(parts[...], axis=0)
    weight_out[...] = jnp.broadcast_to(total[None, :, :256], weight_out.shape)
    bias_out[:, :128] = total[0:1, 256:]
    bias_out[:, 128:] = total[1:2, 256:]


def sum_over_devices(grads):
    part = lax.all_to_all(grads, XY, 0, 0, tiled=True)
    part = pl.pallas_call(sum_kernel, out_shape=jax.ShapeDtypeStruct((16, 8, 384), jnp.float32))(part)
    part = lax.all_to_all(part, ZC, 0, 0, tiled=True)
    part, grad_bias = pl.pallas_call(
        sum_last_kernel,
        out_shape=[
            jax.ShapeDtypeStruct((16, 8, 256), jnp.float32),
            jax.ShapeDtypeStruct((1, 256), jnp.float32),
        ],
    )(part)
    grad_weight = lax.all_to_all(part, XY, 0, 0, tiled=True).reshape(128, 256)
    return grad_weight, grad_bias.reshape(256)


def local(features, adjacency, tile_mask, skip_owner, weight, bias, cotangent):
    ordered = order_adjacency(block_table(), tile_mask, skip_owner, adjacency)
    adj, degree = ordered[:PIECES], ordered[PIECES]
    chip = jnp.concatenate([features, swap_cores(features)])
    far = along_z(chip, 4)
    line = jnp.concatenate([far] + [along_z(chip, step) for step in (3, 2, 1)][::-1])
    plane = jnp.concatenate([line] + [along_xy(line, step, False) for step in SHIFTS[1:]])
    mine = [plane] + [along_xy(plane, step, True) for step in SHIFTS[1:]]
    total = jnp.zeros((128, 128), jnp.float32)
    largest = jnp.zeros((16, 128), jnp.bfloat16)
    for number in range(3):
        feats = mine[number], swap_cores(mine[number])
        total, largest = piece_step(*adj[2 * number : 2 * number + 2], *feats, total, largest)
    activated, grads = last_step(
        *adj[6:8], mine[3], swap_cores(mine[3]), total, largest,
        features, degree, weight, bias.reshape(1, 256), cotangent,
    )
    return (activated, *sum_over_devices(grads))


def solution(mesh):
    fine = Mesh(mesh.devices.reshape(SIZES), NAMES)
    rows = P(NAMES, None)
    return jax.shard_map(
        local,
        mesh=fine,
        in_specs=(rows, rows, rows, P(), P(), P(), rows),
        out_specs=(rows, P(), P()),
        check_vma=False,
    )
```

time: 765 us -> 132 us (0.17)
  waiting for transfers between devices: 571 us -> 31 us
  blocking collectives: 157 us -> 41.1 us
  starting transfers between devices: 0.08 us -> 25.6 us
  Pallas kernels: 0 us -> 25.1 us
  between operations: 14.8 us -> 0.87 us
  matrix products: 9.79 us -> 0 us
  other arithmetic: 8.55 us -> 0.58 us
    all_gather x1 -> x0, waiting for transfers between devices: 408 us -> none  [local(): lax.all_gather(scaled, ('dom', 'inner'), axis=0, tiled=True)]
    psum x1 -> x0, waiting for transfers between devices: 163 us -> none  [local(): lax.psum((local_weight, local_bias), ('dom', 'inner'))]
    pmax x1 -> x0, blocking collectives: 81.4 us -> none  [local(): shared = lax.pmax(jnp.max(jnp.abs(wide)), ('dom', 'inner')) + 1e-06]
    psum x1 -> x0, blocking collectives: 76 us -> none  [local(): lax.psum((local_weight, local_bias), ('dom', 'inner'))]
    all_to_all x0 -> x3, blocking collectives: none -> 41.1 us  [the longest x1 18.6 us: sum_over_devices(): part = lax.all_to_all(part, ZC, 0, 0, tiled=True)]
    ppermute x0 -> x15, waiting for transfers between devices: none -> 31 us  [permute(): lax.ppermute(array, NAMES, [(index_of(*at), index_of(*move(*at))) for at...]
    ppermute x0 -> x15, starting transfers between devices: none -> 25.6 us  [permute(): lax.ppermute(array, NAMES, [(index_of(*at), index_of(*move(*at))) for at...]
    pallas_call x0 -> x7, Pallas kernels: none -> 25.1 us  [the longest x1 12.3 us: order_adjacency(): pl.pallas_call(order_kernel, out_shape=[jax.ShapeDtypeStruct((128, PIECE)...]
  transfers between devices with their start and end apart: 2 -> 15, of which waited for: 2 -> 8; matrix products, arithmetic and copies ran while one was open for 1% -> 1% of each run, Pallas kernels for 0% -> 14%
where the time goes in v1:
time: 132 us; the launch traced here: 131 us
  blocking collectives  41.1 us (31%)
  waiting for transfers between devices  31 us (23%)
  starting transfers between devices  25.6 us (19%)
  Pallas kernels  25.1 us (19%)
  local copies, waits for them, and re-layouts  6.68 us (5%)
    ppermute x15, waiting for transfers between devices, permute(): lax.ppermute(array, NAMES, [(index_of(*at), index_of(*move(*at))) for at...  31 us
    ppermute x15, starting transfers between devices, permute(): lax.ppermute(array, NAMES, [(index_of(*at), index_of(*move(*at))) for at...  25.6 us
    all_to_all x1, blocking collectives, sum_over_devices(): part = lax.all_to_all(part, ZC, 0, 0, tiled=True)  18.6 us
    pallas_call x1, Pallas kernels, order_adjacency(): pl.pallas_call(order_kernel, out_shape=[jax.ShapeDtypeStruct((128, PIECE)...  12.3 us
    all_to_all x1, blocking collectives, sum_over_devices(): part = lax.all_to_all(grads, XY, 0, 0, tiled=True)  11.8 us
    all_to_all x1, blocking collectives, sum_over_devices(): grad_weight = lax.all_to_all(part, XY, 0, 0, tiled=True).reshape(128, 256)  10.7 us
    unnamed x33, local copies, waits for them, and re-layouts  6.6 us
    pallas_call x3, Pallas kernels, piece_step(): pl.pallas_call(piece_kernel, out_shape=[jax.ShapeDtypeStruct((128, 128),...  6.4 us
  transfers between devices with their start and end apart: 15, of which 8 were waited for; matrix products, arithmetic and copies ran while one was open for 1% of the time, Pallas kernels for 14%

profile of v1, /device:TPU:1, one launch (start us, length us, event | category | flops | bytes accessed | tf_op | source)
XLA Modules:
  0.0 131.0 jit_solution(2714743058595872962)
XLA Ops:
  0.6 3.3 %collective-permute-start = (bf16[128,128]{1,0:T(8,128)(2,1)}, bf16[128,128]{1,0:T(8,128)(2,1)S(1)}, u32[]{:S(2)}, u32[]{:S(2)}) collective-permute-start(bf16[128,128]{1,0:T(8,128)(2,1)} %own.1), channel_id=1, source_target_pairs={{0,1},{1,0},{2,3},{3,2},{4,5},{5,4},{6,7},{7,6},{8,9},{9,8},{10,11... | collective-permute-start | bytes 98312 | tf_op jit(solution)/shard_map/ppermute | solution.py:35
  4.0 0.8 constant_dynamic-update-slice_fusion.1
  5.0 7.1 %collective-permute-start.1 = (bf16[256,128]{1,0:T(8,128)(2,1)S(1)}, bf16[256,128]{1,0:T(8,128)(2,1)S(1)}, u32[]{:S(2)}, u32[]{:S(2)}) collective-permute-start(bf16[256,128]{1,0:T(8,128)(2,1)S(1)} %constant_dynamic-update-slice_fusion), channel_id=1, source_target_pairs={{0,0},{1,129},{2,2},{3,131},{4,4},{5,133},{6,6},{7,135},{8,8},{9,1... | collective-permute-start | bytes 196616 | tf_op jit(solution)/shard_map/ppermute | solution.py:35
  12.3 4.7 %collective-permute-start.4 = (bf16[256,128]{1,0:T(8,128)(2,1)S(1)}, bf16[256,128]{1,0:T(8,128)(2,1)S(1)}, u32[]{:S(2)}, u32[]{:S(2)}) collective-permute-start(bf16[256,128]{1,0:T(8,128)(2,1)S(1)} %constant_dynamic-update-slice_fusion), channel_id=1, source_target_pairs={{0,66},{1,131},{2,128},{3,193},{4,70},{5,135},{6,132},{7,197},{8,7... | collective-permute-start | bytes 196616 | tf_op jit(solution)/shard_map/ppermute | solution.py:35
  17.0 1.2 collective-permute-done.3
  18.2 1.4 %collective-permute-done.4 = bf16[256,128]{1,0:T(8,128)(2,1)S(1)} collective-permute-done((bf16[256,128]{1,0:T(8,128)(2,1)S(1)}, bf16[256,128]{1,0:T(8,128)(2,1)S(1)}, u32[]{:S(2)}, u32[]{:S(2)}) %collective-permute-start.4) | collective-permute-done | bytes 65568 | tf_op jit(solution)/shard_map/ppermute | solution.py:35
  19.6 1.4 %collective-permute-start.5 = (bf16[1024,128]{1,0:T(8,128)(2,1)S(1)}, bf16[1024,128]{1,0:T(8,128)(2,1)S(1)}, u32[]{:S(2)}, u32[]{:S(2)}) collective-permute-start(bf16[1024,128]{1,0:T(8,128)(2,1)S(1)} %get-tuple-element.41), channel_id=1, source_target_pairs={{0,16},{1,5},{2,18},{3,7},{4,20},{5,9},{6,22},{7,11},{8,24},{9,13}... | collective-permute-start | bytes 786440 | tf_op jit(solution)/shard_map/ppermute | solution.py:35
  21.0 1.5 %collective-permute-start.6 = (bf16[1024,128]{1,0:T(8,128)(2,1)S(1)}, bf16[1024,128]{1,0:T(8,128)(2,1)S(1)}, u32[]{:S(2)}, u32[]{:S(2)}) collective-permute-start(bf16[1024,128]{1,0:T(8,128)(2,1)S(1)} %get-tuple-element.41), channel_id=1, source_target_pairs={{0,48},{1,13},{2,50},{3,15},{4,52},{5,1},{6,54},{7,3},{8,56},{9,5}... | collective-permute-start | bytes 786440 | tf_op jit(solution)/shard_map/ppermute | solution.py:35
  22.5 1.6 %collective-permute-start.7 = (bf16[1024,128]{1,0:T(8,128)(2,1)S(1)}, bf16[1024,128]{1,0:T(8,128)(2,1)S(1)}, u32[]{:S(2)}, u32[]{:S(2)}) collective-permute-start(bf16[1024,128]{1,0:T(8,128)(2,1)S(1)} %get-tuple-element.41), channel_id=1, source_target_pairs={{0,32},{1,9},{2,34},{3,11},{4,36},{5,13},{6,38},{7,15},{8,40},{9,1... | collective-permute-start | bytes 786440 | tf_op jit(solution)/shard_map/ppermute | solution.py:35
  24.1 2.4 %collective-permute-done.5 = bf16[1024,128]{1,0:T(8,128)(2,1)S(1)} collective-permute-done((bf16[1024,128]{1,0:T(8,128)(2,1)S(1)}, bf16[1024,128]{1,0:T(8,128)(2,1)S(1)}, u32[]{:S(2)}, u32[]{:S(2)}) %collective-permute-start.5) | collective-permute-done | bytes 262176 | tf_op jit(solution)/shard_map/ppermute | solution.py:35
  26.5 2.1 %collective-permute-done.6 = bf16[1024,128]{1,0:T(8,128)(2,1)S(1)} collective-permute-done((bf16[1024,128]{1,0:T(8,128)(2,1)S(1)}, bf16[1024,128]{1,0:T(8,128)(2,1)S(1)}, u32[]{:S(2)}, u32[]{:S(2)}) %collective-permute-start.6) | collective-permute-done | bytes 262176 | tf_op jit(solution)/shard_map/ppermute | solution.py:35
  28.7 1.5 %collective-permute-done.7 = bf16[1024,128]{1,0:T(8,128)(2,1)S(1)} collective-permute-done((bf16[1024,128]{1,0:T(8,128)(2,1)S(1)}, bf16[1024,128]{1,0:T(8,128)(2,1)S(1)}, u32[]{:S(2)}, u32[]{:S(2)}) %collective-permute-start.7) | collective-permute-done | bytes 262176 | tf_op jit(solution)/shard_map/ppermute | solution.py:35
  30.2 1.3 collective-permute-start.12
  31.5 1.5 %collective-permute-start.10 = (bf16[4096,128]{1,0:T(8,128)(2,1)S(1)}, bf16[4096,128]{1,0:T(8,128)(2,1)S(1)}, u32[]{:S(2)}, u32[]{:S(2)}) collective-permute-start(bf16[4096,128]{1,0:T(8,128)(2,1)S(1)} %constant_dynamic-update-slice_fusion.6.feat_a), channel_id=1, source_target_pairs={{0,12},{1,49},{2,14},{3,51},{4,0},{5,53},{6,2},{7,55},{8,4},{9,57}... | collective-permute-start | bytes 3145736 | tf_op jit(solution)/shard_map/ppermute | solution.py:35
  33.0 1.5 %collective-permute-start.8 = (bf16[4096,128]{1,0:T(8,128)(2,1)S(1)}, bf16[4096,128]{1,0:T(8,128)(2,1)}, u32[]{:S(2)}, u32[]{:S(2)}) collective-permute-start(bf16[4096,128]{1,0:T(8,128)(2,1)S(1)} %constant_dynamic-update-slice_fusion.6.feat_a), channel_id=1, source_target_pairs={{0,8},{1,33},{2,10},{3,35},{4,12},{5,37},{6,14},{7,39},{8,0},{9,41... | collective-permute-start | bytes 3145736 | tf_op jit(solution)/shard_map/ppermute | solution.py:35
  34.9 10.4 %collective-permute-done.12.feat_a = bf16[4096,128]{1,0:T(8,128)(2,1)S(1)} collective-permute-done((bf16[4096,128]{1,0:T(8,128)(2,1)S(1)}, bf16[4096,128]{1,0:T(8,128)(2,1)S(1)}, u32[]{:S(2)}, u32[]{:S(2)}) %collective-permute-start.12) | collective-permute-done | bytes 1048608 | tf_op jit(solution)/shard_map/ppermute | solution.py:35
  46.0 11.7 %collective-permute-done.8.feat_a = bf16[4096,128]{1,0:T(8,128)(2,1)} collective-permute-done((bf16[4096,128]{1,0:T(8,128)(2,1)S(1)}, bf16[4096,128]{1,0:T(8,128)(2,1)}, u32[]{:S(2)}, u32[]{:S(2)}) %collective-permute-start.8) | collective-permute-done | bytes 1048608 | tf_op jit(solution)/shard_map/ppermute | solution.py:35
  58.9 12.3 %shard_map.94 = (bf16[128,4096]{1,0:T(8,128)(2,1)}, bf16[128,4096]{1,0:T(8,128)(2,1)}, bf16[128,4096]{1,0:T(8,128)(2,1)}, bf16[128,4096]{1,0:T(8,128)(2,1)}, bf1...) custom-call(s32[256]{0:T(256)} %xor_add_fusion.table, ...), custom_call_target="tpu_custom_call" | custom-call | flops 8388608 | bytes 16777216 | tf_op jit(solution)/shard_map/pallas_call | solution.py:103
  71.2 1.4 %copy-done.4 = bf16[128,4096]{1,0:T(8,128)(2,1)S(1)} copy-done((bf16[128,4096]{1,0:T(8,128)(2,1)S(1)}, bf16[128,4096]{1,0:T(8,128)(2,1)}, u32[]{:S(2)}) %copy-start.4) | copy-done | bytes 1048600
  72.5 1.2 copy-done.5
  73.8 2.2 %shard_map.95 = (f32[128,128]{1,0:T(8,128)S(1)}, bf16[16,128]{1,0:T(8,128)(2,1)S(1)}) custom-call(bf16[128,4096]{1,0:T(8,128)(2,1)S(1)} %copy-done.4, bf16[128,4096]{1,0:T(8,128)(2,1)S(1)} %copy-done.5, bf16[4096,128]{1,0:T(8,128)(2,1)S(1)} %constant_dynamic-update-slice_fusion.6.feat_a, bf16[4096,128]{1,0:T(8,128)(2,1)} %collective-permute-done.14.feat_b, ...), custom_call_target="tpu_custom_call" | custom-call | flops 268435456 | bytes 4194304 | tf_op jit(solution)/shard_map/pallas_call | solution.py:131
  76.0 1.2 copy-done.2
  77.3 1.2 copy-done.3
  78.5 2.1 %shard_map.96 = (f32[128,128]{1,0:T(8,128)S(1)}, bf16[16,128]{1,0:T(8,128)(2,1)S(1)}) custom-call(bf16[128,4096]{1,0:T(8,128)(2,1)S(1)} %copy-done.2, bf16[128,4096]{1,0:T(8,128)(2,1)S(1)} %copy-done.3, bf16[4096,128]{1,0:T(8,128)(2,1)S(1)} %collective-permute-done.12.feat_a, bf16[4096,128]{1,0:T(8,128)(2,1)} %collective-permute-done.13.feat_b, ...), custom_call_target="tpu_custom_call" | custom-call | flops 268435456 | bytes 4194304 | tf_op jit(solution)/shard_map/pallas_call | solution.py:131
  80.6 2.1 %shard_map.97 = (f32[128,128]{1,0:T(8,128)S(1)}, bf16[16,128]{1,0:T(8,128)(2,1)S(1)}) custom-call(bf16[128,4096]{1,0:T(8,128)(2,1)S(1)} %copy-done, bf16[128,4096]{1,0:T(8,128)(2,1)S(1)} %copy-done.1, bf16[4096,128]{1,0:T(8,128)(2,1)S(1)} %collective-permute-done.10.feat_a, bf16[4096,128]{1,0:T(8,128)(2,1)} %collective-permute-done.11.feat_b, ...), custom_call_target="tpu_custom_call" | custom-call | flops 268435456 | bytes 4194304 | tf_op jit(solution)/shard_map/pallas_call | solution.py:131
  82.8 3.2 %shard_map.98 = (bf16[128,256]{1,0:T(8,128)(2,1)}, f32[16,8,384]{2,1,0:T(8,128)S(1)}) custom-call(bf16[128,4096]{1,0:T(8,128)(2,1)S(1)} %copy-done.6, bf16[128,4096]{1,0:T(8,128)(2,1)S(1)} %copy-done.7, bf16[4096,128]{1,0:T(8,128)(2,1)} %collective-permute-done.8.feat_a, bf16[4096,128]{1,0:T(8,128)(2,1)} %collective-permute-done.9.feat_b, ...), custom_call_target="tpu_custom_call" | custom-call | flops 268435456 | bytes 4194304 | tf_op jit(solution)/shard_map/pallas_call | solution.py:170
  86.0 11.8 %all_to_all.15.parts = f32[16,8,384]{2,1,0:T(8,128)} all-to-all(f32[16,8,384]{2,1,0:T(8,128)S(1)} %get-tuple-element.38), channel_id=1, replica_groups=mesh['zh'=4,'x'=4,'y'=4,'zl'=2,'core'=2] {'x','y'}, dimensions={0} | all-to-all | bytes 393216 | tf_op jit(solution)/shard_map/all_to_all | solution.py:197
  97.8 1.6 %shard_map.99 = f32[16,8,384]{2,1,0:T(8,128)} custom-call(f32[16,8,384]{2,1,0:T(8,128)} %all_to_all.15.parts), custom_call_target="tpu_custom_call" | custom-call | tf_op jit(solution)/shard_map/pallas_call | solution.py:198
  99.5 18.6 %all_to_all.16.parts = f32[16,8,384]{2,1,0:T(8,128)} all-to-all(f32[16,8,384]{2,1,0:T(8,128)} %shard_map.99), channel_id=1, replica_groups=mesh['zh'=4,'x'=4,'y'=4,'zl'=2,'core'=2] {'zh','zl','core'}, dimensions={0} | all-to-all | bytes 393216 | tf_op jit(solution)/shard_map/all_to_all | solution.py:199
  118.0 1.6 %shard_map.100 = (f32[16,8,256]{2,1,0:T(8,128)}, f32[1,256]{1,0:T(1,128)}) custom-call(f32[16,8,384]{2,1,0:T(8,128)} %all_to_all.16.parts), custom_call_target="tpu_custom_call" | custom-call | tf_op jit(solution)/shard_map/pallas_call | solution.py:200
  119.6 10.7 %all_to_all.17 = f32[16,8,256]{2,1,0:T(8,128)S(1)} all-to-all(f32[16,8,256]{2,1,0:T(8,128)} %get-tuple-element.39), channel_id=1, replica_groups=mesh['zh'=4,'x'=4,'y'=4,'zl'=2,'core'=2] {'x','y'}, dimensions={0} | all-to-all | bytes 262144 | tf_op jit(solution)/shard_map/all_to_all | solution.py:207
  130.3 0.7 copy.21
  (47 shorter events, 3.0 us)
Async XLA Ops:
  0.6 4.4 %collective-permute-start = (bf16[128,128]{1,0:T(8,128)(2,1)}, bf16[128,128]{1,0:T(8,128)(2,1)S(1)}, u32[]{:S(2)}, u32[]{:S(2)}) collective-permute-start(bf16[128,128]{1,0:T(8,128)(2,1)} %own.1), channel_id=1, source_target_pairs={{0,1},{1,0},{2,3},{3,2},{4,5},{5,4},{6,7},{7,6},{8,9},{9,8},{10,11... | collective-permute-start | bytes 98312 | tf_op jit(solution)/shard_map/ppermute | solution.py:35
  5.0 11.9 %collective-permute-start.1 = (bf16[256,128]{1,0:T(8,128)(2,1)S(1)}, bf16[256,128]{1,0:T(8,128)(2,1)S(1)}, u32[]{:S(2)}, u32[]{:S(2)}) collective-permute-start(bf16[256,128]{1,0:T(8,128)(2,1)S(1)} %constant_dynamic-update-slice_fusion), channel_id=1, source_target_pairs={{0,0},{1,129},{2,2},{3,131},{4,4},{5,133},{6,6},{7,135},{8,8},{9,1... | collective-permute-start | bytes 196616 | tf_op jit(solution)/shard_map/ppermute | solution.py:35
  12.1 4.9 %collective-permute-start.2 = (bf16[256,128]{1,0:T(8,128)(2,1)S(1)}, bf16[256,128]{1,0:T(8,128)(2,1)S(1)}, u32[]{:S(2)}, u32[]{:S(2)}) collective-permute-start(bf16[256,128]{1,0:T(8,128)(2,1)S(1)} %constant_dynamic-update-slice_fusion), channel_id=1, source_target_pairs={{0,2},{1,195},{2,64},{3,1},{4,6},{5,199},{6,68},{7,5},{8,10},{9,20... | collective-permute-start | bytes 196616 | tf_op jit(solution)/shard_map/ppermute | solution.py:35
  12.2 6.0 %collective-permute-start.3 = (bf16[256,128]{1,0:T(8,128)(2,1)S(1)}, bf16[256,128]{1,0:T(8,128)(2,1)S(1)}, u32[]{:S(2)}, u32[]{:S(2)}) collective-permute-start(bf16[256,128]{1,0:T(8,128)(2,1)S(1)} %constant_dynamic-update-slice_fusion), channel_id=1, source_target_pairs={{0,64},{1,193},{2,66},{3,195},{4,68},{5,197},{6,70},{7,199},{8,72}... | collective-permute-start | bytes 196616 | tf_op jit(solution)/shard_map/ppermute | solution.py:35
  12.3 7.3 %collective-permute-start.4 = (bf16[256,128]{1,0:T(8,128)(2,1)S(1)}, bf16[256,128]{1,0:T(8,128)(2,1)S(1)}, u32[]{:S(2)}, u32[]{:S(2)}) collective-permute-start(bf16[256,128]{1,0:T(8,128)(2,1)S(1)} %constant_dynamic-update-slice_fusion), channel_id=1, source_target_pairs={{0,66},{1,131},{2,128},{3,193},{4,70},{5,135},{6,132},{7,197},{8,7... | collective-permute-start | bytes 196616 | tf_op jit(solution)/shard_map/ppermute | solution.py:35
  19.6 6.9 %collective-permute-start.5 = (bf16[1024,128]{1,0:T(8,128)(2,1)S(1)}, bf16[1024,128]{1,0:T(8,128)(2,1)S(1)}, u32[]{:S(2)}, u32[]{:S(2)}) collective-permute-start(bf16[1024,128]{1,0:T(8,128)(2,1)S(1)} %get-tuple-element.41), channel_id=1, source_target_pairs={{0,16},{1,5},{2,18},{3,7},{4,20},{5,9},{6,22},{7,11},{8,24},{9,13}... | collective-permute-start | bytes 786440 | tf_op jit(solution)/shard_map/ppermute | solution.py:35
  21.0 7.7 %collective-permute-start.6 = (bf16[1024,128]{1,0:T(8,128)(2,1)S(1)}, bf16[1024,128]{1,0:T(8,128)(2,1)S(1)}, u32[]{:S(2)}, u32[]{:S(2)}) collective-permute-start(bf16[1024,128]{1,0:T(8,128)(2,1)S(1)} %get-tuple-element.41), channel_id=1, source_target_pairs={{0,48},{1,13},{2,50},{3,15},{4,52},{5,1},{6,54},{7,3},{8,56},{9,5}... | collective-permute-start | bytes 786440 | tf_op jit(solution)/shard_map/ppermute | solution.py:35
  22.5 7.7 %collective-permute-start.7 = (bf16[1024,128]{1,0:T(8,128)(2,1)S(1)}, bf16[1024,128]{1,0:T(8,128)(2,1)S(1)}, u32[]{:S(2)}, u32[]{:S(2)}) collective-permute-start(bf16[1024,128]{1,0:T(8,128)(2,1)S(1)} %get-tuple-element.41), channel_id=1, source_target_pairs={{0,32},{1,9},{2,34},{3,11},{4,36},{5,13},{6,38},{7,15},{8,40},{9,1... | collective-permute-start | bytes 786440 | tf_op jit(solution)/shard_map/ppermute | solution.py:35
  30.2 15.1 %collective-permute-start.12 = (bf16[4096,128]{1,0:T(8,128)(2,1)S(1)}, bf16[4096,128]{1,0:T(8,128)(2,1)S(1)}, u32[]{:S(2)}, u32[]{:S(2)}) collective-permute-start(bf16[4096,128]{1,0:T(8,128)(2,1)S(1)} %constant_dynamic-update-slice_fusion.6.feat_a), channel_id=1, source_target_pairs={{0,4},{1,17},{2,6},{3,19},{4,8},{5,21},{6,10},{7,23},{8,12},{9,25}... | collective-permute-start | bytes 3145736 | tf_op jit(solution)/shard_map/ppermute | solution.py:35
  31.5 14.2 %collective-permute-start.10 = (bf16[4096,128]{1,0:T(8,128)(2,1)S(1)}, bf16[4096,128]{1,0:T(8,128)(2,1)S(1)}, u32[]{:S(2)}, u32[]{:S(2)}) collective-permute-start(bf16[4096,128]{1,0:T(8,128)(2,1)S(1)} %constant_dynamic-update-slice_fusion.6.feat_a), channel_id=1, source_target_pairs={{0,12},{1,49},{2,14},{3,51},{4,0},{5,53},{6,2},{7,55},{8,4},{9,57}... | collective-permute-start | bytes 3145736 | tf_op jit(solution)/shard_map/ppermute | solution.py:35
  33.0 24.8 %collective-permute-start.8 = (bf16[4096,128]{1,0:T(8,128)(2,1)S(1)}, bf16[4096,128]{1,0:T(8,128)(2,1)}, u32[]{:S(2)}, u32[]{:S(2)}) collective-permute-start(bf16[4096,128]{1,0:T(8,128)(2,1)S(1)} %constant_dynamic-update-slice_fusion.6.feat_a), channel_id=1, source_target_pairs={{0,8},{1,33},{2,10},{3,35},{4,12},{5,37},{6,14},{7,39},{8,0},{9,41... | collective-permute-start | bytes 3145736 | tf_op jit(solution)/shard_map/ppermute | solution.py:35
  34.5 36.6 %collective-permute-start.14 = (bf16[4096,128]{1,0:T(8,128)(2,1)S(1)}, bf16[4096,128]{1,0:T(8,128)(2,1)}, u32[]{:S(2)}, u32[]{:S(2)}) collective-permute-start(bf16[4096,128]{1,0:T(8,128)(2,1)S(1)} %constant_dynamic-update-slice_fusion.6.feat_a), channel_id=1, source_target_pairs={{0,1},{1,0},{2,3},{3,2},{4,5},{5,4},{6,7},{7,6},{8,9},{9,8},{10,11... | collective-permute-start | bytes 3145736 | tf_op jit(solution)/shard_map/ppermute | solution.py:35
  45.3 30.7 %collective-permute-start.13 = (bf16[4096,128]{1,0:T(8,128)(2,1)S(1)}, bf16[4096,128]{1,0:T(8,128)(2,1)}, u32[]{:S(2)}, u32[]{:S(2)}) collective-permute-start(bf16[4096,128]{1,0:T(8,128)(2,1)S(1)} %collective-permute-done.12.feat_a), channel_id=1, source_target_pairs={{0,1},{1,0},{2,3},{3,2},{4,5},{5,4},{6,7},{7,6},{8,9},{9,8},{10,11... | collective-permute-start | bytes 3145736 | tf_op jit(solution)/shard_map/ppermute | solution.py:35
  45.7 34.9 %collective-permute-start.11 = (bf16[4096,128]{1,0:T(8,128)(2,1)S(1)}, bf16[4096,128]{1,0:T(8,128)(2,1)}, u32[]{:S(2)}, u32[]{:S(2)}) collective-permute-start(bf16[4096,128]{1,0:T(8,128)(2,1)S(1)} %collective-permute-done.10.feat_a), channel_id=1, source_target_pairs={{0,1},{1,0},{2,3},{3,2},{4,5},{5,4},{6,7},{7,6},{8,9},{9,8},{10,11... | collective-permute-start | bytes 3145736 | tf_op jit(solution)/shard_map/ppermute | solution.py:35
  57.8 24.9 %collective-permute-start.9 = (bf16[4096,128]{1,0:T(8,128)(2,1)}, bf16[4096,128]{1,0:T(8,128)(2,1)}, u32[]{:S(2)}, u32[]{:S(2)}) collective-permute-start(bf16[4096,128]{1,0:T(8,128)(2,1)} %collective-permute-done.8.feat_a), channel_id=1, source_target_pairs={{0,1},{1,0},{2,3},{3,2},{4,5},{5,4},{6,7},{7,6},{8,9},{9,8},{10,11... | collective-permute-start | bytes 3145736 | tf_op jit(solution)/shard_map/ppermute | solution.py:35
  58.8 23.9 %copy-start.8 = (bf16[128,128]{1,0:T(8,128)(2,1)S(1)}, bf16[128,128]{1,0:T(8,128)(2,1)}, u32[]{:S(2)}) copy-start(bf16[128,128]{1,0:T(8,128)(2,1)} %own.1) | copy-start | bytes 98308
  58.8 23.9 %copy-start.9 = (bf16[128,256]{1,0:T(8,128)(2,1)S(1)}, bf16[128,256]{1,0:T(8,128)(2,1)}, u32[]{:S(2)}) copy-start(bf16[128,256]{1,0:T(8,128)(2,1)} %weight.1) | copy-start | bytes 196612
  58.8 23.9 %copy-start.10 = (bf16[128,256]{1,0:T(8,128)(2,1)S(1)}, bf16[128,256]{1,0:T(8,128)(2,1)}, u32[]{:S(2)}) copy-start(bf16[128,256]{1,0:T(8,128)(2,1)} %cotangent.1) | copy-start | bytes 196612
  58.8 23.9 %copy-start.12 = (f32[256]{0:T(256)S(1)}, f32[256]{0:T(256)}, u32[]{:S(2)}) copy-start(f32[256]{0:T(256)} %param.12) | copy-start | bytes 3076
  71.1 9.4 %copy-start = (bf16[128,4096]{1,0:T(8,128)(2,1)S(1)}, bf16[128,4096]{1,0:T(8,128)(2,1)}, u32[]{:S(2)}) copy-start(bf16[128,4096]{1,0:T(8,128)(2,1)} %get-tuple-element.24.adj_a) | copy-start | bytes 3145732
  71.1 9.5 %copy-start.1 = (bf16[128,4096]{1,0:T(8,128)(2,1)S(1)}, bf16[128,4096]{1,0:T(8,128)(2,1)}, u32[]{:S(2)}) copy-start(bf16[128,4096]{1,0:T(8,128)(2,1)} %get-tuple-element.25.adj_b) | copy-start | bytes 3145732
  71.2 1.4 %copy-start.4 = (bf16[128,4096]{1,0:T(8,128)(2,1)S(1)}, bf16[128,4096]{1,0:T(8,128)(2,1)}, u32[]{:S(2)}) copy-start(bf16[128,4096]{1,0:T(8,128)(2,1)} %get-tuple-element.28.adj_a) | copy-start | bytes 3145732
  72.5 1.2 copy-start.5
  73.8 9.0 %copy-start.6 = (bf16[128,4096]{1,0:T(8,128)(2,1)S(1)}, bf16[128,4096]{1,0:T(8,128)(2,1)}, u32[]{:S(2)}) copy-start(bf16[128,4096]{1,0:T(8,128)(2,1)} %get-tuple-element.22.adj_a) | copy-start | bytes 3145732
  73.8 9.0 %copy-start.7 = (bf16[128,4096]{1,0:T(8,128)(2,1)S(1)}, bf16[128,4096]{1,0:T(8,128)(2,1)}, u32[]{:S(2)}) copy-start(bf16[128,4096]{1,0:T(8,128)(2,1)} %get-tuple-element.23.adj_b) | copy-start | bytes 3145732
  73.8 9.0 %copy-start.11 = (f32[128,128]{1,0:T(8,128)S(1)}, f32[128,128]{1,0:T(8,128)}, u32[]{:S(2)}) copy-start(f32[128,128]{1,0:T(8,128)} %get-tuple-element.36.degree) | copy-start | bytes 196612
  76.0 1.2 copy-start.2
  77.2 1.2 copy-start.3

commit v2 on v1

v2 whole, which is shorter than its diff:
```python
import functools

import jax
import jax.numpy as jnp
from jax import lax
from jax.experimental import pallas as pl
from jax.experimental.pallas import tpu as pltpu
from jax.sharding import Mesh, PartitionSpec as P

NAMES = ("zh", "x", "y", "zl", "core")
SIZES = (4, 4, 4, 2, 2)
SHIFTS = (0, 1, 3, 2)
PIECES = 8
PIECE = 4096
HALF = PIECE // 2
BLOCKS = PIECE // 128
VMEM_LIMIT = 24 * 1024 * 1024


def index_of(zh, x, y, zl, core):
    return (((zh * 4 + x) * 4 + y) * 2 + zl) * 2 + core


def coords():
    return [
        (zh, x, y, zl, core)
        for zh in range(4)
        for x in range(4)
        for y in range(4)
        for zl in range(2)
        for core in range(2)
    ]


def permute(array, move):
    return lax.ppermute(array, NAMES, [(index_of(*at), index_of(*move(*at))) for at in coords()])


def swap_cores(array):
    return permute(array, lambda zh, x, y, zl, core: (zh, x, y, zl, 1 - core))


def along_z(array, step):
    def move(zh, x, y, zl, core):
        z = zh * 2 + zl
        if core == 0:
            z = (z + step) % 8 if step < 4 else z
        else:
            z = (z - step) % 8
        return z // 2, x, y, z % 2, core

    return permute(array, move)


def swap_pairs(array):
    return permute(array, lambda zh, x, y, zl, core: (zh, x, y, 1 - zl, core))


def along_zh(array, step):
    return permute(array, lambda zh, x, y, zl, core: ((zh + step) % 4, x, y, zl, core))


def along_xy(array, step, turned):
    def move(zh, x, y, zl, core):
        if (core == 0) != turned:
            return zh, (x + step) % 4, y, zl, core
        return zh, x, (y + step) % 4, zl, core

    return permute(array, move)


def place_table(tile_mask, skip_owner):
    zh, x, y, _, core = (lax.axis_index(n) for n in NAMES)
    z = zh * 2 + lax.axis_index("zl")
    source = lax.iota(jnp.int32, PIECES * BLOCKS)
    up = (z - ((source >> 6) * 2 + ((source >> 1) & 1))) & 7
    first = up < 4
    plane = jnp.where(first, 0, 1)

    def slot_of(shift):
        return shift ^ (shift >> 1)

    from_x, from_y = slot_of((x - (source >> 4)) & 3), slot_of((y - (source >> 2)) & 3)
    outer, inner = jnp.where(first, from_y, from_x), jnp.where(first, from_x, from_y)
    hop = jnp.where(first, up, (8 - up) & 3)
    pair = (source & 1) ^ plane
    place = outer * 64 + (plane ^ core) * 32 + inner * 8 + hop * 2 + pair
    return jnp.concatenate([place, tile_mask[0] * (1 - skip_owner)])


def order_kernel(table, adjacency, ordered, degree):
    chunk = pl.program_id(0)

    def one_partition(owner, total):
        owner = chunk * (BLOCKS // 4) + owner
        live = table[PIECES * BLOCKS + owner].astype(jnp.float32)
        live = jnp.full((1, 1), live).astype(jnp.bfloat16)
        for block in range(4):
            place = table[owner * 4 + block]
            start = (owner * 4 + block - chunk * BLOCKS) * 128
            values = adjacency[:, pl.ds(pl.multiple_of(start, 128), 128)] * live
            ordered[place >> 5, :, pl.ds(pl.multiple_of((place & 31) * 128, 128), 128)] = values
            total = total + values.astype(jnp.float32)
        return total

    @pl.when(chunk == 0)
    def _():
        degree[...] = jnp.zeros_like(degree)

    degree[...] = lax.fori_loop(0, BLOCKS // 4, one_partition, degree[...], unroll=2)

    @pl.when(chunk == PIECES - 1)
    def _():
        degree[...] = jnp.broadcast_to(1.0 + jnp.sum(degree[...], axis=1, keepdims=True), (128, 128))


def order_adjacency(table, adjacency):
    vmem = pl.BlockSpec(memory_space=pltpu.VMEM)
    return pl.pallas_call(
        order_kernel,
        out_shape=[
            jax.ShapeDtypeStruct((PIECES, 128, PIECE), jnp.bfloat16),
            jax.ShapeDtypeStruct((128, 128), jnp.float32),
        ],
        grid=(PIECES,),
        in_specs=[pl.BlockSpec(memory_space=pltpu.SMEM), pl.BlockSpec((128, PIECE), lambda chunk: (0, chunk))],
        out_specs=[vmem, vmem],
        compiler_params=pltpu.CompilerParams(vmem_limit_bytes=VMEM_LIMIT),
        cost_estimate=pl.CostEstimate(flops=1024, bytes_accessed=1024, transcendentals=0),
    )(table, adjacency)


def add_piece(ordered, piece, feat, total, largest, first=0):
    for start in range(0, feat.shape[0], 512):
        rows = feat[start : start + 512, :]
        columns = ordered[piece, :, first + start : first + start + 512]
        total = total + jnp.dot(columns, rows, preferred_element_type=jnp.float32)
        largest = jnp.maximum(largest, jnp.max(jnp.abs(rows).reshape(32, 16, 128), axis=0))
    return total, largest


def piece_kernel(piece, ordered, feat_a, feat_b, total_in, largest_in, total_out, largest_out):
    total, largest = add_piece(ordered, piece, feat_a, total_in[...], largest_in[...])
    total, largest = add_piece(ordered, piece + 1, feat_b, total, largest)
    total_out[...] = total
    largest_out[...] = largest


def piece_step(piece, ordered, feat_a, feat_b, total, largest):
    vmem = pl.BlockSpec(memory_space=pltpu.VMEM)
    return pl.pallas_call(
        functools.partial(piece_kernel, piece),
        out_shape=[
            jax.ShapeDtypeStruct((128, 128), jnp.float32),
            jax.ShapeDtypeStruct((16, 128), jnp.bfloat16),
        ],
        in_specs=[vmem] * 5,
        out_specs=[vmem] * 2,
        compiler_params=pltpu.CompilerParams(vmem_limit_bytes=VMEM_LIMIT // 2),
        cost_estimate=pl.CostEstimate(flops=1024, bytes_accessed=1024, transcendentals=0),
    )(ordered, feat_a, feat_b, total, largest)


def last_kernel(
    core, ordered, feat_a, feat_a2, feat_b, feat_b2, total_in, largest_in,
    own, degree, weight, bias, cotangent, activated, mine, theirs,
):
    total, largest = total_in[...], largest_in[...]
    for number, feat in enumerate((feat_a, feat_a2, feat_b, feat_b2)):
        total, largest = add_piece(ordered, 6 + number // 2, feat, total, largest, number % 2 * HALF)
    factor = 64.0 / (jnp.max(largest.astype(jnp.float32)) + 1e-06)
    summed = (total + own[...].astype(jnp.float32)) * factor
    mixed = (summed / degree[...]).astype(jnp.bfloat16)
    pre = jnp.dot(mixed, weight[...], preferred_element_type=jnp.float32) + bias[...]
    sigma = jax.nn.sigmoid(pre)
    activated[...] = (pre * sigma).astype(jnp.bfloat16)
    delta = cotangent[...].astype(jnp.float32) * (sigma * (1.0 + pre * (1.0 - sigma)))
    grad_weight = lax.dot_general(
        mixed, delta.astype(jnp.bfloat16), (((0,), (0,)), ((), ())), preferred_element_type=jnp.float32
    )
    grad_bias = jnp.sum(delta, axis=0, keepdims=True)
    for half in range(2):
        columns = slice(half * 128, half * 128 + 128)

        @pl.when(core[0] == half)
        def _(columns=columns):
            mine[:128, :] = grad_weight[:, columns]
            mine[128:, :] = jnp.broadcast_to(grad_bias[:, columns], (8, 128))

        @pl.when(core[0] != half)
        def _(columns=columns):
            theirs[:128, :] = grad_weight[:, columns]
            theirs[128:, :] = jnp.broadcast_to(grad_bias[:, columns], (8, 128))


def last_step(*args):
    vmem = pl.BlockSpec(memory_space=pltpu.VMEM)
    return pl.pallas_call(
        last_kernel,
        out_shape=[
            jax.ShapeDtypeStruct((128, 256), jnp.bfloat16),
            jax.ShapeDtypeStruct((136, 128), jnp.float32),
            jax.ShapeDtypeStruct((136, 128), jnp.float32),
        ],
        in_specs=[pl.BlockSpec(memory_space=pltpu.SMEM)] + [vmem] * 12,
        out_specs=[vmem] * 3,
        compiler_params=pltpu.CompilerParams(vmem_limit_bytes=VMEM_LIMIT // 2),
        cost_estimate=pl.CostEstimate(flops=1024, bytes_accessed=1024, transcendentals=0),
    )(*args)


def ring_sum(send, part):
    near = send(part, 1) + send(part, 3)
    return (part + send(part, 2)) + near


def sum_over_devices(mine, theirs, core):
    part = mine + swap_cores(theirs)
    for turned in (False, True):
        part = ring_sum(lambda array, step: along_xy(array, step, turned), part)
    part = part + swap_pairs(part)
    part = ring_sum(along_zh, part)
    other = swap_cores(part)
    left, right = jnp.where(core == 0, part, other), jnp.where(core == 0, other, part)
    both = jnp.concatenate([left, right], axis=1)
    return both[:128], both[128]


def local(features, adjacency, tile_mask, skip_owner, weight, bias, cotangent):
    ordered, degree = order_adjacency(place_table(tile_mask, skip_owner), adjacency)
    chip = jnp.concatenate([features, swap_cores(features)])
    far = along_z(chip, 4)
    line = jnp.concatenate([far] + [along_z(chip, step) for step in (3, 2, 1)][::-1])
    plane = jnp.concatenate([line] + [along_xy(line, step, False) for step in SHIFTS[1:]])
    after, before = along_xy(plane, 1, True), along_xy(plane, 3, True)
    total = jnp.zeros((128, 128), jnp.float32)
    largest = jnp.zeros((16, 128), jnp.bfloat16)
    total, largest = piece_step(0, ordered, plane, swap_cores(plane), total, largest)
    after, before, total = lax.optimization_barrier((after, before, total))
    halves = along_xy(after[:HALF], 1, True), along_xy(before[HALF:], 3, True)
    for number, feat in ((1, after), (2, before)):
        total, largest = piece_step(2 * number, ordered, feat, swap_cores(feat), total, largest)
    *halves, total = lax.optimization_barrier((*halves, total))
    core = lax.axis_index("core")
    activated, mine, theirs = last_step(
        core.reshape(1), ordered, *halves, *(swap_cores(half) for half in halves), total, largest,
        features, degree, weight, bias.reshape(1, 256), cotangent,
    )
    return (activated, *sum_over_devices(mine, theirs, core))


def solution(mesh):
    fine = Mesh(mesh.devices.reshape(SIZES), NAMES)
    rows = P(NAMES, None)
    return jax.shard_map(
        local,
        mesh=fine,
        in_specs=(rows, rows, rows, P(), P(), P(), rows),
        out_specs=(rows, P(), P()),
        check_vma=False,
    )
```

time: 132 us -> 100 us (0.76)
  blocking collectives: 41.1 us -> 0 us
  starting transfers between devices: 25.6 us -> 54.5 us
  Pallas kernels: 25.1 us -> 10.9 us
  waiting for transfers between devices: 31 us -> 27 us
  local copies, waits for them, and re-layouts: 6.68 us -> 4.43 us
  other arithmetic: 0.58 us -> 2.02 us
    all_to_all x3 -> x0, blocking collectives: 41.1 us -> none  [the longest x1 18.6 us: sum_over_devices(): part = lax.all_to_all(part, ZC, 0, 0, tiled=True)]
    ppermute x15 -> x29, starting transfers between devices: 25.6 us -> 54.5 us  [permute(): lax.ppermute(array, NAMES, [(index_of(*at), index_of(*move(*at))) for at...]
    pallas_call x6 -> x4, Pallas kernels: 21.9 us -> 8.99 us  [the longest x1 5.11 us: order_adjacency(): pl.pallas_call(order_kernel, out_shape=[jax.ShapeDtypeStruct((PIECES, 128...]
    ppermute x15 -> x29, waiting for transfers between devices: 31 us -> 27 us  [permute(): lax.ppermute(array, NAMES, [(index_of(*at), index_of(*move(*at))) for at...]
    unnamed x33 -> x16, local copies, waits for them, and re-layouts: 6.6 us -> 4.28 us
    pallas_call x1, Pallas kernels: 3.23 us -> 1.88 us  [last_step(): pl.pallas_call(last_kernel, out_shape=[jax.ShapeDtypeStruct((128, 256), j...]
  transfers between devices with their start and end apart: 15 -> 29, of which waited for: 8 -> 18; matrix products, arithmetic and copies ran while one was open for 1% -> 2% of each run, Pallas kernels for 14% -> 9%
where the time goes in v2:
time: 100 us; the launch traced here: 99.6 us
  starting transfers between devices  54.5 us (54%)
  waiting for transfers between devices  27 us (27%)
  Pallas kernels  10.9 us (11%)
  local copies, waits for them, and re-layouts  4.43 us (4%)
  other arithmetic  2.02 us (2%)
    ppermute x29, starting transfers between devices, permute(): lax.ppermute(array, NAMES, [(index_of(*at), index_of(*move(*at))) for at...  54.5 us
    ppermute x29, waiting for transfers between devices, permute(): lax.ppermute(array, NAMES, [(index_of(*at), index_of(*move(*at))) for at...  27 us
    pallas_call x1, Pallas kernels, order_adjacency(): pl.pallas_call(order_kernel, out_shape=[jax.ShapeDtypeStruct((PIECES, 128...  5.11 us
    unnamed x16, local copies, waits for them, and re-layouts  4.28 us
    pallas_call x3, Pallas kernels, piece_step(): pl.pallas_call(functools.partial(piece_kernel, piece), out_shape=[jax.Sha...  3.88 us
  transfers between devices with their start and end apart: 29, of which 18 were waited for; matrix products, arithmetic and copies ran while one was open for 2% of the time, Pallas kernels for 9%

profile of v2, /device:TPU:1, one launch (start us, length us, event | category | flops | bytes accessed | tf_op | source)
XLA Modules:
  0.0 99.6 jit_solution(13465840245143976123)
XLA Ops:
  0.6 3.3 %collective-permute-start = (bf16[128,128]{1,0:T(8,128)(2,1)}, bf16[128,128]{1,0:T(8,128)(2,1)S(1)}, u32[]{:S(2)}, u32[]{:S(2)}) collective-permute-start(bf16[128,128]{1,0:T(8,128)(2,1)} %own.1), channel_id=1, source_target_pairs={{0,1},{1,0},{2,3},{3,2},{4,5},{5,4},{6,7},{7,6},{8,9},{9,8},{10,11... | collective-permute-start | bytes 98312 | tf_op jit(solution)/shard_map/ppermute | solution.py:36
  5.0 7.1 %collective-permute-start.1 = (bf16[256,128]{1,0:T(8,128)(2,1)S(1)}, bf16[256,128]{1,0:T(8,128)(2,1)S(1)}, u32[]{:S(2)}, u32[]{:S(2)}) collective-permute-start(bf16[256,128]{1,0:T(8,128)(2,1)S(1)} %constant_dynamic-update-slice_fusion), channel_id=1, source_target_pairs={{0,0},{1,129},{2,2},{3,131},{4,4},{5,133},{6,6},{7,135},{8,8},{9,1... | collective-permute-start | bytes 196616 | tf_op jit(solution)/shard_map/ppermute | solution.py:36
  12.3 4.7 %collective-permute-start.4 = (bf16[256,128]{1,0:T(8,128)(2,1)S(1)}, bf16[256,128]{1,0:T(8,128)(2,1)S(1)}, u32[]{:S(2)}, u32[]{:S(2)}) collective-permute-start(bf16[256,128]{1,0:T(8,128)(2,1)S(1)} %constant_dynamic-update-slice_fusion), channel_id=1, source_target_pairs={{0,66},{1,131},{2,128},{3,193},{4,70},{5,135},{6,132},{7,197},{8,7... | collective-permute-start | bytes 196616 | tf_op jit(solution)/shard_map/ppermute | solution.py:36
  18.2 1.4 %collective-permute-done.4 = bf16[256,128]{1,0:T(8,128)(2,1)S(1)} collective-permute-done((bf16[256,128]{1,0:T(8,128)(2,1)S(1)}, bf16[256,128]{1,0:T(8,128)(2,1)S(1)}, u32[]{:S(2)}, u32[]{:S(2)}) %collective-permute-start.4) | collective-permute-done | bytes 65568 | tf_op jit(solution)/shard_map/ppermute | solution.py:36
  19.6 1.4 %collective-permute-start.5 = (bf16[1024,128]{1,0:T(8,128)(2,1)S(1)}, bf16[1024,128]{1,0:T(8,128)(2,1)S(1)}, u32[]{:S(2)}, u32[]{:S(2)}) collective-permute-start(bf16[1024,128]{1,0:T(8,128)(2,1)S(1)} %get-tuple-element.39), channel_id=1, source_target_pairs={{0,16},{1,5},{2,18},{3,7},{4,20},{5,9},{6,22},{7,11},{8,24},{9,13}... | collective-permute-start | bytes 786440 | tf_op jit(solution)/shard_map/ppermute | solution.py:36
  21.0 1.5 %collective-permute-start.6 = (bf16[1024,128]{1,0:T(8,128)(2,1)S(1)}, bf16[1024,128]{1,0:T(8,128)(2,1)S(1)}, u32[]{:S(2)}, u32[]{:S(2)}) collective-permute-start(bf16[1024,128]{1,0:T(8,128)(2,1)S(1)} %get-tuple-element.39), channel_id=1, source_target_pairs={{0,48},{1,13},{2,50},{3,15},{4,52},{5,1},{6,54},{7,3},{8,56},{9,5}... | collective-permute-start | bytes 786440 | tf_op jit(solution)/shard_map/ppermute | solution.py:36
  22.5 1.6 %collective-permute-start.7 = (bf16[1024,128]{1,0:T(8,128)(2,1)S(1)}, bf16[1024,128]{1,0:T(8,128)(2,1)S(1)}, u32[]{:S(2)}, u32[]{:S(2)}) collective-permute-start(bf16[1024,128]{1,0:T(8,128)(2,1)S(1)} %get-tuple-element.39), channel_id=1, source_target_pairs={{0,32},{1,9},{2,34},{3,11},{4,36},{5,13},{6,38},{7,15},{8,40},{9,1... | collective-permute-start | bytes 786440 | tf_op jit(solution)/shard_map/ppermute | solution.py:36
  24.1 2.4 %collective-permute-done.5 = bf16[1024,128]{1,0:T(8,128)(2,1)S(1)} collective-permute-done((bf16[1024,128]{1,0:T(8,128)(2,1)S(1)}, bf16[1024,128]{1,0:T(8,128)(2,1)S(1)}, u32[]{:S(2)}, u32[]{:S(2)}) %collective-permute-start.5) | collective-permute-done | bytes 262176 | tf_op jit(solution)/shard_map/ppermute | solution.py:36
  26.5 2.1 %collective-permute-done.6 = bf16[1024,128]{1,0:T(8,128)(2,1)S(1)} collective-permute-done((bf16[1024,128]{1,0:T(8,128)(2,1)S(1)}, bf16[1024,128]{1,0:T(8,128)(2,1)S(1)}, u32[]{:S(2)}, u32[]{:S(2)}) %collective-permute-start.6) | collective-permute-done | bytes 262176 | tf_op jit(solution)/shard_map/ppermute | solution.py:36
  28.7 1.5 %collective-permute-done.7 = bf16[1024,128]{1,0:T(8,128)(2,1)S(1)} collective-permute-done((bf16[1024,128]{1,0:T(8,128)(2,1)S(1)}, bf16[1024,128]{1,0:T(8,128)(2,1)S(1)}, u32[]{:S(2)}, u32[]{:S(2)}) %collective-permute-start.7) | collective-permute-done | bytes 262176 | tf_op jit(solution)/shard_map/ppermute | solution.py:36
  31.6 1.5 %collective-permute-start.9 = (bf16[4096,128]{1,0:T(8,128)(2,1)S(1)}, bf16[4096,128]{1,0:T(8,128)(2,1)S(1)}, u32[]{:S(2)}, u32[]{:S(2)}) collective-permute-start(bf16[4096,128]{1,0:T(8,128)(2,1)S(1)} %constant_dynamic-update-slice_fusion.6.feat_a), channel_id=1, source_target_pairs={{0,12},{1,49},{2,14},{3,51},{4,0},{5,53},{6,2},{7,55},{8,4},{9,57}... | collective-permute-start | bytes 3145736 | tf_op jit(solution)/shard_map/ppermute | solution.py:36
  33.8 3.4 %copy-done = bf16[128,32768]{1,0:T(8,128)(2,1)S(1)} copy-done((bf16[128,32768]{1,0:T(8,128)(2,1)S(1)}, bf16[128,32768]{1,0:T(8,128)(2,1)}, u32[]{:S(2)}) %copy-start) | copy-done | bytes 8388632
  37.1 5.1 %shard_map.94 = (bf16[8,128,4096]{2,1,0:T(8,128)(2,1)S(1)}, f32[128,128]{1,0:T(8,128)S(1)}) custom-call(s32[320]{0:T(512)S(1)} %pad_add_fusion.table, bf16[128,32768]{1,0:T(8,128)(2,1)S(1)} %copy-done), custom_call_target="tpu_custom_call" | custom-call | flops 1024 | bytes 1024 | tf_op jit(solution)/shard_map/pallas_call | solution.py:119
  42.3 2.1 %shard_map.95 = (f32[128,128]{1,0:T(8,128)S(1)}, bf16[16,128]{1,0:T(8,128)(2,1)S(1)}) custom-call(bf16[8,128,4096]{2,1,0:T(8,128)(2,1)S(1)} %get-tuple-element.20.ordered, bf16[4096,128]{1,0:T(8,128)(2,1)S(1)} %constant_dynamic-update-slice_fusion.6.feat_a, bf16[4096,128]{1,0:T(8,128)(2,1)} %collective-permute-done.10.feat_b, ...), custom_call_target="tpu_custom_call" | custom-call | flops 1024 | bytes 1024 | tf_op jit(solution)/shard_map/pallas_call | solution.py:151
  46.9 1.3 %collective-permute-start.11 = (bf16[2048,128]{1,0:T(8,128)(2,1)S(1)}, bf16[2048,128]{1,0:T(8,128)(2,1)S(1)}, u32[]{:S(2)}, u32[]{:S(2)}) collective-permute-start(bf16[2048,128]{1,0:T(8,128)(2,1)S(1)} %slice.12), channel_id=1, source_target_pairs={{0,4},{1,17},{2,6},{3,19},{4,8},{5,21},{6,10},{7,23},{8,12},{9,25}... | collective-permute-start | bytes 1572872 | tf_op jit(solution)/shard_map/ppermute | solution.py:36
  48.2 1.5 %collective-permute-start.12 = (bf16[2048,128]{1,0:T(8,128)(2,1)S(1)}, bf16[2048,128]{1,0:T(8,128)(2,1)S(1)}, u32[]{:S(2)}, u32[]{:S(2)}) collective-permute-start(bf16[2048,128]{1,0:T(8,128)(2,1)S(1)} %slice.13), channel_id=1, source_target_pairs={{0,12},{1,49},{2,14},{3,51},{4,0},{5,53},{6,2},{7,55},{8,4},{9,57}... | collective-permute-start | bytes 1572872 | tf_op jit(solution)/shard_map/ppermute | solution.py:36
  51.5 5.0 %collective-permute-done.11.feat_a = bf16[2048,128]{1,0:T(8,128)(2,1)S(1)} collective-permute-done((bf16[2048,128]{1,0:T(8,128)(2,1)S(1)}, bf16[2048,128]{1,0:T(8,128)(2,1)S(1)}, u32[]{:S(2)}, u32[]{:S(2)}) %collective-permute-start.11) | collective-permute-done | bytes 524320 | tf_op jit(solution)/shard_map/ppermute | solution.py:36
  56.5 1.4 %collective-permute-start.15 = (bf16[2048,128]{1,0:T(8,128)(2,1)S(1)}, bf16[2048,128]{1,0:T(8,128)(2,1)S(1)}, u32[]{:S(2)}, u32[]{:S(2)}) collective-permute-start(bf16[2048,128]{1,0:T(8,128)(2,1)S(1)} %collective-permute-done.11.feat_a), channel_id=1, source_target_pairs={{0,1},{1,0},{2,3},{3,2},{4,5},{5,4},{6,7},{7,6},{8,9},{9,8},{10,11... | collective-permute-start | bytes 1572872 | tf_op jit(solution)/shard_map/ppermute | solution.py:36
  57.9 1.5 %collective-permute-done.15.feat_b = bf16[2048,128]{1,0:T(8,128)(2,1)S(1)} collective-permute-done((bf16[2048,128]{1,0:T(8,128)(2,1)S(1)}, bf16[2048,128]{1,0:T(8,128)(2,1)S(1)}, u32[]{:S(2)}, u32[]{:S(2)}) %collective-permute-start.15) | collective-permute-done | bytes 524320 | tf_op jit(solution)/shard_map/ppermute | solution.py:36
  60.2 1.9 %shard_map.98 = (bf16[128,256]{1,0:T(8,128)(2,1)}, f32[136,128]{1,0:T(8,128)S(1)}, f32[136,128]{1,0:T(8,128)S(1)}) custom-call(s32[1]{0:T(128)} %bitcast.core, bf16[8,128,4096]{2,1,0:T(8,128)(2,1)S(1)} %get-tuple-element.20.ordered, bf16[2048,128]{1,0:T(8,128)(2,1)S(1)} %collective-permute-done.11.feat_a, ...), custom_call_target="tpu_custom_call" | custom-call | flops 1024 | bytes 1024 | tf_op jit(solution)/shard_map/pallas_call | solution.py:198
  63.4 3.3 %collective-permute-start.18 = (f32[136,128]{1,0:T(8,128)S(1)}, f32[136,128]{1,0:T(8,128)S(1)}, u32[]{:S(2)}, u32[]{:S(2)}) collective-permute-start(f32[136,128]{1,0:T(8,128)S(1)} %add.57), channel_id=1, source_target_pairs={{0,32},{1,9},{2,34},{3,11},{4,36},{5,13},{6,38},{7,15},{8,40},{9,1... | collective-permute-start | bytes 208904 | tf_op jit(solution)/shard_map/ppermute | solution.py:36
  67.2 2.1 %collective-permute-start.20 = (f32[136,128]{1,0:T(8,128)S(1)}, f32[136,128]{1,0:T(8,128)S(1)}, u32[]{:S(2)}, u32[]{:S(2)}) collective-permute-start(f32[136,128]{1,0:T(8,128)S(1)} %add.57), channel_id=1, source_target_pairs={{0,48},{1,13},{2,50},{3,15},{4,52},{5,1},{6,54},{7,3},{8,56},{9,5}... | collective-permute-start | bytes 208904 | tf_op jit(solution)/shard_map/ppermute | solution.py:36
  69.3 2.0 %collective-permute-done.19 = f32[136,128]{1,0:T(8,128)S(1)} collective-permute-done((f32[136,128]{1,0:T(8,128)S(1)}, f32[136,128]{1,0:T(8,128)S(1)}, u32[]{:S(2)}, u32[]{:S(2)}) %collective-permute-start.19) | collective-permute-done | bytes 69664 | tf_op jit(solution)/shard_map/ppermute | solution.py:36
  71.3 2.5 %collective-permute-start.21 = (f32[136,128]{1,0:T(8,128)S(1)}, f32[136,128]{1,0:T(8,128)S(1)}, u32[]{:S(2)}, u32[]{:S(2)}) collective-permute-start(f32[136,128]{1,0:T(8,128)S(1)} %add_add_fusion.2), channel_id=1, source_target_pairs={{0,8},{1,33},{2,10},{3,35},{4,12},{5,37},{6,14},{7,39},{8,0},{9,41... | collective-permute-start | bytes 208904 | tf_op jit(solution)/shard_map/ppermute | solution.py:36
  74.2 2.4 %collective-permute-start.23 = (f32[136,128]{1,0:T(8,128)S(1)}, f32[136,128]{1,0:T(8,128)S(1)}, u32[]{:S(2)}, u32[]{:S(2)}) collective-permute-start(f32[136,128]{1,0:T(8,128)S(1)} %add_add_fusion.2), channel_id=1, source_target_pairs={{0,12},{1,49},{2,14},{3,51},{4,0},{5,53},{6,2},{7,55},{8,4},{9,57}... | collective-permute-start | bytes 208904 | tf_op jit(solution)/shard_map/ppermute | solution.py:36
  76.6 1.7 %collective-permute-done.22 = f32[136,128]{1,0:T(8,128)S(1)} collective-permute-done((f32[136,128]{1,0:T(8,128)S(1)}, f32[136,128]{1,0:T(8,128)S(1)}, u32[]{:S(2)}, u32[]{:S(2)}) %collective-permute-start.22) | collective-permute-done | bytes 69664 | tf_op jit(solution)/shard_map/ppermute | solution.py:36
  78.3 2.5 %collective-permute-start.24 = (f32[136,128]{1,0:T(8,128)S(1)}, f32[136,128]{1,0:T(8,128)S(1)}, u32[]{:S(2)}, u32[]{:S(2)}) collective-permute-start(f32[136,128]{1,0:T(8,128)S(1)} %add_add_fusion.1), channel_id=1, source_target_pairs={{0,2},{1,3},{2,0},{3,1},{4,6},{5,7},{6,4},{7,5},{8,10},{9,11},{10,... | collective-permute-start | bytes 208904 | tf_op jit(solution)/shard_map/ppermute | solution.py:36
  80.8 1.7 %collective-permute-done.24 = f32[136,128]{1,0:T(8,128)S(1)} collective-permute-done((f32[136,128]{1,0:T(8,128)S(1)}, f32[136,128]{1,0:T(8,128)S(1)}, u32[]{:S(2)}, u32[]{:S(2)}) %collective-permute-start.24) | collective-permute-done | bytes 69664 | tf_op jit(solution)/shard_map/ppermute | solution.py:36
  82.5 3.8 %collective-permute-start.25 = (f32[136,128]{1,0:T(8,128)S(1)}, f32[136,128]{1,0:T(8,128)S(1)}, u32[]{:S(2)}, u32[]{:S(2)}) collective-permute-start(f32[136,128]{1,0:T(8,128)S(1)} %add.64), channel_id=1, source_target_pairs={{0,128},{1,129},{2,130},{3,131},{4,132},{5,133},{6,134},{7,135},{8... | collective-permute-start | bytes 208904 | tf_op jit(solution)/shard_map/ppermute | solution.py:36
  87.0 2.8 %collective-permute-start.27 = (f32[136,128]{1,0:T(8,128)S(1)}, f32[136,128]{1,0:T(8,128)S(1)}, u32[]{:S(2)}, u32[]{:S(2)}) collective-permute-start(f32[136,128]{1,0:T(8,128)S(1)} %add.64), channel_id=1, source_target_pairs={{0,192},{1,193},{2,194},{3,195},{4,196},{5,197},{6,198},{7,199},{8... | collective-permute-start | bytes 208904 | tf_op jit(solution)/shard_map/ppermute | solution.py:36
  90.2 1.3 %collective-permute-done.26 = f32[136,128]{1,0:T(8,128)S(1)} collective-permute-done((f32[136,128]{1,0:T(8,128)S(1)}, f32[136,128]{1,0:T(8,128)S(1)}, u32[]{:S(2)}, u32[]{:S(2)}) %collective-permute-start.26) | collective-permute-done | bytes 69664 | tf_op jit(solution)/shard_map/ppermute | solution.py:36
  92.4 5.1 %collective-permute-start.28 = (f32[136,128]{1,0:T(8,128)S(1)}, f32[136,128]{1,0:T(8,128)S(1)}, u32[]{:S(2)}, u32[]{:S(2)}) collective-permute-start(f32[136,128]{1,0:T(8,128)S(1)} %add_add_fusion), channel_id=1, source_target_pairs={{0,1},{1,0},{2,3},{3,2},{4,5},{5,4},{6,7},{7,6},{8,9},{9,8},{10,11... | collective-permute-start | bytes 208904 | tf_op jit(solution)/shard_map/ppermute | solution.py:36
  (65 shorter events, 16.1 us)
Async XLA Ops:
  0.6 4.4 %collective-permute-start = (bf16[128,128]{1,0:T(8,128)(2,1)}, bf16[128,128]{1,0:T(8,128)(2,1)S(1)}, u32[]{:S(2)}, u32[]{:S(2)}) collective-permute-start(bf16[128,128]{1,0:T(8,128)(2,1)} %own.1), channel_id=1, source_target_pairs={{0,1},{1,0},{2,3},{3,2},{4,5},{5,4},{6,7},{7,6},{8,9},{9,8},{10,11... | collective-permute-start | bytes 98312 | tf_op jit(solution)/shard_map/ppermute | solution.py:36
  5.0 11.9 %collective-permute-start.1 = (bf16[256,128]{1,0:T(8,128)(2,1)S(1)}, bf16[256,128]{1,0:T(8,128)(2,1)S(1)}, u32[]{:S(2)}, u32[]{:S(2)}) collective-permute-start(bf16[256,128]{1,0:T(8,128)(2,1)S(1)} %constant_dynamic-update-slice_fusion), channel_id=1, source_target_pairs={{0,0},{1,129},{2,2},{3,131},{4,4},{5,133},{6,6},{7,135},{8,8},{9,1... | collective-permute-start | bytes 196616 | tf_op jit(solution)/shard_map/ppermute | solution.py:36
  12.1 4.9 %collective-permute-start.2 = (bf16[256,128]{1,0:T(8,128)(2,1)S(1)}, bf16[256,128]{1,0:T(8,128)(2,1)S(1)}, u32[]{:S(2)}, u32[]{:S(2)}) collective-permute-start(bf16[256,128]{1,0:T(8,128)(2,1)S(1)} %constant_dynamic-update-slice_fusion), channel_id=1, source_target_pairs={{0,2},{1,195},{2,64},{3,1},{4,6},{5,199},{6,68},{7,5},{8,10},{9,20... | collective-permute-start | bytes 196616 | tf_op jit(solution)/shard_map/ppermute | solution.py:36
  12.2 6.0 %collective-permute-start.3 = (bf16[256,128]{1,0:T(8,128)(2,1)S(1)}, bf16[256,128]{1,0:T(8,128)(2,1)S(1)}, u32[]{:S(2)}, u32[]{:S(2)}) collective-permute-start(bf16[256,128]{1,0:T(8,128)(2,1)S(1)} %constant_dynamic-update-slice_fusion), channel_id=1, source_target_pairs={{0,64},{1,193},{2,66},{3,195},{4,68},{5,197},{6,70},{7,199},{8,72}... | collective-permute-start | bytes 196616 | tf_op jit(solution)/shard_map/ppermute | solution.py:36
  12.3 7.3 %collective-permute-start.4 = (bf16[256,128]{1,0:T(8,128)(2,1)S(1)}, bf16[256,128]{1,0:T(8,128)(2,1)S(1)}, u32[]{:S(2)}, u32[]{:S(2)}) collective-permute-start(bf16[256,128]{1,0:T(8,128)(2,1)S(1)} %constant_dynamic-update-slice_fusion), channel_id=1, source_target_pairs={{0,66},{1,131},{2,128},{3,193},{4,70},{5,135},{6,132},{7,197},{8,7... | collective-permute-start | bytes 196616 | tf_op jit(solution)/shard_map/ppermute | solution.py:36
  19.6 6.9 %collective-permute-start.5 = (bf16[1024,128]{1,0:T(8,128)(2,1)S(1)}, bf16[1024,128]{1,0:T(8,128)(2,1)S(1)}, u32[]{:S(2)}, u32[]{:S(2)}) collective-permute-start(bf16[1024,128]{1,0:T(8,128)(2,1)S(1)} %get-tuple-element.39), channel_id=1, source_target_pairs={{0,16},{1,5},{2,18},{3,7},{4,20},{5,9},{6,22},{7,11},{8,24},{9,13}... | collective-permute-start | bytes 786440 | tf_op jit(solution)/shard_map/ppermute | solution.py:36
  21.0 7.7 %collective-permute-start.6 = (bf16[1024,128]{1,0:T(8,128)(2,1)S(1)}, bf16[1024,128]{1,0:T(8,128)(2,1)S(1)}, u32[]{:S(2)}, u32[]{:S(2)}) collective-permute-start(bf16[1024,128]{1,0:T(8,128)(2,1)S(1)} %get-tuple-element.39), channel_id=1, source_target_pairs={{0,48},{1,13},{2,50},{3,15},{4,52},{5,1},{6,54},{7,3},{8,56},{9,5}... | collective-permute-start | bytes 786440 | tf_op jit(solution)/shard_map/ppermute | solution.py:36
  22.5 7.7 %collective-permute-start.7 = (bf16[1024,128]{1,0:T(8,128)(2,1)S(1)}, bf16[1024,128]{1,0:T(8,128)(2,1)S(1)}, u32[]{:S(2)}, u32[]{:S(2)}) collective-permute-start(bf16[1024,128]{1,0:T(8,128)(2,1)S(1)} %get-tuple-element.39), channel_id=1, source_target_pairs={{0,32},{1,9},{2,34},{3,11},{4,36},{5,13},{6,38},{7,15},{8,40},{9,1... | collective-permute-start | bytes 786440 | tf_op jit(solution)/shard_map/ppermute | solution.py:36
  30.2 12.1 %collective-permute-start.10 = (bf16[4096,128]{1,0:T(8,128)(2,1)S(1)}, bf16[4096,128]{1,0:T(8,128)(2,1)}, u32[]{:S(2)}, u32[]{:S(2)}) collective-permute-start(bf16[4096,128]{1,0:T(8,128)(2,1)S(1)} %constant_dynamic-update-slice_fusion.6.feat_a), channel_id=1, source_target_pairs={{0,1},{1,0},{2,3},{3,2},{4,5},{5,4},{6,7},{7,6},{8,9},{9,8},{10,11... | collective-permute-start | bytes 3145736 | tf_op jit(solution)/shard_map/ppermute | solution.py:36
  30.3 15.2 %collective-permute-start.8 = (bf16[4096,128]{1,0:T(8,128)(2,1)S(1)}, bf16[4096,128]{1,0:T(8,128)(2,1)S(1)}, u32[]{:S(2)}, u32[]{:S(2)}) collective-permute-start(bf16[4096,128]{1,0:T(8,128)(2,1)S(1)} %constant_dynamic-update-slice_fusion.6.feat_a), channel_id=1, source_target_pairs={{0,4},{1,17},{2,6},{3,19},{4,8},{5,21},{6,10},{7,23},{8,12},{9,25}... | collective-permute-start | bytes 3145736 | tf_op jit(solution)/shard_map/ppermute | solution.py:36
  31.6 13.9 %collective-permute-start.9 = (bf16[4096,128]{1,0:T(8,128)(2,1)S(1)}, bf16[4096,128]{1,0:T(8,128)(2,1)S(1)}, u32[]{:S(2)}, u32[]{:S(2)}) collective-permute-start(bf16[4096,128]{1,0:T(8,128)(2,1)S(1)} %constant_dynamic-update-slice_fusion.6.feat_a), channel_id=1, source_target_pairs={{0,12},{1,49},{2,14},{3,51},{4,0},{5,53},{6,2},{7,55},{8,4},{9,57}... | collective-permute-start | bytes 3145736 | tf_op jit(solution)/shard_map/ppermute | solution.py:36
  45.5 4.2 %collective-permute-start.14 = (bf16[4096,128]{1,0:T(8,128)(2,1)S(1)}, bf16[4096,128]{1,0:T(8,128)(2,1)S(1)}, u32[]{:S(2)}, u32[]{:S(2)}) collective-permute-start(bf16[4096,128]{1,0:T(8,128)(2,1)S(1)} %collective-permute-done.8.feat_a), channel_id=1, source_target_pairs={{0,1},{1,0},{2,3},{3,2},{4,5},{5,4},{6,7},{7,6},{8,9},{9,8},{10,11... | collective-permute-start | bytes 3145736 | tf_op jit(solution)/shard_map/ppermute | solution.py:36
  46.8 3.8 %collective-permute-start.13 = (bf16[4096,128]{1,0:T(8,128)(2,1)S(1)}, bf16[4096,128]{1,0:T(8,128)(2,1)S(1)}, u32[]{:S(2)}, u32[]{:S(2)}) collective-permute-start(bf16[4096,128]{1,0:T(8,128)(2,1)S(1)} %collective-permute-done.9.feat_a), channel_id=1, source_target_pairs={{0,1},{1,0},{2,3},{3,2},{4,5},{5,4},{6,7},{7,6},{8,9},{9,8},{10,11... | collective-permute-start | bytes 3145736 | tf_op jit(solution)/shard_map/ppermute | solution.py:36
  46.9 9.6 %collective-permute-start.11 = (bf16[2048,128]{1,0:T(8,128)(2,1)S(1)}, bf16[2048,128]{1,0:T(8,128)(2,1)S(1)}, u32[]{:S(2)}, u32[]{:S(2)}) collective-permute-start(bf16[2048,128]{1,0:T(8,128)(2,1)S(1)} %slice.12), channel_id=1, source_target_pairs={{0,4},{1,17},{2,6},{3,19},{4,8},{5,21},{6,10},{7,23},{8,12},{9,25}... | collective-permute-start | bytes 1572872 | tf_op jit(solution)/shard_map/ppermute | solution.py:36
  48.2 8.3 %collective-permute-start.12 = (bf16[2048,128]{1,0:T(8,128)(2,1)S(1)}, bf16[2048,128]{1,0:T(8,128)(2,1)S(1)}, u32[]{:S(2)}, u32[]{:S(2)}) collective-permute-start(bf16[2048,128]{1,0:T(8,128)(2,1)S(1)} %slice.13), channel_id=1, source_target_pairs={{0,12},{1,49},{2,14},{3,51},{4,0},{5,53},{6,2},{7,55},{8,4},{9,57}... | collective-permute-start | bytes 1572872 | tf_op jit(solution)/shard_map/ppermute | solution.py:36
  49.7 10.4 %copy-start.1 = (bf16[128,128]{1,0:T(8,128)(2,1)S(1)}, bf16[128,128]{1,0:T(8,128)(2,1)}, u32[]{:S(2)}) copy-start(bf16[128,128]{1,0:T(8,128)(2,1)} %own.1) | copy-start | bytes 98308
  49.7 10.4 %copy-start.2 = (bf16[128,256]{1,0:T(8,128)(2,1)S(1)}, bf16[128,256]{1,0:T(8,128)(2,1)}, u32[]{:S(2)}) copy-start(bf16[128,256]{1,0:T(8,128)(2,1)} %weight.1) | copy-start | bytes 196612
  49.7 10.4 %copy-start.3 = (bf16[128,256]{1,0:T(8,128)(2,1)S(1)}, bf16[128,256]{1,0:T(8,128)(2,1)}, u32[]{:S(2)}) copy-start(bf16[128,256]{1,0:T(8,128)(2,1)} %cotangent.1) | copy-start | bytes 196612
  56.5 2.9 %collective-permute-start.15 = (bf16[2048,128]{1,0:T(8,128)(2,1)S(1)}, bf16[2048,128]{1,0:T(8,128)(2,1)S(1)}, u32[]{:S(2)}, u32[]{:S(2)}) collective-permute-start(bf16[2048,128]{1,0:T(8,128)(2,1)S(1)} %collective-permute-done.11.feat_a), channel_id=1, source_target_pairs={{0,1},{1,0},{2,3},{3,2},{4,5},{5,4},{6,7},{7,6},{8,9},{9,8},{10,11... | collective-permute-start | bytes 1572872 | tf_op jit(solution)/shard_map/ppermute | solution.py:36
  57.9 2.3 %collective-permute-start.16 = (bf16[2048,128]{1,0:T(8,128)(2,1)S(1)}, bf16[2048,128]{1,0:T(8,128)(2,1)S(1)}, u32[]{:S(2)}, u32[]{:S(2)}) collective-permute-start(bf16[2048,128]{1,0:T(8,128)(2,1)S(1)} %collective-permute-done.12.feat_a2), channel_id=1, source_target_pairs={{0,1},{1,0},{2,3},{3,2},{4,5},{5,4},{6,7},{7,6},{8,9},{9,8},{10,11... | collective-permute-start | bytes 1572872 | tf_op jit(solution)/shard_map/ppermute | solution.py:36
  62.1 1.3 %collective-permute-start.17 = (f32[136,128]{1,0:T(8,128)S(1)}, f32[136,128]{1,0:T(8,128)S(1)}, u32[]{:S(2)}, u32[]{:S(2)}) collective-permute-start(f32[136,128]{1,0:T(8,128)S(1)} %get-tuple-element.36), channel_id=1, source_target_pairs={{0,1},{1,0},{2,3},{3,2},{4,5},{5,4},{6,7},{7,6},{8,9},{9,8},{10,11... | collective-permute-start | bytes 208904 | tf_op jit(solution)/shard_map/ppermute | solution.py:36
  63.4 6.0 %collective-permute-start.18 = (f32[136,128]{1,0:T(8,128)S(1)}, f32[136,128]{1,0:T(8,128)S(1)}, u32[]{:S(2)}, u32[]{:S(2)}) collective-permute-start(f32[136,128]{1,0:T(8,128)S(1)} %add.57), channel_id=1, source_target_pairs={{0,32},{1,9},{2,34},{3,11},{4,36},{5,13},{6,38},{7,15},{8,40},{9,1... | collective-permute-start | bytes 208904 | tf_op jit(solution)/shard_map/ppermute | solution.py:36
  66.7 4.7 %collective-permute-start.19 = (f32[136,128]{1,0:T(8,128)S(1)}, f32[136,128]{1,0:T(8,128)S(1)}, u32[]{:S(2)}, u32[]{:S(2)}) collective-permute-start(f32[136,128]{1,0:T(8,128)S(1)} %add.57), channel_id=1, source_target_pairs={{0,16},{1,5},{2,18},{3,7},{4,20},{5,9},{6,22},{7,11},{8,24},{9,13}... | collective-permute-start | bytes 208904 | tf_op jit(solution)/shard_map/ppermute | solution.py:36
  67.2 4.1 %collective-permute-start.20 = (f32[136,128]{1,0:T(8,128)S(1)}, f32[136,128]{1,0:T(8,128)S(1)}, u32[]{:S(2)}, u32[]{:S(2)}) collective-permute-start(f32[136,128]{1,0:T(8,128)S(1)} %add.57), channel_id=1, source_target_pairs={{0,48},{1,13},{2,50},{3,15},{4,52},{5,1},{6,54},{7,3},{8,56},{9,5}... | collective-permute-start | bytes 208904 | tf_op jit(solution)/shard_map/ppermute | solution.py:36
  71.3 5.2 %collective-permute-start.21 = (f32[136,128]{1,0:T(8,128)S(1)}, f32[136,128]{1,0:T(8,128)S(1)}, u32[]{:S(2)}, u32[]{:S(2)}) collective-permute-start(f32[136,128]{1,0:T(8,128)S(1)} %add_add_fusion.2), channel_id=1, source_target_pairs={{0,8},{1,33},{2,10},{3,35},{4,12},{5,37},{6,14},{7,39},{8,0},{9,41... | collective-permute-start | bytes 208904 | tf_op jit(solution)/shard_map/ppermute | solution.py:36
  73.9 4.4 %collective-permute-start.22 = (f32[136,128]{1,0:T(8,128)S(1)}, f32[136,128]{1,0:T(8,128)S(1)}, u32[]{:S(2)}, u32[]{:S(2)}) collective-permute-start(f32[136,128]{1,0:T(8,128)S(1)} %add_add_fusion.2), channel_id=1, source_target_pairs={{0,4},{1,17},{2,6},{3,19},{4,8},{5,21},{6,10},{7,23},{8,12},{9,25}... | collective-permute-start | bytes 208904 | tf_op jit(solution)/shard_map/ppermute | solution.py:36
  74.2 4.1 %collective-permute-start.23 = (f32[136,128]{1,0:T(8,128)S(1)}, f32[136,128]{1,0:T(8,128)S(1)}, u32[]{:S(2)}, u32[]{:S(2)}) collective-permute-start(f32[136,128]{1,0:T(8,128)S(1)} %add_add_fusion.2), channel_id=1, source_target_pairs={{0,12},{1,49},{2,14},{3,51},{4,0},{5,53},{6,2},{7,55},{8,4},{9,57}... | collective-permute-start | bytes 208904 | tf_op jit(solution)/shard_map/ppermute | solution.py:36
  78.3 4.2 %collective-permute-start.24 = (f32[136,128]{1,0:T(8,128)S(1)}, f32[136,128]{1,0:T(8,128)S(1)}, u32[]{:S(2)}, u32[]{:S(2)}) collective-permute-start(f32[136,128]{1,0:T(8,128)S(1)} %add_add_fusion.1), channel_id=1, source_target_pairs={{0,2},{1,3},{2,0},{3,1},{4,6},{5,7},{6,4},{7,5},{8,10},{9,11},{10,... | collective-permute-start | bytes 208904 | tf_op jit(solution)/shard_map/ppermute | solution.py:36
  82.5 7.7 %collective-permute-start.25 = (f32[136,128]{1,0:T(8,128)S(1)}, f32[136,128]{1,0:T(8,128)S(1)}, u32[]{:S(2)}, u32[]{:S(2)}) collective-permute-start(f32[136,128]{1,0:T(8,128)S(1)} %add.64), channel_id=1, source_target_pairs={{0,128},{1,129},{2,130},{3,131},{4,132},{5,133},{6,134},{7,135},{8... | collective-permute-start | bytes 208904 | tf_op jit(solution)/shard_map/ppermute | solution.py:36
  86.3 5.3 %collective-permute-start.26 = (f32[136,128]{1,0:T(8,128)S(1)}, f32[136,128]{1,0:T(8,128)S(1)}, u32[]{:S(2)}, u32[]{:S(2)}) collective-permute-start(f32[136,128]{1,0:T(8,128)S(1)} %add.64), channel_id=1, source_target_pairs={{0,64},{1,65},{2,66},{3,67},{4,68},{5,69},{6,70},{7,71},{8,72},{9,... | collective-permute-start | bytes 208904 | tf_op jit(solution)/shard_map/ppermute | solution.py:36
  87.0 5.3 %collective-permute-start.27 = (f32[136,128]{1,0:T(8,128)S(1)}, f32[136,128]{1,0:T(8,128)S(1)}, u32[]{:S(2)}, u32[]{:S(2)}) collective-permute-start(f32[136,128]{1,0:T(8,128)S(1)} %add.64), channel_id=1, source_target_pairs={{0,192},{1,193},{2,194},{3,195},{4,196},{5,197},{6,198},{7,199},{8... | collective-permute-start | bytes 208904 | tf_op jit(solution)/shard_map/ppermute | solution.py:36
  92.4 6.0 %collective-permute-start.28 = (f32[136,128]{1,0:T(8,128)S(1)}, f32[136,128]{1,0:T(8,128)S(1)}, u32[]{:S(2)}, u32[]{:S(2)}) collective-permute-start(f32[136,128]{1,0:T(8,128)S(1)} %add_add_fusion), channel_id=1, source_target_pairs={{0,1},{1,0},{2,3},{3,2},{4,5},{5,4},{6,7},{7,6},{8,9},{9,8},{10,11... | collective-permute-start | bytes 208904 | tf_op jit(solution)/shard_map/ppermute | solution.py:36
  (2 other events, 13.8 us)

commit v3 on v2

--- a/solution.py
+++ b/solution.py
@@ -13,6 +13,7 @@
 PIECES = 8
 PIECE = 4096
 HALF = PIECE // 2
+FIRST = 3
 BLOCKS = PIECE // 128
 VMEM_LIMIT = 24 * 1024 * 1024
 
@@ -84,91 +85,110 @@
     outer, inner = jnp.where(first, from_y, from_x), jnp.where(first, from_x, from_y)
     hop = jnp.where(first, up, (8 - up) & 3)
     pair = (source & 1) ^ plane
-    place = outer * 64 + (plane ^ core) * 32 + inner * 8 + hop * 2 + pair
+    place = (plane ^ core) * 128 + outer * 32 + inner * 8 + hop * 2 + pair
     return jnp.concatenate([place, tile_mask[0] * (1 - skip_owner)])
 
 
-def order_kernel(table, adjacency, ordered, degree):
-    chunk = pl.program_id(0)
-
-    def one_partition(owner, total):
-        owner = chunk * (BLOCKS // 4) + owner
-        live = table[PIECES * BLOCKS + owner].astype(jnp.float32)
-        live = jnp.full((1, 1), live).astype(jnp.bfloat16)
-        for block in range(4):
-            place = table[owner * 4 + block]
-            start = (owner * 4 + block - chunk * BLOCKS) * 128
-            values = adjacency[:, pl.ds(pl.multiple_of(start, 128), 128)] * live
-            ordered[place >> 5, :, pl.ds(pl.multiple_of((place & 31) * 128, 128), 128)] = values
-            total = total + values.astype(jnp.float32)
-        return total
-
-    @pl.when(chunk == 0)
-    def _():
-        degree[...] = jnp.zeros_like(degree)
-
-    degree[...] = lax.fori_loop(0, BLOCKS // 4, one_partition, degree[...], unroll=2)
+def order_kernel(first, table, adjacency, *refs):
+    own, give, degree = refs[-3:]
+    chunk = pl.program_id(0) + first
+
+    if first == 0:
+
+        @pl.when(chunk == 0)
+        def _():
+            degree[...] = jnp.zeros_like(degree)
+
+    else:
+
+        @pl.when(chunk == first)
+        def _():
+            degree[...] = refs[2][...]
+
+    def put(out, low):
+        total = degree[...]
+        for chip in range(low, BLOCKS // 2, 2):
+            live = table[PIECES * BLOCKS + chunk * (BLOCKS // 4) + chip // 2].astype(jnp.float32)
+            live = jnp.full((1, 1), live).astype(jnp.bfloat16)
+            for block in (chip * 2, chip * 2 + 1):
+                spot = table[chunk * BLOCKS + block]
+                values = adjacency[:, block * 128 : block * 128 + 128] * live
+                out[(spot >> 5) & 3, :, pl.ds(pl.multiple_of((spot & 31) * 128, 128), 128)] = values
+                total = total + values.astype(jnp.float32)
+        degree[...] = total
+
+    for low in range(2):
+        place = table[chunk * BLOCKS + low * 2]
+        pl.when(place < 128)(functools.partial(put, own, low))
+        pl.when(place >= 128)(functools.partial(put, give, low))
 
     @pl.when(chunk == PIECES - 1)
     def _():
         degree[...] = jnp.broadcast_to(1.0 + jnp.sum(degree[...], axis=1, keepdims=True), (128, 128))
 
 
-def order_adjacency(table, adjacency):
+def order_adjacency(first, count, table, adjacency, *before):
     vmem = pl.BlockSpec(memory_space=pltpu.VMEM)
     return pl.pallas_call(
-        order_kernel,
+        functools.partial(order_kernel, first),
         out_shape=[
-            jax.ShapeDtypeStruct((PIECES, 128, PIECE), jnp.bfloat16),
+            jax.ShapeDtypeStruct((PIECES // 2, 128, PIECE), jnp.bfloat16),
+            jax.ShapeDtypeStruct((PIECES // 2, 128, PIECE), jnp.bfloat16),
             jax.ShapeDtypeStruct((128, 128), jnp.float32),
         ],
-        grid=(PIECES,),
-        in_specs=[pl.BlockSpec(memory_space=pltpu.SMEM), pl.BlockSpec((128, PIECE), lambda chunk: (0, chunk))],
-        out_specs=[vmem, vmem],
+        grid=(count,),
+        in_specs=[
+            pl.BlockSpec(memory_space=pltpu.SMEM),
+            pl.BlockSpec((128, PIECE), lambda chunk: (0, chunk + first)),
+            *[vmem] * len(before),
+        ],
+        out_specs=[vmem] * 3,
+        input_output_aliases={2 + number: number for number in range(len(before))},
         compiler_params=pltpu.CompilerParams(vmem_limit_bytes=VMEM_LIMIT),
         cost_estimate=pl.CostEstimate(flops=1024, bytes_accessed=1024, transcendentals=0),
-    )(table, adjacency)
-
-
-def add_piece(ordered, piece, feat, total, largest, first=0):
-    for start in range(0, feat.shape[0], 512):
-        rows = feat[start : start + 512, :]
-        columns = ordered[piece, :, first + start : first + start + 512]
-        total = total + jnp.dot(columns, rows, preferred_element_type=jnp.float32)
-        largest = jnp.maximum(largest, jnp.max(jnp.abs(rows).reshape(32, 16, 128), axis=0))
-    return total, largest
-
-
-def piece_kernel(piece, ordered, feat_a, feat_b, total_in, largest_in, total_out, largest_out):
-    total, largest = add_piece(ordered, piece, feat_a, total_in[...], largest_in[...])
-    total, largest = add_piece(ordered, piece + 1, feat_b, total, largest)
-    total_out[...] = total
+    )(table, pltpu.with_memory_space_constraint(adjacency, pltpu.HBM), *before)
+
+
+def piece_kernel(spots, last, own, got, *refs):
+    feats, (ours, theirs, largest, ours_out, theirs_out, largest_out) = refs[: len(spots)], refs[len(spots) :]
+    ours, theirs, largest = ours[...], theirs[...], largest[...]
+    for (piece, first), feat in zip(spots, feats, strict=True):
+        for start in range(0, feat.shape[0], 512):
+            rows = feat[start : start + 512, :]
+            columns = slice(first + start, first + start + 512)
+            ours = ours + jnp.dot(own[piece, :, columns], rows, preferred_element_type=jnp.float32)
+            theirs = theirs + jnp.dot(got[piece, :, columns], rows, preferred_element_type=jnp.float32)
+            largest = jnp.maximum(largest, jnp.max(jnp.abs(rows).reshape(32, 16, 128), axis=0))
+    ours_out[...] = ours
     largest_out[...] = largest
-
-
-def piece_step(piece, ordered, feat_a, feat_b, total, largest):
+    theirs_out[:128, :] = theirs
+    if last:
+        wide = largest.astype(jnp.float32)
+        theirs_out[128:, :] = jnp.maximum(wide[:8], wide[8:])
+
+
+def piece_step(spots, last, own, got, feats, sums):
     vmem = pl.BlockSpec(memory_space=pltpu.VMEM)
     return pl.pallas_call(
-        functools.partial(piece_kernel, piece),
+        functools.partial(piece_kernel, spots, last),
         out_shape=[
             jax.ShapeDtypeStruct((128, 128), jnp.float32),
+            jax.ShapeDtypeStruct((136 if last else 128, 128), jnp.float32),
             jax.ShapeDtypeStruct((16, 128), jnp.bfloat16),
         ],
-        in_specs=[vmem] * 5,
-        out_specs=[vmem] * 2,
+        in_specs=[vmem] * (5 + len(spots)),
+        out_specs=[vmem] * 3,
         compiler_params=pltpu.CompilerParams(vmem_limit_bytes=VMEM_LIMIT // 2),
         cost_estimate=pl.CostEstimate(flops=1024, bytes_accessed=1024, transcendentals=0),
-    )(ordered, feat_a, feat_b, total, largest)
+    )(own, got, *feats, *sums)
 
 
 def last_kernel(
-    core, ordered, feat_a, feat_a2, feat_b, feat_b2, total_in, largest_in,
-    own, degree, weight, bias, cotangent, activated, mine, theirs,
+    core, ours, partial, largest_in, own, degree, weight, bias, cotangent, activated, mine, theirs
 ):
-    total, largest = total_in[...], largest_in[...]
-    for number, feat in enumerate((feat_a, feat_a2, feat_b, feat_b2)):
-        total, largest = add_piece(ordered, 6 + number // 2, feat, total, largest, number % 2 * HALF)
-    factor = 64.0 / (jnp.max(largest.astype(jnp.float32)) + 1e-06)
+    total = ours[...] + partial[:128, :]
+    largest = jnp.maximum(jnp.max(largest_in[...].astype(jnp.float32)), jnp.max(partial[128:, :]))
+    factor = 64.0 / (largest + 1e-06)
     summed = (total + own[...].astype(jnp.float32)) * factor
     mixed = (summed / degree[...]).astype(jnp.bfloat16)
     pre = jnp.dot(mixed, weight[...], preferred_element_type=jnp.float32) + bias[...]
@@ -202,7 +222,7 @@
             jax.ShapeDtypeStruct((136, 128), jnp.float32),
             jax.ShapeDtypeStruct((136, 128), jnp.float32),
         ],
-        in_specs=[pl.BlockSpec(memory_space=pltpu.SMEM)] + [vmem] * 12,
+        in_specs=[pl.BlockSpec(memory_space=pltpu.SMEM)] + [vmem] * 8,
         out_specs=[vmem] * 3,
         compiler_params=pltpu.CompilerParams(vmem_limit_bytes=VMEM_LIMIT // 2),
         cost_estimate=pl.CostEstimate(flops=1024, bytes_accessed=1024, transcendentals=0),
@@ -227,23 +247,31 @@
 
 
 def local(features, adjacency, tile_mask, skip_owner, weight, bias, cotangent):
-    ordered, degree = order_adjacency(place_table(tile_mask, skip_owner), adjacency)
+    table = place_table(tile_mask, skip_owner)
+    ordered = order_adjacency(0, FIRST, table, adjacency)
     chip = jnp.concatenate([features, swap_cores(features)])
     far = along_z(chip, 4)
     line = jnp.concatenate([far] + [along_z(chip, step) for step in (3, 2, 1)][::-1])
+    line, *ordered = lax.optimization_barrier((line, *ordered))
+    own, give, degree = order_adjacency(FIRST, PIECES - FIRST, table, adjacency, *ordered)
     plane = jnp.concatenate([line] + [along_xy(line, step, False) for step in SHIFTS[1:]])
-    after, before = along_xy(plane, 1, True), along_xy(plane, 3, True)
-    total = jnp.zeros((128, 128), jnp.float32)
-    largest = jnp.zeros((16, 128), jnp.bfloat16)
-    total, largest = piece_step(0, ordered, plane, swap_cores(plane), total, largest)
-    after, before, total = lax.optimization_barrier((after, before, total))
-    halves = along_xy(after[:HALF], 1, True), along_xy(before[HALF:], 3, True)
-    for number, feat in ((1, after), (2, before)):
-        total, largest = piece_step(2 * number, ordered, feat, swap_cores(feat), total, largest)
-    *halves, total = lax.optimization_barrier((*halves, total))
+    plane, own, give, degree = lax.optimization_barrier((plane, own, give, degree))
+    got = swap_cores(give)
+    front, back = plane[:HALF], plane[HALF:]
+    front_after, back_before = along_xy(front, 1, True), along_xy(back, 3, True)
+    back_after, front_before = along_xy(back, 1, True), along_xy(front, 3, True)
+    front_after, back_before, got = lax.optimization_barrier((front_after, back_before, got))
+    halves = along_xy(front_after, 1, True), along_xy(back_before, 3, True)
+    zero = jnp.zeros((128, 128), jnp.float32)
+    sums = zero, zero, jnp.zeros((16, 128), jnp.bfloat16)
+    sums = piece_step(
+        ((0, 0), (1, 0), (2, HALF)), False, own, got, (plane, front_after, back_before), sums
+    )
+    sums = piece_step(((1, HALF), (2, 0)), False, own, got, (back_after, front_before), sums)
+    ours, theirs, largest = piece_step(((3, 0), (3, HALF)), True, own, got, halves, sums)
     core = lax.axis_index("core")
     activated, mine, theirs = last_step(
-        core.reshape(1), ordered, *halves, *(swap_cores(half) for half in halves), total, largest,
+        core.reshape(1), ours, swap_cores(theirs), largest,
         features, degree, weight, bias.reshape(1, 256), cotangent,
     )
     return (activated, *sum_over_devices(mine, theirs, core))

time: 100 us -> 93.4 us (0.934)
  waiting for transfers between devices: 27 us -> 22.5 us
  local copies, waits for them, and re-layouts: 4.43 us -> 0.87 us
  Pallas kernels: 10.9 us -> 12.8 us
    ppermute x29 -> x28, waiting for transfers between devices: 27 us -> 22.5 us  [permute(): lax.ppermute(array, NAMES, [(index_of(*at), index_of(*move(*at))) for at...]
    unnamed x16 -> x9, local copies, waits for them, and re-layouts: 4.28 us -> 0.78 us
    pallas_call x4 -> x5, Pallas kernels: 8.99 us -> 11.7 us  [the longest x2 8.68 us: order_adjacency(): pl.pallas_call(functools.partial(order_kernel, first), out_shape=[jax.Sha...]
    ppermute x29 -> x28, starting transfers between devices: 54.5 us -> 53.7 us  [permute(): lax.ppermute(array, NAMES, [(index_of(*at), index_of(*move(*at))) for at...]
  transfers between devices with their start and end apart: 29 -> 28, of which waited for: 18 -> 13; matrix products, arithmetic and copies ran while one was open for 2% -> 2% of each run, Pallas kernels for 9% -> 12%
where the time goes in v3:
time: 93.4 us; the launch traced here: 92.8 us
  starting transfers between devices  53.7 us (57%)
  waiting for transfers between devices  22.5 us (24%)
  Pallas kernels  12.8 us (14%)
  other arithmetic  2.1 us (2%)
    ppermute x28, starting transfers between devices, permute(): lax.ppermute(array, NAMES, [(index_of(*at), index_of(*move(*at))) for at...  53.7 us
    ppermute x28, waiting for transfers between devices, permute(): lax.ppermute(array, NAMES, [(index_of(*at), index_of(*move(*at))) for at...  22.5 us
    pallas_call x2, Pallas kernels, order_adjacency(): pl.pallas_call(functools.partial(order_kernel, first), out_shape=[jax.Sha...  8.68 us
    pallas_call x3, Pallas kernels, piece_step(): pl.pallas_call(functools.partial(piece_kernel, spots, last), out_shape=[j...  3.01 us
  transfers between devices with their start and end apart: 28, of which 13 were waited for; matrix products, arithmetic and copies ran while one was open for 2% of the time, Pallas kernels for 12%

profile of v3, /device:TPU:1, one launch (start us, length us, event | category | flops | bytes accessed | tf_op | source)
XLA Modules:
  0.0 92.8 jit_solution(9337292694678487154)
XLA Ops:
  0.6 3.3 %collective-permute-start = (bf16[128,128]{1,0:T(8,128)(2,1)}, bf16[128,128]{1,0:T(8,128)(2,1)S(1)}, u32[]{:S(2)}, u32[]{:S(2)}) collective-permute-start(bf16[128,128]{1,0:T(8,128)(2,1)} %own.1), channel_id=1, source_target_pairs={{0,1},{1,0},{2,3},{3,2},{4,5},{5,4},{6,7},{7,6},{8,9},{9,8},{10,11... | collective-permute-start | bytes 98312 | tf_op jit(solution)/shard_map/ppermute | solution.py:37
  5.4 7.1 %collective-permute-start.1 = (bf16[256,128]{1,0:T(8,128)(2,1)S(1)}, bf16[256,128]{1,0:T(8,128)(2,1)S(1)}, u32[]{:S(2)}, u32[]{:S(2)}) collective-permute-start(bf16[256,128]{1,0:T(8,128)(2,1)S(1)} %constant_dynamic-update-slice_fusion), channel_id=1, source_target_pairs={{0,0},{1,129},{2,2},{3,131},{4,4},{5,133},{6,6},{7,135},{8,8},{9,1... | collective-permute-start | bytes 196616 | tf_op jit(solution)/shard_map/ppermute | solution.py:37
  12.7 4.7 %collective-permute-start.4 = (bf16[256,128]{1,0:T(8,128)(2,1)S(1)}, bf16[256,128]{1,0:T(8,128)(2,1)S(1)}, u32[]{:S(2)}, u32[]{:S(2)}) collective-permute-start(bf16[256,128]{1,0:T(8,128)(2,1)S(1)} %constant_dynamic-update-slice_fusion), channel_id=1, source_target_pairs={{0,66},{1,131},{2,128},{3,193},{4,70},{5,135},{6,132},{7,197},{8,7... | collective-permute-start | bytes 196616 | tf_op jit(solution)/shard_map/ppermute | solution.py:37
  17.4 3.4 %shard_map.94 = (bf16[4,128,4096]{2,1,0:T(8,128)(2,1)S(1)}, bf16[4,128,4096]{2,1,0:T(8,128)(2,1)S(1)}, f32[128,128]{1,0:T(8,128)S(1)}) custom-call(s32[320]{0:T(512)S(1)} %pad_add_fusion.table, bf16[128,32768]{1,0:T(8,128)(2,1)} %adjacency.3), custom_call_target="tpu_custom_call" | custom-call | flops 1024 | bytes 1024 | tf_op jit(solution)/shard_map/pallas_call | solution.py:132
  20.9 1.4 %collective-permute-start.5 = (bf16[1024,128]{1,0:T(8,128)(2,1)S(1)}, bf16[1024,128]{1,0:T(8,128)(2,1)S(1)}, u32[]{:S(2)}, u32[]{:S(2)}) collective-permute-start(bf16[1024,128]{1,0:T(8,128)(2,1)S(1)} %pad_maximum_fusion.1), channel_id=1, source_target_pairs={{0,16},{1,5},{2,18},{3,7},{4,20},{5,9},{6,22},{7,11},{8,24},{9,13}... | collective-permute-start | bytes 786440 | tf_op jit(solution)/shard_map/ppermute | solution.py:37
  22.3 1.5 %collective-permute-start.6 = (bf16[1024,128]{1,0:T(8,128)(2,1)S(1)}, bf16[1024,128]{1,0:T(8,128)(2,1)S(1)}, u32[]{:S(2)}, u32[]{:S(2)}) collective-permute-start(bf16[1024,128]{1,0:T(8,128)(2,1)S(1)} %pad_maximum_fusion.1), channel_id=1, source_target_pairs={{0,48},{1,13},{2,50},{3,15},{4,52},{5,1},{6,54},{7,3},{8,56},{9,5}... | collective-permute-start | bytes 786440 | tf_op jit(solution)/shard_map/ppermute | solution.py:37
  23.8 1.6 %collective-permute-start.7 = (bf16[1024,128]{1,0:T(8,128)(2,1)S(1)}, bf16[1024,128]{1,0:T(8,128)(2,1)S(1)}, u32[]{:S(2)}, u32[]{:S(2)}) collective-permute-start(bf16[1024,128]{1,0:T(8,128)(2,1)S(1)} %pad_maximum_fusion.1), channel_id=1, source_target_pairs={{0,32},{1,9},{2,34},{3,11},{4,36},{5,13},{6,38},{7,15},{8,40},{9,1... | collective-permute-start | bytes 786440 | tf_op jit(solution)/shard_map/ppermute | solution.py:37
  25.3 5.3 %shard_map.95 = (bf16[4,128,4096]{2,1,0:T(8,128)(2,1)S(1)}, bf16[4,128,4096]{2,1,0:T(8,128)(2,1)S(1)}, f32[128,128]{1,0:T(8,128)S(1)}) custom-call(s32[320]{0:T(512)S(1)} %pad_add_fusion.table, bf16[128,32768]{1,0:T(8,128)(2,1)} %adjacency.3, ...), custom_call_target="tpu_custom_call", output_to_operand_aliasing={{0}: (2, {}), {1}: (3, {}), {2}: (4, {})} | custom-call | flops 1024 | bytes 1024 | tf_op jit(solution)/shard_map/pallas_call | solution.py:132
  31.7 1.3 %collective-permute-start.8 = (bf16[2048,128]{1,0:T(8,128)(2,1)S(1)}, bf16[2048,128]{1,0:T(8,128)(2,1)S(1)}, u32[]{:S(2)}, u32[]{:S(2)}) collective-permute-start(bf16[2048,128]{1,0:T(8,128)(2,1)S(1)} %get-tuple-element.62), channel_id=1, source_target_pairs={{0,4},{1,17},{2,6},{3,19},{4,8},{5,21},{6,10},{7,23},{8,12},{9,25}... | collective-permute-start | bytes 1572872 | tf_op jit(solution)/shard_map/ppermute | solution.py:37
  33.0 1.5 %collective-permute-start.9 = (bf16[2048,128]{1,0:T(8,128)(2,1)S(1)}, bf16[2048,128]{1,0:T(8,128)(2,1)S(1)}, u32[]{:S(2)}, u32[]{:S(2)}) collective-permute-start(bf16[2048,128]{1,0:T(8,128)(2,1)S(1)} %get-tuple-element.61), channel_id=1, source_target_pairs={{0,12},{1,49},{2,14},{3,51},{4,0},{5,53},{6,2},{7,55},{8,4},{9,57}... | collective-permute-start | bytes 1572872 | tf_op jit(solution)/shard_map/ppermute | solution.py:37
  34.5 2.7 %collective-permute-start.14 = (bf16[2048,128]{1,0:T(8,128)(2,1)S(1)}, bf16[2048,128]{1,0:T(8,128)(2,1)S(1)}, u32[]{:S(2)}, u32[]{:S(2)}) collective-permute-start(bf16[2048,128]{1,0:T(8,128)(2,1)S(1)} %get-tuple-element.62), channel_id=1, source_target_pairs={{0,12},{1,49},{2,14},{3,51},{4,0},{5,53},{6,2},{7,55},{8,4},{9,57}... | collective-permute-start | bytes 1572872 | tf_op jit(solution)/shard_map/ppermute | solution.py:37
  37.1 4.2 %collective-permute-done.8.refs_1_ = bf16[2048,128]{1,0:T(8,128)(2,1)S(1)} collective-permute-done((bf16[2048,128]{1,0:T(8,128)(2,1)S(1)}, bf16[2048,128]{1,0:T(8,128)(2,1)S(1)}, u32[]{:S(2)}, u32[]{:S(2)}) %collective-permute-start.8) | collective-permute-done | bytes 524320 | tf_op jit(solution)/shard_map/ppermute | solution.py:37
  41.3 1.2 %collective-permute-start.11 = (bf16[2048,128]{1,0:T(8,128)(2,1)S(1)}, bf16[2048,128]{1,0:T(8,128)(2,1)S(1)}, u32[]{:S(2)}, u32[]{:S(2)}) collective-permute-start(bf16[2048,128]{1,0:T(8,128)(2,1)S(1)} %collective-permute-done.8.refs_1_), channel_id=1, source_target_pairs={{0,4},{1,17},{2,6},{3,19},{4,8},{5,21},{6,10},{7,23},{8,12},{9,25}... | collective-permute-start | bytes 1572872 | tf_op jit(solution)/shard_map/ppermute | solution.py:37
  42.5 1.5 %collective-permute-start.12 = (bf16[2048,128]{1,0:T(8,128)(2,1)S(1)}, bf16[2048,128]{1,0:T(8,128)(2,1)S(1)}, u32[]{:S(2)}, u32[]{:S(2)}) collective-permute-start(bf16[2048,128]{1,0:T(8,128)(2,1)S(1)} %collective-permute-done.9.refs_2_), channel_id=1, source_target_pairs={{0,12},{1,49},{2,14},{3,51},{4,0},{5,53},{6,2},{7,55},{8,4},{9,57}... | collective-permute-start | bytes 1572872 | tf_op jit(solution)/shard_map/ppermute | solution.py:37
  44.0 1.4 %shard_map.96 = (f32[128,128]{1,0:T(8,128)S(1)}, f32[128,128]{1,0:T(8,128)S(1)}, bf16[16,128]{1,0:T(8,128)(2,1)S(1)}) custom-call(bf16[4,128,4096]{2,1,0:T(8,128)(2,1)S(1)} %get-tuple-element.42.own, bf16[4,128,4096]{2,1,0:T(8,128)(2,1)S(1)} %collective-permute-done.10.got, bf16[4096,128]{1,0:T(8,128)(2,1)S(1)} %pad_maximum_fusion.refs_0_, ...), custom_call_target="tpu_custom_call" | custom-call | flops 1024 | bytes 1024 | tf_op jit(solution)/shard_map/pallas_call | solution.py:172
  45.4 1.5 %collective-permute-done.13.refs_0_ = bf16[2048,128]{1,0:T(8,128)(2,1)S(1)} collective-permute-done((bf16[2048,128]{1,0:T(8,128)(2,1)S(1)}, bf16[2048,128]{1,0:T(8,128)(2,1)S(1)}, u32[]{:S(2)}, u32[]{:S(2)}) %collective-permute-start.13) | collective-permute-done | bytes 524320 | tf_op jit(solution)/shard_map/ppermute | solution.py:37
  47.7 4.8 %collective-permute-done.11.refs_0_ = bf16[2048,128]{1,0:T(8,128)(2,1)S(1)} collective-permute-done((bf16[2048,128]{1,0:T(8,128)(2,1)S(1)}, bf16[2048,128]{1,0:T(8,128)(2,1)S(1)}, u32[]{:S(2)}, u32[]{:S(2)}) %collective-permute-start.11) | collective-permute-done | bytes 524320 | tf_op jit(solution)/shard_map/ppermute | solution.py:37
  53.4 1.4 %collective-permute-start.15 = (f32[136,128]{1,0:T(8,128)S(1)}, f32[136,128]{1,0:T(8,128)S(1)}, u32[]{:S(2)}, u32[]{:S(2)}) collective-permute-start(f32[136,128]{1,0:T(8,128)S(1)} %get-tuple-element.55), channel_id=1, source_target_pairs={{0,1},{1,0},{2,3},{3,2},{4,5},{5,4},{6,7},{7,6},{8,9},{9,8},{10,11... | collective-permute-start | bytes 208904 | tf_op jit(solution)/shard_map/ppermute | solution.py:37
  58.1 2.4 %collective-permute-start.17 = (f32[136,128]{1,0:T(8,128)S(1)}, f32[136,128]{1,0:T(8,128)S(1)}, u32[]{:S(2)}, u32[]{:S(2)}) collective-permute-start(f32[136,128]{1,0:T(8,128)S(1)} %add.57), channel_id=1, source_target_pairs={{0,32},{1,9},{2,34},{3,11},{4,36},{5,13},{6,38},{7,15},{8,40},{9,1... | collective-permute-start | bytes 208904 | tf_op jit(solution)/shard_map/ppermute | solution.py:37
  60.6 1.2 %collective-permute-start.18 = (f32[136,128]{1,0:T(8,128)S(1)}, f32[136,128]{1,0:T(8,128)S(1)}, u32[]{:S(2)}, u32[]{:S(2)}) collective-permute-start(f32[136,128]{1,0:T(8,128)S(1)} %add.57), channel_id=1, source_target_pairs={{0,16},{1,5},{2,18},{3,7},{4,20},{5,9},{6,22},{7,11},{8,24},{9,13}... | collective-permute-start | bytes 208904 | tf_op jit(solution)/shard_map/ppermute | solution.py:37
  61.7 1.5 %collective-permute-start.19 = (f32[136,128]{1,0:T(8,128)S(1)}, f32[136,128]{1,0:T(8,128)S(1)}, u32[]{:S(2)}, u32[]{:S(2)}) collective-permute-start(f32[136,128]{1,0:T(8,128)S(1)} %add.57), channel_id=1, source_target_pairs={{0,48},{1,13},{2,50},{3,15},{4,52},{5,1},{6,54},{7,3},{8,56},{9,5}... | collective-permute-start | bytes 208904 | tf_op jit(solution)/shard_map/ppermute | solution.py:37
  63.3 1.7 %collective-permute-done.18 = f32[136,128]{1,0:T(8,128)S(1)} collective-permute-done((f32[136,128]{1,0:T(8,128)S(1)}, f32[136,128]{1,0:T(8,128)S(1)}, u32[]{:S(2)}, u32[]{:S(2)}) %collective-permute-start.18) | collective-permute-done | bytes 69664 | tf_op jit(solution)/shard_map/ppermute | solution.py:37
  65.0 3.0 %collective-permute-start.20 = (f32[136,128]{1,0:T(8,128)S(1)}, f32[136,128]{1,0:T(8,128)S(1)}, u32[]{:S(2)}, u32[]{:S(2)}) collective-permute-start(f32[136,128]{1,0:T(8,128)S(1)} %add_add_fusion.2), channel_id=1, source_target_pairs={{0,8},{1,33},{2,10},{3,35},{4,12},{5,37},{6,14},{7,39},{8,0},{9,41... | collective-permute-start | bytes 208904 | tf_op jit(solution)/shard_map/ppermute | solution.py:37
  68.1 2.6 %collective-permute-start.22 = (f32[136,128]{1,0:T(8,128)S(1)}, f32[136,128]{1,0:T(8,128)S(1)}, u32[]{:S(2)}, u32[]{:S(2)}) collective-permute-start(f32[136,128]{1,0:T(8,128)S(1)} %add_add_fusion.2), channel_id=1, source_target_pairs={{0,12},{1,49},{2,14},{3,51},{4,0},{5,53},{6,2},{7,55},{8,4},{9,57}... | collective-permute-start | bytes 208904 | tf_op jit(solution)/shard_map/ppermute | solution.py:37
  70.7 2.0 %collective-permute-done.21 = f32[136,128]{1,0:T(8,128)S(1)} collective-permute-done((f32[136,128]{1,0:T(8,128)S(1)}, f32[136,128]{1,0:T(8,128)S(1)}, u32[]{:S(2)}, u32[]{:S(2)}) %collective-permute-start.21) | collective-permute-done | bytes 69664 | tf_op jit(solution)/shard_map/ppermute | solution.py:37
  72.7 1.6 %collective-permute-start.23 = (f32[136,128]{1,0:T(8,128)S(1)}, f32[136,128]{1,0:T(8,128)S(1)}, u32[]{:S(2)}, u32[]{:S(2)}) collective-permute-start(f32[136,128]{1,0:T(8,128)S(1)} %add_add_fusion.1), channel_id=1, source_target_pairs={{0,2},{1,3},{2,0},{3,1},{4,6},{5,7},{6,4},{7,5},{8,10},{9,11},{10,... | collective-permute-start | bytes 208904 | tf_op jit(solution)/shard_map/ppermute | solution.py:37
  74.3 1.7 %collective-permute-done.23 = f32[136,128]{1,0:T(8,128)S(1)} collective-permute-done((f32[136,128]{1,0:T(8,128)S(1)}, f32[136,128]{1,0:T(8,128)S(1)}, u32[]{:S(2)}, u32[]{:S(2)}) %collective-permute-start.23) | collective-permute-done | bytes 69664 | tf_op jit(solution)/shard_map/ppermute | solution.py:37
  76.0 3.8 %collective-permute-start.24 = (f32[136,128]{1,0:T(8,128)S(1)}, f32[136,128]{1,0:T(8,128)S(1)}, u32[]{:S(2)}, u32[]{:S(2)}) collective-permute-start(f32[136,128]{1,0:T(8,128)S(1)} %add.64), channel_id=1, source_target_pairs={{0,128},{1,129},{2,130},{3,131},{4,132},{5,133},{6,134},{7,135},{8... | collective-permute-start | bytes 208904 | tf_op jit(solution)/shard_map/ppermute | solution.py:37
  80.5 2.8 %collective-permute-start.26 = (f32[136,128]{1,0:T(8,128)S(1)}, f32[136,128]{1,0:T(8,128)S(1)}, u32[]{:S(2)}, u32[]{:S(2)}) collective-permute-start(f32[136,128]{1,0:T(8,128)S(1)} %add.64), channel_id=1, source_target_pairs={{0,192},{1,193},{2,194},{3,195},{4,196},{5,197},{6,198},{7,199},{8... | collective-permute-start | bytes 208904 | tf_op jit(solution)/shard_map/ppermute | solution.py:37
  83.9 1.2 %collective-permute-done.25 = f32[136,128]{1,0:T(8,128)S(1)} collective-permute-done((f32[136,128]{1,0:T(8,128)S(1)}, f32[136,128]{1,0:T(8,128)S(1)}, u32[]{:S(2)}, u32[]{:S(2)}) %collective-permute-start.25) | collective-permute-done | bytes 69664 | tf_op jit(solution)/shard_map/ppermute | solution.py:37
  85.1 1.4 %collective-permute-done.26 = f32[136,128]{1,0:T(8,128)S(1)} collective-permute-done((f32[136,128]{1,0:T(8,128)S(1)}, f32[136,128]{1,0:T(8,128)S(1)}, u32[]{:S(2)}, u32[]{:S(2)}) %collective-permute-start.26) | collective-permute-done | bytes 69664 | tf_op jit(solution)/shard_map/ppermute | solution.py:37
  86.5 4.2 %collective-permute-start.27 = (f32[136,128]{1,0:T(8,128)S(1)}, f32[136,128]{1,0:T(8,128)S(1)}, u32[]{:S(2)}, u32[]{:S(2)}) collective-permute-start(f32[136,128]{1,0:T(8,128)S(1)} %add_add_fusion), channel_id=1, source_target_pairs={{0,1},{1,0},{2,3},{3,2},{4,5},{5,4},{6,7},{7,6},{8,9},{9,8},{10,11... | collective-permute-start | bytes 208904 | tf_op jit(solution)/shard_map/ppermute | solution.py:37
  (56 shorter events, 11.3 us)
Async XLA Ops:
  0.6 4.8 %collective-permute-start = (bf16[128,128]{1,0:T(8,128)(2,1)}, bf16[128,128]{1,0:T(8,128)(2,1)S(1)}, u32[]{:S(2)}, u32[]{:S(2)}) collective-permute-start(bf16[128,128]{1,0:T(8,128)(2,1)} %own.1), channel_id=1, source_target_pairs={{0,1},{1,0},{2,3},{3,2},{4,5},{5,4},{6,7},{7,6},{8,9},{9,8},{10,11... | collective-permute-start | bytes 98312 | tf_op jit(solution)/shard_map/ppermute | solution.py:37
  5.4 15.4 %collective-permute-start.1 = (bf16[256,128]{1,0:T(8,128)(2,1)S(1)}, bf16[256,128]{1,0:T(8,128)(2,1)S(1)}, u32[]{:S(2)}, u32[]{:S(2)}) collective-permute-start(bf16[256,128]{1,0:T(8,128)(2,1)S(1)} %constant_dynamic-update-slice_fusion), channel_id=1, source_target_pairs={{0,0},{1,129},{2,2},{3,131},{4,4},{5,133},{6,6},{7,135},{8,8},{9,1... | collective-permute-start | bytes 196616 | tf_op jit(solution)/shard_map/ppermute | solution.py:37
  12.5 8.3 %collective-permute-start.2 = (bf16[256,128]{1,0:T(8,128)(2,1)S(1)}, bf16[256,128]{1,0:T(8,128)(2,1)S(1)}, u32[]{:S(2)}, u32[]{:S(2)}) collective-permute-start(bf16[256,128]{1,0:T(8,128)(2,1)S(1)} %constant_dynamic-update-slice_fusion), channel_id=1, source_target_pairs={{0,2},{1,195},{2,64},{3,1},{4,6},{5,199},{6,68},{7,5},{8,10},{9,20... | collective-permute-start | bytes 196616 | tf_op jit(solution)/shard_map/ppermute | solution.py:37
  12.6 8.2 %collective-permute-start.3 = (bf16[256,128]{1,0:T(8,128)(2,1)S(1)}, bf16[256,128]{1,0:T(8,128)(2,1)S(1)}, u32[]{:S(2)}, u32[]{:S(2)}) collective-permute-start(bf16[256,128]{1,0:T(8,128)(2,1)S(1)} %constant_dynamic-update-slice_fusion), channel_id=1, source_target_pairs={{0,64},{1,193},{2,66},{3,195},{4,68},{5,197},{6,70},{7,199},{8,72}... | collective-permute-start | bytes 196616 | tf_op jit(solution)/shard_map/ppermute | solution.py:37
  12.7 8.1 %collective-permute-start.4 = (bf16[256,128]{1,0:T(8,128)(2,1)S(1)}, bf16[256,128]{1,0:T(8,128)(2,1)S(1)}, u32[]{:S(2)}, u32[]{:S(2)}) collective-permute-start(bf16[256,128]{1,0:T(8,128)(2,1)S(1)} %constant_dynamic-update-slice_fusion), channel_id=1, source_target_pairs={{0,66},{1,131},{2,128},{3,193},{4,70},{5,135},{6,132},{7,197},{8,7... | collective-permute-start | bytes 196616 | tf_op jit(solution)/shard_map/ppermute | solution.py:37
  20.9 9.7 %collective-permute-start.5 = (bf16[1024,128]{1,0:T(8,128)(2,1)S(1)}, bf16[1024,128]{1,0:T(8,128)(2,1)S(1)}, u32[]{:S(2)}, u32[]{:S(2)}) collective-permute-start(bf16[1024,128]{1,0:T(8,128)(2,1)S(1)} %pad_maximum_fusion.1), channel_id=1, source_target_pairs={{0,16},{1,5},{2,18},{3,7},{4,20},{5,9},{6,22},{7,11},{8,24},{9,13}... | collective-permute-start | bytes 786440 | tf_op jit(solution)/shard_map/ppermute | solution.py:37
  22.3 8.4 %collective-permute-start.6 = (bf16[1024,128]{1,0:T(8,128)(2,1)S(1)}, bf16[1024,128]{1,0:T(8,128)(2,1)S(1)}, u32[]{:S(2)}, u32[]{:S(2)}) collective-permute-start(bf16[1024,128]{1,0:T(8,128)(2,1)S(1)} %pad_maximum_fusion.1), channel_id=1, source_target_pairs={{0,48},{1,13},{2,50},{3,15},{4,52},{5,1},{6,54},{7,3},{8,56},{9,5}... | collective-permute-start | bytes 786440 | tf_op jit(solution)/shard_map/ppermute | solution.py:37
  23.8 7.7 %collective-permute-start.7 = (bf16[1024,128]{1,0:T(8,128)(2,1)S(1)}, bf16[1024,128]{1,0:T(8,128)(2,1)S(1)}, u32[]{:S(2)}, u32[]{:S(2)}) collective-permute-start(bf16[1024,128]{1,0:T(8,128)(2,1)S(1)} %pad_maximum_fusion.1), channel_id=1, source_target_pairs={{0,32},{1,9},{2,34},{3,11},{4,36},{5,13},{6,38},{7,15},{8,40},{9,1... | collective-permute-start | bytes 786440 | tf_op jit(solution)/shard_map/ppermute | solution.py:37
  31.5 9.8 %collective-permute-start.10 = (bf16[4,128,4096]{2,1,0:T(8,128)(2,1)S(1)}, bf16[4,128,4096]{2,1,0:T(8,128)(2,1)S(1)}, u32[]{:S(2)}, u32[]{:S(2)}) collective-permute-start(bf16[4,128,4096]{2,1,0:T(8,128)(2,1)S(1)} %get-tuple-element.44), channel_id=1, source_target_pairs={{0,1},{1,0},{2,3},{3,2},{4,5},{5,4},{6,7},{7,6},{8,9},{9,8},{10,11... | collective-permute-start | bytes 12582920 | tf_op jit(solution)/shard_map/ppermute | solution.py:37
  31.7 9.6 %collective-permute-start.8 = (bf16[2048,128]{1,0:T(8,128)(2,1)S(1)}, bf16[2048,128]{1,0:T(8,128)(2,1)S(1)}, u32[]{:S(2)}, u32[]{:S(2)}) collective-permute-start(bf16[2048,128]{1,0:T(8,128)(2,1)S(1)} %get-tuple-element.62), channel_id=1, source_target_pairs={{0,4},{1,17},{2,6},{3,19},{4,8},{5,21},{6,10},{7,23},{8,12},{9,25}... | collective-permute-start | bytes 1572872 | tf_op jit(solution)/shard_map/ppermute | solution.py:37
  33.0 8.3 %collective-permute-start.9 = (bf16[2048,128]{1,0:T(8,128)(2,1)S(1)}, bf16[2048,128]{1,0:T(8,128)(2,1)S(1)}, u32[]{:S(2)}, u32[]{:S(2)}) collective-permute-start(bf16[2048,128]{1,0:T(8,128)(2,1)S(1)} %get-tuple-element.61), channel_id=1, source_target_pairs={{0,12},{1,49},{2,14},{3,51},{4,0},{5,53},{6,2},{7,55},{8,4},{9,57}... | collective-permute-start | bytes 1572872 | tf_op jit(solution)/shard_map/ppermute | solution.py:37
  34.4 12.5 %collective-permute-start.13 = (bf16[2048,128]{1,0:T(8,128)(2,1)S(1)}, bf16[2048,128]{1,0:T(8,128)(2,1)S(1)}, u32[]{:S(2)}, u32[]{:S(2)}) collective-permute-start(bf16[2048,128]{1,0:T(8,128)(2,1)S(1)} %get-tuple-element.61), channel_id=1, source_target_pairs={{0,4},{1,17},{2,6},{3,19},{4,8},{5,21},{6,10},{7,23},{8,12},{9,25}... | collective-permute-start | bytes 1572872 | tf_op jit(solution)/shard_map/ppermute | solution.py:37
  34.5 12.5 %collective-permute-start.14 = (bf16[2048,128]{1,0:T(8,128)(2,1)S(1)}, bf16[2048,128]{1,0:T(8,128)(2,1)S(1)}, u32[]{:S(2)}, u32[]{:S(2)}) collective-permute-start(bf16[2048,128]{1,0:T(8,128)(2,1)S(1)} %get-tuple-element.62), channel_id=1, source_target_pairs={{0,12},{1,49},{2,14},{3,51},{4,0},{5,53},{6,2},{7,55},{8,4},{9,57}... | collective-permute-start | bytes 1572872 | tf_op jit(solution)/shard_map/ppermute | solution.py:37
  41.3 11.2 %collective-permute-start.11 = (bf16[2048,128]{1,0:T(8,128)(2,1)S(1)}, bf16[2048,128]{1,0:T(8,128)(2,1)S(1)}, u32[]{:S(2)}, u32[]{:S(2)}) collective-permute-start(bf16[2048,128]{1,0:T(8,128)(2,1)S(1)} %collective-permute-done.8.refs_1_), channel_id=1, source_target_pairs={{0,4},{1,17},{2,6},{3,19},{4,8},{5,21},{6,10},{7,23},{8,12},{9,25}... | collective-permute-start | bytes 1572872 | tf_op jit(solution)/shard_map/ppermute | solution.py:37
  42.5 10.0 %collective-permute-start.12 = (bf16[2048,128]{1,0:T(8,128)(2,1)S(1)}, bf16[2048,128]{1,0:T(8,128)(2,1)S(1)}, u32[]{:S(2)}, u32[]{:S(2)}) collective-permute-start(bf16[2048,128]{1,0:T(8,128)(2,1)S(1)} %collective-permute-done.9.refs_2_), channel_id=1, source_target_pairs={{0,12},{1,49},{2,14},{3,51},{4,0},{5,53},{6,2},{7,55},{8,4},{9,57}... | collective-permute-start | bytes 1572872 | tf_op jit(solution)/shard_map/ppermute | solution.py:37
  52.5 3.2 %copy-start = (bf16[128,128]{1,0:T(8,128)(2,1)S(1)}, bf16[128,128]{1,0:T(8,128)(2,1)}, u32[]{:S(2)}) copy-start(bf16[128,128]{1,0:T(8,128)(2,1)} %own.1) | copy-start | bytes 98308
  52.5 3.2 %copy-start.1 = (bf16[128,256]{1,0:T(8,128)(2,1)S(1)}, bf16[128,256]{1,0:T(8,128)(2,1)}, u32[]{:S(2)}) copy-start(bf16[128,256]{1,0:T(8,128)(2,1)} %weight.1) | copy-start | bytes 196612
  52.6 3.2 %copy-start.2 = (bf16[128,256]{1,0:T(8,128)(2,1)S(1)}, bf16[128,256]{1,0:T(8,128)(2,1)}, u32[]{:S(2)}) copy-start(bf16[128,256]{1,0:T(8,128)(2,1)} %cotangent.1) | copy-start | bytes 196612
  52.6 3.1 %copy-start.3 = (f32[256]{0:T(256)S(1)}, f32[256]{0:T(256)}, u32[]{:S(2)}) copy-start(f32[256]{0:T(256)} %param.12) | copy-start | bytes 3076
  53.4 2.3 %collective-permute-start.15 = (f32[136,128]{1,0:T(8,128)S(1)}, f32[136,128]{1,0:T(8,128)S(1)}, u32[]{:S(2)}, u32[]{:S(2)}) collective-permute-start(f32[136,128]{1,0:T(8,128)S(1)} %get-tuple-element.55), channel_id=1, source_target_pairs={{0,1},{1,0},{2,3},{3,2},{4,5},{5,4},{6,7},{7,6},{8,9},{9,8},{10,11... | collective-permute-start | bytes 208904 | tf_op jit(solution)/shard_map/ppermute | solution.py:37
  56.8 1.3 %collective-permute-start.16 = (f32[136,128]{1,0:T(8,128)S(1)}, f32[136,128]{1,0:T(8,128)S(1)}, u32[]{:S(2)}, u32[]{:S(2)}) collective-permute-start(f32[136,128]{1,0:T(8,128)S(1)} %get-tuple-element.60), channel_id=1, source_target_pairs={{0,1},{1,0},{2,3},{3,2},{4,5},{5,4},{6,7},{7,6},{8,9},{9,8},{10,11... | collective-permute-start | bytes 208904 | tf_op jit(solution)/shard_map/ppermute | solution.py:37
  58.1 5.1 %collective-permute-start.17 = (f32[136,128]{1,0:T(8,128)S(1)}, f32[136,128]{1,0:T(8,128)S(1)}, u32[]{:S(2)}, u32[]{:S(2)}) collective-permute-start(f32[136,128]{1,0:T(8,128)S(1)} %add.57), channel_id=1, source_target_pairs={{0,32},{1,9},{2,34},{3,11},{4,36},{5,13},{6,38},{7,15},{8,40},{9,1... | collective-permute-start | bytes 208904 | tf_op jit(solution)/shard_map/ppermute | solution.py:37
  60.6 4.4 %collective-permute-start.18 = (f32[136,128]{1,0:T(8,128)S(1)}, f32[136,128]{1,0:T(8,128)S(1)}, u32[]{:S(2)}, u32[]{:S(2)}) collective-permute-start(f32[136,128]{1,0:T(8,128)S(1)} %add.57), channel_id=1, source_target_pairs={{0,16},{1,5},{2,18},{3,7},{4,20},{5,9},{6,22},{7,11},{8,24},{9,13}... | collective-permute-start | bytes 208904 | tf_op jit(solution)/shard_map/ppermute | solution.py:37
  61.7 3.2 %collective-permute-start.19 = (f32[136,128]{1,0:T(8,128)S(1)}, f32[136,128]{1,0:T(8,128)S(1)}, u32[]{:S(2)}, u32[]{:S(2)}) collective-permute-start(f32[136,128]{1,0:T(8,128)S(1)} %add.57), channel_id=1, source_target_pairs={{0,48},{1,13},{2,50},{3,15},{4,52},{5,1},{6,54},{7,3},{8,56},{9,5}... | collective-permute-start | bytes 208904 | tf_op jit(solution)/shard_map/ppermute | solution.py:37
  65.0 5.7 %collective-permute-start.20 = (f32[136,128]{1,0:T(8,128)S(1)}, f32[136,128]{1,0:T(8,128)S(1)}, u32[]{:S(2)}, u32[]{:S(2)}) collective-permute-start(f32[136,128]{1,0:T(8,128)S(1)} %add_add_fusion.2), channel_id=1, source_target_pairs={{0,8},{1,33},{2,10},{3,35},{4,12},{5,37},{6,14},{7,39},{8,0},{9,41... | collective-permute-start | bytes 208904 | tf_op jit(solution)/shard_map/ppermute | solution.py:37
  68.0 4.6 %collective-permute-start.21 = (f32[136,128]{1,0:T(8,128)S(1)}, f32[136,128]{1,0:T(8,128)S(1)}, u32[]{:S(2)}, u32[]{:S(2)}) collective-permute-start(f32[136,128]{1,0:T(8,128)S(1)} %add_add_fusion.2), channel_id=1, source_target_pairs={{0,4},{1,17},{2,6},{3,19},{4,8},{5,21},{6,10},{7,23},{8,12},{9,25}... | collective-permute-start | bytes 208904 | tf_op jit(solution)/shard_map/ppermute | solution.py:37
  68.1 4.5 %collective-permute-start.22 = (f32[136,128]{1,0:T(8,128)S(1)}, f32[136,128]{1,0:T(8,128)S(1)}, u32[]{:S(2)}, u32[]{:S(2)}) collective-permute-start(f32[136,128]{1,0:T(8,128)S(1)} %add_add_fusion.2), channel_id=1, source_target_pairs={{0,12},{1,49},{2,14},{3,51},{4,0},{5,53},{6,2},{7,55},{8,4},{9,57}... | collective-permute-start | bytes 208904 | tf_op jit(solution)/shard_map/ppermute | solution.py:37
  72.7 3.3 %collective-permute-start.23 = (f32[136,128]{1,0:T(8,128)S(1)}, f32[136,128]{1,0:T(8,128)S(1)}, u32[]{:S(2)}, u32[]{:S(2)}) collective-permute-start(f32[136,128]{1,0:T(8,128)S(1)} %add_add_fusion.1), channel_id=1, source_target_pairs={{0,2},{1,3},{2,0},{3,1},{4,6},{5,7},{6,4},{7,5},{8,10},{9,11},{10,... | collective-permute-start | bytes 208904 | tf_op jit(solution)/shard_map/ppermute | solution.py:37
  76.0 7.9 %collective-permute-start.24 = (f32[136,128]{1,0:T(8,128)S(1)}, f32[136,128]{1,0:T(8,128)S(1)}, u32[]{:S(2)}, u32[]{:S(2)}) collective-permute-start(f32[136,128]{1,0:T(8,128)S(1)} %add.64), channel_id=1, source_target_pairs={{0,128},{1,129},{2,130},{3,131},{4,132},{5,133},{6,134},{7,135},{8... | collective-permute-start | bytes 208904 | tf_op jit(solution)/shard_map/ppermute | solution.py:37
  79.8 5.3 %collective-permute-start.25 = (f32[136,128]{1,0:T(8,128)S(1)}, f32[136,128]{1,0:T(8,128)S(1)}, u32[]{:S(2)}, u32[]{:S(2)}) collective-permute-start(f32[136,128]{1,0:T(8,128)S(1)} %add.64), channel_id=1, source_target_pairs={{0,64},{1,65},{2,66},{3,67},{4,68},{5,69},{6,70},{7,71},{8,72},{9,... | collective-permute-start | bytes 208904 | tf_op jit(solution)/shard_map/ppermute | solution.py:37
  80.5 6.0 %collective-permute-start.26 = (f32[136,128]{1,0:T(8,128)S(1)}, f32[136,128]{1,0:T(8,128)S(1)}, u32[]{:S(2)}, u32[]{:S(2)}) collective-permute-start(f32[136,128]{1,0:T(8,128)S(1)} %add.64), channel_id=1, source_target_pairs={{0,192},{1,193},{2,194},{3,195},{4,196},{5,197},{6,198},{7,199},{8... | collective-permute-start | bytes 208904 | tf_op jit(solution)/shard_map/ppermute | solution.py:37
  86.5 5.1 %collective-permute-start.27 = (f32[136,128]{1,0:T(8,128)S(1)}, f32[136,128]{1,0:T(8,128)S(1)}, u32[]{:S(2)}, u32[]{:S(2)}) collective-permute-start(f32[136,128]{1,0:T(8,128)S(1)} %add_add_fusion), channel_id=1, source_target_pairs={{0,1},{1,0},{2,3},{3,2},{4,5},{5,4},{6,7},{7,6},{8,9},{9,8},{10,11... | collective-permute-start | bytes 208904 | tf_op jit(solution)/shard_map/ppermute | solution.py:37

commit v4 on v3

--- a/solution.py
+++ b/solution.py
@@ -83,7 +83,7 @@
 
     from_x, from_y = slot_of((x - (source >> 4)) & 3), slot_of((y - (source >> 2)) & 3)
     outer, inner = jnp.where(first, from_y, from_x), jnp.where(first, from_x, from_y)
-    hop = jnp.where(first, up, (8 - up) & 3)
+    hop = (3 - jnp.where(first, up, 8 - up)) & 3
     pair = (source & 1) ^ plane
     place = (plane ^ core) * 128 + outer * 32 + inner * 8 + hop * 2 + pair
     return jnp.concatenate([place, tile_mask[0] * (1 - skip_owner)])
@@ -250,14 +250,13 @@
     table = place_table(tile_mask, skip_owner)
     ordered = order_adjacency(0, FIRST, table, adjacency)
     chip = jnp.concatenate([features, swap_cores(features)])
-    far = along_z(chip, 4)
-    line = jnp.concatenate([far] + [along_z(chip, step) for step in (3, 2, 1)][::-1])
+    line = jnp.concatenate([along_z(chip, step) for step in (3, 2, 1, 4)])
     line, *ordered = lax.optimization_barrier((line, *ordered))
     own, give, degree = order_adjacency(FIRST, PIECES - FIRST, table, adjacency, *ordered)
-    plane = jnp.concatenate([line] + [along_xy(line, step, False) for step in SHIFTS[1:]])
-    plane, own, give, degree = lax.optimization_barrier((plane, own, give, degree))
+    slots = [line] + [along_xy(line, step, False) for step in SHIFTS[1:]]
+    front, back = jnp.concatenate(slots[:2]), jnp.concatenate(slots[2:])
+    front, back, own, give, degree = lax.optimization_barrier((front, back, own, give, degree))
     got = swap_cores(give)
-    front, back = plane[:HALF], plane[HALF:]
     front_after, back_before = along_xy(front, 1, True), along_xy(back, 3, True)
     back_after, front_before = along_xy(back, 1, True), along_xy(front, 3, True)
     front_after, back_before, got = lax.optimization_barrier((front_after, back_before, got))
@@ -265,7 +264,7 @@
     zero = jnp.zeros((128, 128), jnp.float32)
     sums = zero, zero, jnp.zeros((16, 128), jnp.bfloat16)
     sums = piece_step(
-        ((0, 0), (1, 0), (2, HALF)), False, own, got, (plane, front_after, back_before), sums
+        ((0, 0), (0, HALF), (1, 0), (2, HALF)), False, own, got, (front, back, front_after, back_before), sums
     )
     sums = piece_step(((1, HALF), (2, 0)), False, own, got, (back_after, front_before), sums)
     ours, theirs, largest = piece_step(((3, 0), (3, HALF)), True, own, got, halves, sums)

time: 93.4 us -> 93.1 us (level)
  no operation moved by 1% of the time
where the time goes in v4:
time: 93.1 us; the launch traced here: 92.7 us
  starting transfers between devices  54.1 us (58%)
  waiting for transfers between devices  22.1 us (24%)
  Pallas kernels  12.9 us (14%)
  other arithmetic  2.11 us (2%)
    ppermute x28, starting transfers between devices, permute(): lax.ppermute(array, NAMES, [(index_of(*at), index_of(*move(*at))) for at...  54.1 us
    ppermute x28, waiting for transfers between devices, permute(): lax.ppermute(array, NAMES, [(index_of(*at), index_of(*move(*at))) for at...  22.1 us
    pallas_call x2, Pallas kernels, order_adjacency(): pl.pallas_call(functools.partial(order_kernel, first), out_shape=[jax.Sha...  8.78 us
    pallas_call x3, Pallas kernels, piece_step(): pl.pallas_call(functools.partial(piece_kernel, spots, last), out_shape=[j...  2.97 us
  transfers between devices with their start and end apart: 28, of which 13 were waited for; matrix products, arithmetic and copies ran while one was open for 2% of the time, Pallas kernels for 12%

profile of v4, /device:TPU:1, one launch (start us, length us, event | category | flops | bytes accessed | tf_op | source)
XLA Modules:
  0.0 92.7 jit_solution(11772183175897413363)
XLA Ops:
  0.6 3.3 %collective-permute-start = (bf16[128,128]{1,0:T(8,128)(2,1)}, bf16[128,128]{1,0:T(8,128)(2,1)S(1)}, u32[]{:S(2)}, u32[]{:S(2)}) collective-permute-start(bf16[128,128]{1,0:T(8,128)(2,1)} %own.1), channel_id=1, source_target_pairs={{0,1},{1,0},{2,3},{3,2},{4,5},{5,4},{6,7},{7,6},{8,9},{9,8},{10,11... | collective-permute-start | bytes 98312 | tf_op jit(solution)/shard_map/ppermute | solution.py:37
  5.4 4.8 %collective-permute-start.1 = (bf16[256,128]{1,0:T(8,128)(2,1)S(1)}, bf16[256,128]{1,0:T(8,128)(2,1)S(1)}, u32[]{:S(2)}, u32[]{:S(2)}) collective-permute-start(bf16[256,128]{1,0:T(8,128)(2,1)S(1)} %constant_dynamic-update-slice_fusion), channel_id=1, source_target_pairs={{0,66},{1,131},{2,128},{3,193},{4,70},{5,135},{6,132},{7,197},{8,7... | collective-permute-start | bytes 196616 | tf_op jit(solution)/shard_map/ppermute | solution.py:37
  11.0 6.4 %collective-permute-start.4 = (bf16[256,128]{1,0:T(8,128)(2,1)S(1)}, bf16[256,128]{1,0:T(8,128)(2,1)S(1)}, u32[]{:S(2)}, u32[]{:S(2)}) collective-permute-start(bf16[256,128]{1,0:T(8,128)(2,1)S(1)} %constant_dynamic-update-slice_fusion), channel_id=1, source_target_pairs={{0,0},{1,129},{2,2},{3,131},{4,4},{5,133},{6,6},{7,135},{8,8},{9,1... | collective-permute-start | bytes 196616 | tf_op jit(solution)/shard_map/ppermute | solution.py:37
  17.4 3.5 %shard_map.94 = (bf16[4,128,4096]{2,1,0:T(8,128)(2,1)S(1)}, bf16[4,128,4096]{2,1,0:T(8,128)(2,1)S(1)}, f32[128,128]{1,0:T(8,128)S(1)}) custom-call(s32[320]{0:T(512)S(1)} %pad_add_fusion.table, bf16[128,32768]{1,0:T(8,128)(2,1)} %adjacency.3), custom_call_target="tpu_custom_call" | custom-call | flops 1024 | bytes 1024 | tf_op jit(solution)/shard_map/pallas_call | solution.py:132
  20.9 1.4 %collective-permute-start.5 = (bf16[1024,128]{1,0:T(8,128)(2,1)S(1)}, bf16[1024,128]{1,0:T(8,128)(2,1)S(1)}, u32[]{:S(2)}, u32[]{:S(2)}) collective-permute-start(bf16[1024,128]{1,0:T(8,128)(2,1)S(1)} %pad_maximum_fusion.2), channel_id=1, source_target_pairs={{0,16},{1,5},{2,18},{3,7},{4,20},{5,9},{6,22},{7,11},{8,24},{9,13}... | collective-permute-start | bytes 786440 | tf_op jit(solution)/shard_map/ppermute | solution.py:37
  22.3 1.5 %collective-permute-start.6 = (bf16[1024,128]{1,0:T(8,128)(2,1)S(1)}, bf16[1024,128]{1,0:T(8,128)(2,1)S(1)}, u32[]{:S(2)}, u32[]{:S(2)}) collective-permute-start(bf16[1024,128]{1,0:T(8,128)(2,1)S(1)} %pad_maximum_fusion.2), channel_id=1, source_target_pairs={{0,48},{1,13},{2,50},{3,15},{4,52},{5,1},{6,54},{7,3},{8,56},{9,5}... | collective-permute-start | bytes 786440 | tf_op jit(solution)/shard_map/ppermute | solution.py:37
  23.8 1.5 %collective-permute-start.7 = (bf16[1024,128]{1,0:T(8,128)(2,1)S(1)}, bf16[1024,128]{1,0:T(8,128)(2,1)S(1)}, u32[]{:S(2)}, u32[]{:S(2)}) collective-permute-start(bf16[1024,128]{1,0:T(8,128)(2,1)S(1)} %pad_maximum_fusion.2), channel_id=1, source_target_pairs={{0,32},{1,9},{2,34},{3,11},{4,36},{5,13},{6,38},{7,15},{8,40},{9,1... | collective-permute-start | bytes 786440 | tf_op jit(solution)/shard_map/ppermute | solution.py:37
  25.4 5.3 %shard_map.95 = (bf16[4,128,4096]{2,1,0:T(8,128)(2,1)S(1)}, bf16[4,128,4096]{2,1,0:T(8,128)(2,1)S(1)}, f32[128,128]{1,0:T(8,128)S(1)}) custom-call(s32[320]{0:T(512)S(1)} %pad_add_fusion.table, bf16[128,32768]{1,0:T(8,128)(2,1)} %adjacency.3, ...), custom_call_target="tpu_custom_call", output_to_operand_aliasing={{0}: (2, {}), {1}: (3, {}), {2}: (4, {})} | custom-call | flops 1024 | bytes 1024 | tf_op jit(solution)/shard_map/pallas_call | solution.py:132
  31.6 1.3 %collective-permute-start.8 = (bf16[2048,128]{1,0:T(8,128)(2,1)S(1)}, bf16[2048,128]{1,0:T(8,128)(2,1)S(1)}, u32[]{:S(2)}, u32[]{:S(2)}) collective-permute-start(bf16[2048,128]{1,0:T(8,128)(2,1)S(1)} %pad_maximum_fusion.refs_0_), channel_id=1, source_target_pairs={{0,4},{1,17},{2,6},{3,19},{4,8},{5,21},{6,10},{7,23},{8,12},{9,25}... | collective-permute-start | bytes 1572872 | tf_op jit(solution)/shard_map/ppermute | solution.py:37
  32.9 1.5 %collective-permute-start.9 = (bf16[2048,128]{1,0:T(8,128)(2,1)S(1)}, bf16[2048,128]{1,0:T(8,128)(2,1)S(1)}, u32[]{:S(2)}, u32[]{:S(2)}) collective-permute-start(bf16[2048,128]{1,0:T(8,128)(2,1)S(1)} %pad_maximum_fusion.1.refs_1_), channel_id=1, source_target_pairs={{0,12},{1,49},{2,14},{3,51},{4,0},{5,53},{6,2},{7,55},{8,4},{9,57}... | collective-permute-start | bytes 1572872 | tf_op jit(solution)/shard_map/ppermute | solution.py:37
  34.4 2.7 %collective-permute-start.14 = (bf16[2048,128]{1,0:T(8,128)(2,1)S(1)}, bf16[2048,128]{1,0:T(8,128)(2,1)S(1)}, u32[]{:S(2)}, u32[]{:S(2)}) collective-permute-start(bf16[2048,128]{1,0:T(8,128)(2,1)S(1)} %pad_maximum_fusion.refs_0_), channel_id=1, source_target_pairs={{0,12},{1,49},{2,14},{3,51},{4,0},{5,53},{6,2},{7,55},{8,4},{9,57}... | collective-permute-start | bytes 1572872 | tf_op jit(solution)/shard_map/ppermute | solution.py:37
  37.0 4.2 %collective-permute-done.8.refs_2_ = bf16[2048,128]{1,0:T(8,128)(2,1)S(1)} collective-permute-done((bf16[2048,128]{1,0:T(8,128)(2,1)S(1)}, bf16[2048,128]{1,0:T(8,128)(2,1)S(1)}, u32[]{:S(2)}, u32[]{:S(2)}) %collective-permute-start.8) | collective-permute-done | bytes 524320 | tf_op jit(solution)/shard_map/ppermute | solution.py:37
  41.2 1.2 %collective-permute-start.11 = (bf16[2048,128]{1,0:T(8,128)(2,1)S(1)}, bf16[2048,128]{1,0:T(8,128)(2,1)S(1)}, u32[]{:S(2)}, u32[]{:S(2)}) collective-permute-start(bf16[2048,128]{1,0:T(8,128)(2,1)S(1)} %collective-permute-done.8.refs_2_), channel_id=1, source_target_pairs={{0,4},{1,17},{2,6},{3,19},{4,8},{5,21},{6,10},{7,23},{8,12},{9,25}... | collective-permute-start | bytes 1572872 | tf_op jit(solution)/shard_map/ppermute | solution.py:37
  42.4 1.5 %collective-permute-start.12 = (bf16[2048,128]{1,0:T(8,128)(2,1)S(1)}, bf16[2048,128]{1,0:T(8,128)(2,1)S(1)}, u32[]{:S(2)}, u32[]{:S(2)}) collective-permute-start(bf16[2048,128]{1,0:T(8,128)(2,1)S(1)} %collective-permute-done.9.refs_3_), channel_id=1, source_target_pairs={{0,12},{1,49},{2,14},{3,51},{4,0},{5,53},{6,2},{7,55},{8,4},{9,57}... | collective-permute-start | bytes 1572872 | tf_op jit(solution)/shard_map/ppermute | solution.py:37
  43.9 1.4 %shard_map.96 = (f32[128,128]{1,0:T(8,128)S(1)}, f32[128,128]{1,0:T(8,128)S(1)}, bf16[16,128]{1,0:T(8,128)(2,1)S(1)}) custom-call(bf16[4,128,4096]{2,1,0:T(8,128)(2,1)S(1)} %get-tuple-element.43.own, bf16[4,128,4096]{2,1,0:T(8,128)(2,1)S(1)} %collective-permute-done.10.got, bf16[2048,128]{1,0:T(8,128)(2,1)S(1)} %pad_maximum_fusion.refs_0_, ...), custom_call_target="tpu_custom_call" | custom-call | flops 1024 | bytes 1024 | tf_op jit(solution)/shard_map/pallas_call | solution.py:172
  45.4 1.5 %collective-permute-done.13.refs_0_ = bf16[2048,128]{1,0:T(8,128)(2,1)S(1)} collective-permute-done((bf16[2048,128]{1,0:T(8,128)(2,1)S(1)}, bf16[2048,128]{1,0:T(8,128)(2,1)S(1)}, u32[]{:S(2)}, u32[]{:S(2)}) %collective-permute-start.13) | collective-permute-done | bytes 524320 | tf_op jit(solution)/shard_map/ppermute | solution.py:37
  47.6 4.8 %collective-permute-done.11.refs_0_ = bf16[2048,128]{1,0:T(8,128)(2,1)S(1)} collective-permute-done((bf16[2048,128]{1,0:T(8,128)(2,1)S(1)}, bf16[2048,128]{1,0:T(8,128)(2,1)S(1)}, u32[]{:S(2)}, u32[]{:S(2)}) %collective-permute-start.11) | collective-permute-done | bytes 524320 | tf_op jit(solution)/shard_map/ppermute | solution.py:37
  53.3 1.4 %collective-permute-start.15 = (f32[136,128]{1,0:T(8,128)S(1)}, f32[136,128]{1,0:T(8,128)S(1)}, u32[]{:S(2)}, u32[]{:S(2)}) collective-permute-start(f32[136,128]{1,0:T(8,128)S(1)} %get-tuple-element.57), channel_id=1, source_target_pairs={{0,1},{1,0},{2,3},{3,2},{4,5},{5,4},{6,7},{7,6},{8,9},{9,8},{10,11... | collective-permute-start | bytes 208904 | tf_op jit(solution)/shard_map/ppermute | solution.py:37
  54.6 0.9 collective-permute-done.15.partial
  55.6 1.1 %shard_map.99 = (bf16[128,256]{1,0:T(8,128)(2,1)}, f32[136,128]{1,0:T(8,128)S(1)}, f32[136,128]{1,0:T(8,128)S(1)}) custom-call(s32[1]{0:T(128)} %bitcast.core, f32[128,128]{1,0:T(8,128)S(1)} %get-tuple-element.56.ours, f32[136,128]{1,0:T(8,128)S(1)} %collective-permute-done.15.partial, bf16[16,128]{1,0:T(8,128)(2,1)S(1)} %get-tuple-element.58.largest_in, ...), custom_call_target="tpu_custom_call" | custom-call | flops 1024 | bytes 1024 | tf_op jit(solution)/shard_map/pallas_call | solution.py:218
  58.0 2.4 %collective-permute-start.17 = (f32[136,128]{1,0:T(8,128)S(1)}, f32[136,128]{1,0:T(8,128)S(1)}, u32[]{:S(2)}, u32[]{:S(2)}) collective-permute-start(f32[136,128]{1,0:T(8,128)S(1)} %add.57), channel_id=1, source_target_pairs={{0,32},{1,9},{2,34},{3,11},{4,36},{5,13},{6,38},{7,15},{8,40},{9,1... | collective-permute-start | bytes 208904 | tf_op jit(solution)/shard_map/ppermute | solution.py:37
  60.4 1.2 %collective-permute-start.18 = (f32[136,128]{1,0:T(8,128)S(1)}, f32[136,128]{1,0:T(8,128)S(1)}, u32[]{:S(2)}, u32[]{:S(2)}) collective-permute-start(f32[136,128]{1,0:T(8,128)S(1)} %add.57), channel_id=1, source_target_pairs={{0,16},{1,5},{2,18},{3,7},{4,20},{5,9},{6,22},{7,11},{8,24},{9,13}... | collective-permute-start | bytes 208904 | tf_op jit(solution)/shard_map/ppermute | solution.py:37
  61.6 1.5 %collective-permute-start.19 = (f32[136,128]{1,0:T(8,128)S(1)}, f32[136,128]{1,0:T(8,128)S(1)}, u32[]{:S(2)}, u32[]{:S(2)}) collective-permute-start(f32[136,128]{1,0:T(8,128)S(1)} %add.57), channel_id=1, source_target_pairs={{0,48},{1,13},{2,50},{3,15},{4,52},{5,1},{6,54},{7,3},{8,56},{9,5}... | collective-permute-start | bytes 208904 | tf_op jit(solution)/shard_map/ppermute | solution.py:37
  63.1 1.7 %collective-permute-done.18 = f32[136,128]{1,0:T(8,128)S(1)} collective-permute-done((f32[136,128]{1,0:T(8,128)S(1)}, f32[136,128]{1,0:T(8,128)S(1)}, u32[]{:S(2)}, u32[]{:S(2)}) %collective-permute-start.18) | collective-permute-done | bytes 69664 | tf_op jit(solution)/shard_map/ppermute | solution.py:37
  64.8 3.0 %collective-permute-start.20 = (f32[136,128]{1,0:T(8,128)S(1)}, f32[136,128]{1,0:T(8,128)S(1)}, u32[]{:S(2)}, u32[]{:S(2)}) collective-permute-start(f32[136,128]{1,0:T(8,128)S(1)} %add_add_fusion.2), channel_id=1, source_target_pairs={{0,8},{1,33},{2,10},{3,35},{4,12},{5,37},{6,14},{7,39},{8,0},{9,41... | collective-permute-start | bytes 208904 | tf_op jit(solution)/shard_map/ppermute | solution.py:37
  68.0 2.6 %collective-permute-start.22 = (f32[136,128]{1,0:T(8,128)S(1)}, f32[136,128]{1,0:T(8,128)S(1)}, u32[]{:S(2)}, u32[]{:S(2)}) collective-permute-start(f32[136,128]{1,0:T(8,128)S(1)} %add_add_fusion.2), channel_id=1, source_target_pairs={{0,12},{1,49},{2,14},{3,51},{4,0},{5,53},{6,2},{7,55},{8,4},{9,57}... | collective-permute-start | bytes 208904 | tf_op jit(solution)/shard_map/ppermute | solution.py:37
  70.5 2.0 %collective-permute-done.21 = f32[136,128]{1,0:T(8,128)S(1)} collective-permute-done((f32[136,128]{1,0:T(8,128)S(1)}, f32[136,128]{1,0:T(8,128)S(1)}, u32[]{:S(2)}, u32[]{:S(2)}) %collective-permute-start.21) | collective-permute-done | bytes 69664 | tf_op jit(solution)/shard_map/ppermute | solution.py:37
  73.3 2.4 %collective-permute-done.23 = f32[136,128]{1,0:T(8,128)S(1)} collective-permute-done((f32[136,128]{1,0:T(8,128)S(1)}, f32[136,128]{1,0:T(8,128)S(1)}, u32[]{:S(2)}, u32[]{:S(2)}) %collective-permute-start.23) | collective-permute-done | bytes 69664 | tf_op jit(solution)/shard_map/ppermute | solution.py:37
  75.8 3.6 %collective-permute-start.24 = (f32[136,128]{1,0:T(8,128)S(1)}, f32[136,128]{1,0:T(8,128)S(1)}, u32[]{:S(2)}, u32[]{:S(2)}) collective-permute-start(f32[136,128]{1,0:T(8,128)S(1)} %add.64), channel_id=1, source_target_pairs={{0,128},{1,129},{2,130},{3,131},{4,132},{5,133},{6,134},{7,135},{8... | collective-permute-start | bytes 208904 | tf_op jit(solution)/shard_map/ppermute | solution.py:37
  79.3 3.6 %collective-permute-start.26 = (f32[136,128]{1,0:T(8,128)S(1)}, f32[136,128]{1,0:T(8,128)S(1)}, u32[]{:S(2)}, u32[]{:S(2)}) collective-permute-start(f32[136,128]{1,0:T(8,128)S(1)} %add.64), channel_id=1, source_target_pairs={{0,192},{1,193},{2,194},{3,195},{4,196},{5,197},{6,198},{7,199},{8... | collective-permute-start | bytes 208904 | tf_op jit(solution)/shard_map/ppermute | solution.py:37
  83.0 1.7 %collective-permute-done.25 = f32[136,128]{1,0:T(8,128)S(1)} collective-permute-done((f32[136,128]{1,0:T(8,128)S(1)}, f32[136,128]{1,0:T(8,128)S(1)}, u32[]{:S(2)}, u32[]{:S(2)}) %collective-permute-start.25) | collective-permute-done | bytes 69664 | tf_op jit(solution)/shard_map/ppermute | solution.py:37
  84.9 5.7 %collective-permute-start.27 = (f32[136,128]{1,0:T(8,128)S(1)}, f32[136,128]{1,0:T(8,128)S(1)}, u32[]{:S(2)}, u32[]{:S(2)}) collective-permute-start(f32[136,128]{1,0:T(8,128)S(1)} %add_add_fusion), channel_id=1, source_target_pairs={{0,1},{1,0},{2,3},{3,2},{4,5},{5,4},{6,7},{7,6},{8,9},{9,8},{10,11... | collective-permute-start | bytes 208904 | tf_op jit(solution)/shard_map/ppermute | solution.py:37
  (56 shorter events, 9.4 us)
Async XLA Ops:
  0.6 4.8 %collective-permute-start = (bf16[128,128]{1,0:T(8,128)(2,1)}, bf16[128,128]{1,0:T(8,128)(2,1)S(1)}, u32[]{:S(2)}, u32[]{:S(2)}) collective-permute-start(bf16[128,128]{1,0:T(8,128)(2,1)} %own.1), channel_id=1, source_target_pairs={{0,1},{1,0},{2,3},{3,2},{4,5},{5,4},{6,7},{7,6},{8,9},{9,8},{10,11... | collective-permute-start | bytes 98312 | tf_op jit(solution)/shard_map/ppermute | solution.py:37
  5.4 15.4 %collective-permute-start.1 = (bf16[256,128]{1,0:T(8,128)(2,1)S(1)}, bf16[256,128]{1,0:T(8,128)(2,1)S(1)}, u32[]{:S(2)}, u32[]{:S(2)}) collective-permute-start(bf16[256,128]{1,0:T(8,128)(2,1)S(1)} %constant_dynamic-update-slice_fusion), channel_id=1, source_target_pairs={{0,66},{1,131},{2,128},{3,193},{4,70},{5,135},{6,132},{7,197},{8,7... | collective-permute-start | bytes 196616 | tf_op jit(solution)/shard_map/ppermute | solution.py:37
  10.2 10.6 %collective-permute-start.2 = (bf16[256,128]{1,0:T(8,128)(2,1)S(1)}, bf16[256,128]{1,0:T(8,128)(2,1)S(1)}, u32[]{:S(2)}, u32[]{:S(2)}) collective-permute-start(bf16[256,128]{1,0:T(8,128)(2,1)S(1)} %constant_dynamic-update-slice_fusion), channel_id=1, source_target_pairs={{0,64},{1,193},{2,66},{3,195},{4,68},{5,197},{6,70},{7,199},{8,72}... | collective-permute-start | bytes 196616 | tf_op jit(solution)/shard_map/ppermute | solution.py:37
  10.5 10.4 %collective-permute-start.3 = (bf16[256,128]{1,0:T(8,128)(2,1)S(1)}, bf16[256,128]{1,0:T(8,128)(2,1)S(1)}, u32[]{:S(2)}, u32[]{:S(2)}) collective-permute-start(bf16[256,128]{1,0:T(8,128)(2,1)S(1)} %constant_dynamic-update-slice_fusion), channel_id=1, source_target_pairs={{0,2},{1,195},{2,64},{3,1},{4,6},{5,199},{6,68},{7,5},{8,10},{9,20... | collective-permute-start | bytes 196616 | tf_op jit(solution)/shard_map/ppermute | solution.py:37
  11.0 9.9 %collective-permute-start.4 = (bf16[256,128]{1,0:T(8,128)(2,1)S(1)}, bf16[256,128]{1,0:T(8,128)(2,1)S(1)}, u32[]{:S(2)}, u32[]{:S(2)}) collective-permute-start(bf16[256,128]{1,0:T(8,128)(2,1)S(1)} %constant_dynamic-update-slice_fusion), channel_id=1, source_target_pairs={{0,0},{1,129},{2,2},{3,131},{4,4},{5,133},{6,6},{7,135},{8,8},{9,1... | collective-permute-start | bytes 196616 | tf_op jit(solution)/shard_map/ppermute | solution.py:37
  20.9 9.8 %collective-permute-start.5 = (bf16[1024,128]{1,0:T(8,128)(2,1)S(1)}, bf16[1024,128]{1,0:T(8,128)(2,1)S(1)}, u32[]{:S(2)}, u32[]{:S(2)}) collective-permute-start(bf16[1024,128]{1,0:T(8,128)(2,1)S(1)} %pad_maximum_fusion.2), channel_id=1, source_target_pairs={{0,16},{1,5},{2,18},{3,7},{4,20},{5,9},{6,22},{7,11},{8,24},{9,13}... | collective-permute-start | bytes 786440 | tf_op jit(solution)/shard_map/ppermute | solution.py:37
  22.3 8.4 %collective-permute-start.6 = (bf16[1024,128]{1,0:T(8,128)(2,1)S(1)}, bf16[1024,128]{1,0:T(8,128)(2,1)S(1)}, u32[]{:S(2)}, u32[]{:S(2)}) collective-permute-start(bf16[1024,128]{1,0:T(8,128)(2,1)S(1)} %pad_maximum_fusion.2), channel_id=1, source_target_pairs={{0,48},{1,13},{2,50},{3,15},{4,52},{5,1},{6,54},{7,3},{8,56},{9,5}... | collective-permute-start | bytes 786440 | tf_op jit(solution)/shard_map/ppermute | solution.py:37
  23.8 7.7 %collective-permute-start.7 = (bf16[1024,128]{1,0:T(8,128)(2,1)S(1)}, bf16[1024,128]{1,0:T(8,128)(2,1)S(1)}, u32[]{:S(2)}, u32[]{:S(2)}) collective-permute-start(bf16[1024,128]{1,0:T(8,128)(2,1)S(1)} %pad_maximum_fusion.2), channel_id=1, source_target_pairs={{0,32},{1,9},{2,34},{3,11},{4,36},{5,13},{6,38},{7,15},{8,40},{9,1... | collective-permute-start | bytes 786440 | tf_op jit(solution)/shard_map/ppermute | solution.py:37
  31.5 9.7 %collective-permute-start.10 = (bf16[4,128,4096]{2,1,0:T(8,128)(2,1)S(1)}, bf16[4,128,4096]{2,1,0:T(8,128)(2,1)S(1)}, u32[]{:S(2)}, u32[]{:S(2)}) collective-permute-start(bf16[4,128,4096]{2,1,0:T(8,128)(2,1)S(1)} %get-tuple-element.46), channel_id=1, source_target_pairs={{0,1},{1,0},{2,3},{3,2},{4,5},{5,4},{6,7},{7,6},{8,9},{9,8},{10,11... | collective-permute-start | bytes 12582920 | tf_op jit(solution)/shard_map/ppermute | solution.py:37
  31.6 9.6 %collective-permute-start.8 = (bf16[2048,128]{1,0:T(8,128)(2,1)S(1)}, bf16[2048,128]{1,0:T(8,128)(2,1)S(1)}, u32[]{:S(2)}, u32[]{:S(2)}) collective-permute-start(bf16[2048,128]{1,0:T(8,128)(2,1)S(1)} %pad_maximum_fusion.refs_0_), channel_id=1, source_target_pairs={{0,4},{1,17},{2,6},{3,19},{4,8},{5,21},{6,10},{7,23},{8,12},{9,25}... | collective-permute-start | bytes 1572872 | tf_op jit(solution)/shard_map/ppermute | solution.py:37
  32.9 8.3 %collective-permute-start.9 = (bf16[2048,128]{1,0:T(8,128)(2,1)S(1)}, bf16[2048,128]{1,0:T(8,128)(2,1)S(1)}, u32[]{:S(2)}, u32[]{:S(2)}) collective-permute-start(bf16[2048,128]{1,0:T(8,128)(2,1)S(1)} %pad_maximum_fusion.1.refs_1_), channel_id=1, source_target_pairs={{0,12},{1,49},{2,14},{3,51},{4,0},{5,53},{6,2},{7,55},{8,4},{9,57}... | collective-permute-start | bytes 1572872 | tf_op jit(solution)/shard_map/ppermute | solution.py:37
  34.4 12.5 %collective-permute-start.13 = (bf16[2048,128]{1,0:T(8,128)(2,1)S(1)}, bf16[2048,128]{1,0:T(8,128)(2,1)S(1)}, u32[]{:S(2)}, u32[]{:S(2)}) collective-permute-start(bf16[2048,128]{1,0:T(8,128)(2,1)S(1)} %pad_maximum_fusion.1.refs_1_), channel_id=1, source_target_pairs={{0,4},{1,17},{2,6},{3,19},{4,8},{5,21},{6,10},{7,23},{8,12},{9,25}... | collective-permute-start | bytes 1572872 | tf_op jit(solution)/shard_map/ppermute | solution.py:37
  34.4 12.5 %collective-permute-start.14 = (bf16[2048,128]{1,0:T(8,128)(2,1)S(1)}, bf16[2048,128]{1,0:T(8,128)(2,1)S(1)}, u32[]{:S(2)}, u32[]{:S(2)}) collective-permute-start(bf16[2048,128]{1,0:T(8,128)(2,1)S(1)} %pad_maximum_fusion.refs_0_), channel_id=1, source_target_pairs={{0,12},{1,49},{2,14},{3,51},{4,0},{5,53},{6,2},{7,55},{8,4},{9,57}... | collective-permute-start | bytes 1572872 | tf_op jit(solution)/shard_map/ppermute | solution.py:37
  41.2 11.2 %collective-permute-start.11 = (bf16[2048,128]{1,0:T(8,128)(2,1)S(1)}, bf16[2048,128]{1,0:T(8,128)(2,1)S(1)}, u32[]{:S(2)}, u32[]{:S(2)}) collective-permute-start(bf16[2048,128]{1,0:T(8,128)(2,1)S(1)} %collective-permute-done.8.refs_2_), channel_id=1, source_target_pairs={{0,4},{1,17},{2,6},{3,19},{4,8},{5,21},{6,10},{7,23},{8,12},{9,25}... | collective-permute-start | bytes 1572872 | tf_op jit(solution)/shard_map/ppermute | solution.py:37
  42.4 10.0 %collective-permute-start.12 = (bf16[2048,128]{1,0:T(8,128)(2,1)S(1)}, bf16[2048,128]{1,0:T(8,128)(2,1)S(1)}, u32[]{:S(2)}, u32[]{:S(2)}) collective-permute-start(bf16[2048,128]{1,0:T(8,128)(2,1)S(1)} %collective-permute-done.9.refs_3_), channel_id=1, source_target_pairs={{0,12},{1,49},{2,14},{3,51},{4,0},{5,53},{6,2},{7,55},{8,4},{9,57}... | collective-permute-start | bytes 1572872 | tf_op jit(solution)/shard_map/ppermute | solution.py:37
  52.5 3.1 %copy-start = (bf16[128,128]{1,0:T(8,128)(2,1)S(1)}, bf16[128,128]{1,0:T(8,128)(2,1)}, u32[]{:S(2)}) copy-start(bf16[128,128]{1,0:T(8,128)(2,1)} %own.1) | copy-start | bytes 98308
  52.5 3.1 %copy-start.1 = (bf16[128,256]{1,0:T(8,128)(2,1)S(1)}, bf16[128,256]{1,0:T(8,128)(2,1)}, u32[]{:S(2)}) copy-start(bf16[128,256]{1,0:T(8,128)(2,1)} %weight.1) | copy-start | bytes 196612
  52.5 3.1 %copy-start.2 = (bf16[128,256]{1,0:T(8,128)(2,1)S(1)}, bf16[128,256]{1,0:T(8,128)(2,1)}, u32[]{:S(2)}) copy-start(bf16[128,256]{1,0:T(8,128)(2,1)} %cotangent.1) | copy-start | bytes 196612
  52.5 3.1 %copy-start.3 = (f32[256]{0:T(256)S(1)}, f32[256]{0:T(256)}, u32[]{:S(2)}) copy-start(f32[256]{0:T(256)} %param.12) | copy-start | bytes 3076
  53.3 2.3 %collective-permute-start.15 = (f32[136,128]{1,0:T(8,128)S(1)}, f32[136,128]{1,0:T(8,128)S(1)}, u32[]{:S(2)}, u32[]{:S(2)}) collective-permute-start(f32[136,128]{1,0:T(8,128)S(1)} %get-tuple-element.57), channel_id=1, source_target_pairs={{0,1},{1,0},{2,3},{3,2},{4,5},{5,4},{6,7},{7,6},{8,9},{9,8},{10,11... | collective-permute-start | bytes 208904 | tf_op jit(solution)/shard_map/ppermute | solution.py:37
  56.7 1.3 %collective-permute-start.16 = (f32[136,128]{1,0:T(8,128)S(1)}, f32[136,128]{1,0:T(8,128)S(1)}, u32[]{:S(2)}, u32[]{:S(2)}) collective-permute-start(f32[136,128]{1,0:T(8,128)S(1)} %get-tuple-element.62), channel_id=1, source_target_pairs={{0,1},{1,0},{2,3},{3,2},{4,5},{5,4},{6,7},{7,6},{8,9},{9,8},{10,11... | collective-permute-start | bytes 208904 | tf_op jit(solution)/shard_map/ppermute | solution.py:37
  58.0 5.1 %collective-permute-start.17 = (f32[136,128]{1,0:T(8,128)S(1)}, f32[136,128]{1,0:T(8,128)S(1)}, u32[]{:S(2)}, u32[]{:S(2)}) collective-permute-start(f32[136,128]{1,0:T(8,128)S(1)} %add.57), channel_id=1, source_target_pairs={{0,32},{1,9},{2,34},{3,11},{4,36},{5,13},{6,38},{7,15},{8,40},{9,1... | collective-permute-start | bytes 208904 | tf_op jit(solution)/shard_map/ppermute | solution.py:37
  60.4 4.4 %collective-permute-start.18 = (f32[136,128]{1,0:T(8,128)S(1)}, f32[136,128]{1,0:T(8,128)S(1)}, u32[]{:S(2)}, u32[]{:S(2)}) collective-permute-start(f32[136,128]{1,0:T(8,128)S(1)} %add.57), channel_id=1, source_target_pairs={{0,16},{1,5},{2,18},{3,7},{4,20},{5,9},{6,22},{7,11},{8,24},{9,13}... | collective-permute-start | bytes 208904 | tf_op jit(solution)/shard_map/ppermute | solution.py:37
  61.6 3.2 %collective-permute-start.19 = (f32[136,128]{1,0:T(8,128)S(1)}, f32[136,128]{1,0:T(8,128)S(1)}, u32[]{:S(2)}, u32[]{:S(2)}) collective-permute-start(f32[136,128]{1,0:T(8,128)S(1)} %add.57), channel_id=1, source_target_pairs={{0,48},{1,13},{2,50},{3,15},{4,52},{5,1},{6,54},{7,3},{8,56},{9,5}... | collective-permute-start | bytes 208904 | tf_op jit(solution)/shard_map/ppermute | solution.py:37
  64.8 5.7 %collective-permute-start.20 = (f32[136,128]{1,0:T(8,128)S(1)}, f32[136,128]{1,0:T(8,128)S(1)}, u32[]{:S(2)}, u32[]{:S(2)}) collective-permute-start(f32[136,128]{1,0:T(8,128)S(1)} %add_add_fusion.2), channel_id=1, source_target_pairs={{0,8},{1,33},{2,10},{3,35},{4,12},{5,37},{6,14},{7,39},{8,0},{9,41... | collective-permute-start | bytes 208904 | tf_op jit(solution)/shard_map/ppermute | solution.py:37
  67.9 4.6 %collective-permute-start.21 = (f32[136,128]{1,0:T(8,128)S(1)}, f32[136,128]{1,0:T(8,128)S(1)}, u32[]{:S(2)}, u32[]{:S(2)}) collective-permute-start(f32[136,128]{1,0:T(8,128)S(1)} %add_add_fusion.2), channel_id=1, source_target_pairs={{0,4},{1,17},{2,6},{3,19},{4,8},{5,21},{6,10},{7,23},{8,12},{9,25}... | collective-permute-start | bytes 208904 | tf_op jit(solution)/shard_map/ppermute | solution.py:37
  68.0 4.5 %collective-permute-start.22 = (f32[136,128]{1,0:T(8,128)S(1)}, f32[136,128]{1,0:T(8,128)S(1)}, u32[]{:S(2)}, u32[]{:S(2)}) collective-permute-start(f32[136,128]{1,0:T(8,128)S(1)} %add_add_fusion.2), channel_id=1, source_target_pairs={{0,12},{1,49},{2,14},{3,51},{4,0},{5,53},{6,2},{7,55},{8,4},{9,57}... | collective-permute-start | bytes 208904 | tf_op jit(solution)/shard_map/ppermute | solution.py:37
  72.5 3.2 %collective-permute-start.23 = (f32[136,128]{1,0:T(8,128)S(1)}, f32[136,128]{1,0:T(8,128)S(1)}, u32[]{:S(2)}, u32[]{:S(2)}) collective-permute-start(f32[136,128]{1,0:T(8,128)S(1)} %add_add_fusion.1), channel_id=1, source_target_pairs={{0,2},{1,3},{2,0},{3,1},{4,6},{5,7},{6,4},{7,5},{8,10},{9,11},{10,... | collective-permute-start | bytes 208904 | tf_op jit(solution)/shard_map/ppermute | solution.py:37
  75.8 7.3 %collective-permute-start.24 = (f32[136,128]{1,0:T(8,128)S(1)}, f32[136,128]{1,0:T(8,128)S(1)}, u32[]{:S(2)}, u32[]{:S(2)}) collective-permute-start(f32[136,128]{1,0:T(8,128)S(1)} %add.64), channel_id=1, source_target_pairs={{0,128},{1,129},{2,130},{3,131},{4,132},{5,133},{6,134},{7,135},{8... | collective-permute-start | bytes 208904 | tf_op jit(solution)/shard_map/ppermute | solution.py:37
  79.3 5.4 %collective-permute-start.25 = (f32[136,128]{1,0:T(8,128)S(1)}, f32[136,128]{1,0:T(8,128)S(1)}, u32[]{:S(2)}, u32[]{:S(2)}) collective-permute-start(f32[136,128]{1,0:T(8,128)S(1)} %add.64), channel_id=1, source_target_pairs={{0,64},{1,65},{2,66},{3,67},{4,68},{5,69},{6,70},{7,71},{8,72},{9,... | collective-permute-start | bytes 208904 | tf_op jit(solution)/shard_map/ppermute | solution.py:37
  79.3 5.5 %collective-permute-start.26 = (f32[136,128]{1,0:T(8,128)S(1)}, f32[136,128]{1,0:T(8,128)S(1)}, u32[]{:S(2)}, u32[]{:S(2)}) collective-permute-start(f32[136,128]{1,0:T(8,128)S(1)} %add.64), channel_id=1, source_target_pairs={{0,192},{1,193},{2,194},{3,195},{4,196},{5,197},{6,198},{7,199},{8... | collective-permute-start | bytes 208904 | tf_op jit(solution)/shard_map/ppermute | solution.py:37
  84.9 6.6 %collective-permute-start.27 = (f32[136,128]{1,0:T(8,128)S(1)}, f32[136,128]{1,0:T(8,128)S(1)}, u32[]{:S(2)}, u32[]{:S(2)}) collective-permute-start(f32[136,128]{1,0:T(8,128)S(1)} %add_add_fusion), channel_id=1, source_target_pairs={{0,1},{1,0},{2,3},{3,2},{4,5},{5,4},{6,7},{7,6},{8,9},{9,8},{10,11... | collective-permute-start | bytes 208904 | tf_op jit(solution)/shard_map/ppermute | solution.py:37

commit v5 on v4

--- a/solution.py
+++ b/solution.py
@@ -239,7 +239,8 @@
     for turned in (False, True):
         part = ring_sum(lambda array, step: along_xy(array, step, turned), part)
     part = part + swap_pairs(part)
-    part = ring_sum(along_zh, part)
+    part = part.astype(jnp.bfloat16).astype(jnp.float32)
+    part = ring_sum(lambda array, step: along_zh(array.astype(jnp.bfloat16), step).astype(jnp.float32), part)
     other = swap_cores(part)
     left, right = jnp.where(core == 0, part, other), jnp.where(core == 0, other, part)
     both = jnp.concatenate([left, right], axis=1)

time: 93.1 us -> 92.4 us (level)
  transfers between devices with their start and end apart: 28 -> 28, of which waited for: 13 -> 11; matrix products, arithmetic and copies ran while one was open for 2% -> 2% of each run, Pallas kernels for 12% -> 12%
where the time goes in v5:
time: 92.4 us; the launch traced here: 92.1 us
  starting transfers between devices  53.9 us (58%)
  waiting for transfers between devices  21.6 us (23%)
  Pallas kernels  12.9 us (14%)
  other arithmetic  2.11 us (2%)
    ppermute x28, starting transfers between devices, permute(): lax.ppermute(array, NAMES, [(index_of(*at), index_of(*move(*at))) for at...  53.9 us
    ppermute x28, waiting for transfers between devices, permute(): lax.ppermute(array, NAMES, [(index_of(*at), index_of(*move(*at))) for at...  21.6 us
    pallas_call x2, Pallas kernels, order_adjacency(): pl.pallas_call(functools.partial(order_kernel, first), out_shape=[jax.Sha...  8.78 us
    pallas_call x3, Pallas kernels, piece_step(): pl.pallas_call(functools.partial(piece_kernel, spots, last), out_shape=[j...  2.97 us
  transfers between devices with their start and end apart: 28, of which 11 were waited for; matrix products, arithmetic and copies ran while one was open for 2% of the time, Pallas kernels for 12%

profile of v5, /device:TPU:1, one launch (start us, length us, event | category | flops | bytes accessed | tf_op | source)
XLA Modules:
  0.0 92.1 jit_solution(4285256111642240270)
XLA Ops:
  0.6 3.3 %collective-permute-start = (bf16[128,128]{1,0:T(8,128)(2,1)}, bf16[128,128]{1,0:T(8,128)(2,1)S(1)}, u32[]{:S(2)}, u32[]{:S(2)}) collective-permute-start(bf16[128,128]{1,0:T(8,128)(2,1)} %own.1), channel_id=1, source_target_pairs={{0,1},{1,0},{2,3},{3,2},{4,5},{5,4},{6,7},{7,6},{8,9},{9,8},{10,11... | collective-permute-start | bytes 98312 | tf_op jit(solution)/shard_map/ppermute | solution.py:37
  5.4 4.8 %collective-permute-start.1 = (bf16[256,128]{1,0:T(8,128)(2,1)S(1)}, bf16[256,128]{1,0:T(8,128)(2,1)S(1)}, u32[]{:S(2)}, u32[]{:S(2)}) collective-permute-start(bf16[256,128]{1,0:T(8,128)(2,1)S(1)} %constant_dynamic-update-slice_fusion), channel_id=1, source_target_pairs={{0,66},{1,131},{2,128},{3,193},{4,70},{5,135},{6,132},{7,197},{8,7... | collective-permute-start | bytes 196616 | tf_op jit(solution)/shard_map/ppermute | solution.py:37
  11.0 6.4 %collective-permute-start.4 = (bf16[256,128]{1,0:T(8,128)(2,1)S(1)}, bf16[256,128]{1,0:T(8,128)(2,1)S(1)}, u32[]{:S(2)}, u32[]{:S(2)}) collective-permute-start(bf16[256,128]{1,0:T(8,128)(2,1)S(1)} %constant_dynamic-update-slice_fusion), channel_id=1, source_target_pairs={{0,0},{1,129},{2,2},{3,131},{4,4},{5,133},{6,6},{7,135},{8,8},{9,1... | collective-permute-start | bytes 196616 | tf_op jit(solution)/shard_map/ppermute | solution.py:37
  17.4 3.5 %shard_map.94 = (bf16[4,128,4096]{2,1,0:T(8,128)(2,1)S(1)}, bf16[4,128,4096]{2,1,0:T(8,128)(2,1)S(1)}, f32[128,128]{1,0:T(8,128)S(1)}) custom-call(s32[320]{0:T(512)S(1)} %pad_add_fusion.table, bf16[128,32768]{1,0:T(8,128)(2,1)} %adjacency.3), custom_call_target="tpu_custom_call" | custom-call | flops 1024 | bytes 1024 | tf_op jit(solution)/shard_map/pallas_call | solution.py:132
  20.9 1.4 %collective-permute-start.5 = (bf16[1024,128]{1,0:T(8,128)(2,1)S(1)}, bf16[1024,128]{1,0:T(8,128)(2,1)S(1)}, u32[]{:S(2)}, u32[]{:S(2)}) collective-permute-start(bf16[1024,128]{1,0:T(8,128)(2,1)S(1)} %pad_maximum_fusion.2), channel_id=1, source_target_pairs={{0,16},{1,5},{2,18},{3,7},{4,20},{5,9},{6,22},{7,11},{8,24},{9,13}... | collective-permute-start | bytes 786440 | tf_op jit(solution)/shard_map/ppermute | solution.py:37
  22.3 1.5 %collective-permute-start.6 = (bf16[1024,128]{1,0:T(8,128)(2,1)S(1)}, bf16[1024,128]{1,0:T(8,128)(2,1)S(1)}, u32[]{:S(2)}, u32[]{:S(2)}) collective-permute-start(bf16[1024,128]{1,0:T(8,128)(2,1)S(1)} %pad_maximum_fusion.2), channel_id=1, source_target_pairs={{0,48},{1,13},{2,50},{3,15},{4,52},{5,1},{6,54},{7,3},{8,56},{9,5}... | collective-permute-start | bytes 786440 | tf_op jit(solution)/shard_map/ppermute | solution.py:37
  23.8 1.5 %collective-permute-start.7 = (bf16[1024,128]{1,0:T(8,128)(2,1)S(1)}, bf16[1024,128]{1,0:T(8,128)(2,1)S(1)}, u32[]{:S(2)}, u32[]{:S(2)}) collective-permute-start(bf16[1024,128]{1,0:T(8,128)(2,1)S(1)} %pad_maximum_fusion.2), channel_id=1, source_target_pairs={{0,32},{1,9},{2,34},{3,11},{4,36},{5,13},{6,38},{7,15},{8,40},{9,1... | collective-permute-start | bytes 786440 | tf_op jit(solution)/shard_map/ppermute | solution.py:37
  25.4 5.3 %shard_map.95 = (bf16[4,128,4096]{2,1,0:T(8,128)(2,1)S(1)}, bf16[4,128,4096]{2,1,0:T(8,128)(2,1)S(1)}, f32[128,128]{1,0:T(8,128)S(1)}) custom-call(s32[320]{0:T(512)S(1)} %pad_add_fusion.table, bf16[128,32768]{1,0:T(8,128)(2,1)} %adjacency.3, ...), custom_call_target="tpu_custom_call", output_to_operand_aliasing={{0}: (2, {}), {1}: (3, {}), {2}: (4, {})} | custom-call | flops 1024 | bytes 1024 | tf_op jit(solution)/shard_map/pallas_call | solution.py:132
  31.6 1.3 %collective-permute-start.8 = (bf16[2048,128]{1,0:T(8,128)(2,1)S(1)}, bf16[2048,128]{1,0:T(8,128)(2,1)S(1)}, u32[]{:S(2)}, u32[]{:S(2)}) collective-permute-start(bf16[2048,128]{1,0:T(8,128)(2,1)S(1)} %pad_maximum_fusion.refs_0_), channel_id=1, source_target_pairs={{0,4},{1,17},{2,6},{3,19},{4,8},{5,21},{6,10},{7,23},{8,12},{9,25}... | collective-permute-start | bytes 1572872 | tf_op jit(solution)/shard_map/ppermute | solution.py:37
  32.9 1.5 %collective-permute-start.9 = (bf16[2048,128]{1,0:T(8,128)(2,1)S(1)}, bf16[2048,128]{1,0:T(8,128)(2,1)S(1)}, u32[]{:S(2)}, u32[]{:S(2)}) collective-permute-start(bf16[2048,128]{1,0:T(8,128)(2,1)S(1)} %pad_maximum_fusion.1.refs_1_), channel_id=1, source_target_pairs={{0,12},{1,49},{2,14},{3,51},{4,0},{5,53},{6,2},{7,55},{8,4},{9,57}... | collective-permute-start | bytes 1572872 | tf_op jit(solution)/shard_map/ppermute | solution.py:37
  34.4 2.7 %collective-permute-start.14 = (bf16[2048,128]{1,0:T(8,128)(2,1)S(1)}, bf16[2048,128]{1,0:T(8,128)(2,1)S(1)}, u32[]{:S(2)}, u32[]{:S(2)}) collective-permute-start(bf16[2048,128]{1,0:T(8,128)(2,1)S(1)} %pad_maximum_fusion.refs_0_), channel_id=1, source_target_pairs={{0,12},{1,49},{2,14},{3,51},{4,0},{5,53},{6,2},{7,55},{8,4},{9,57}... | collective-permute-start | bytes 1572872 | tf_op jit(solution)/shard_map/ppermute | solution.py:37
  37.0 4.2 %collective-permute-done.8.refs_2_ = bf16[2048,128]{1,0:T(8,128)(2,1)S(1)} collective-permute-done((bf16[2048,128]{1,0:T(8,128)(2,1)S(1)}, bf16[2048,128]{1,0:T(8,128)(2,1)S(1)}, u32[]{:S(2)}, u32[]{:S(2)}) %collective-permute-start.8) | collective-permute-done | bytes 524320 | tf_op jit(solution)/shard_map/ppermute | solution.py:37
  41.2 1.2 %collective-permute-start.11 = (bf16[2048,128]{1,0:T(8,128)(2,1)S(1)}, bf16[2048,128]{1,0:T(8,128)(2,1)S(1)}, u32[]{:S(2)}, u32[]{:S(2)}) collective-permute-start(bf16[2048,128]{1,0:T(8,128)(2,1)S(1)} %collective-permute-done.8.refs_2_), channel_id=1, source_target_pairs={{0,4},{1,17},{2,6},{3,19},{4,8},{5,21},{6,10},{7,23},{8,12},{9,25}... | collective-permute-start | bytes 1572872 | tf_op jit(solution)/shard_map/ppermute | solution.py:37
  42.4 1.5 %collective-permute-start.12 = (bf16[2048,128]{1,0:T(8,128)(2,1)S(1)}, bf16[2048,128]{1,0:T(8,128)(2,1)S(1)}, u32[]{:S(2)}, u32[]{:S(2)}) collective-permute-start(bf16[2048,128]{1,0:T(8,128)(2,1)S(1)} %collective-permute-done.9.refs_3_), channel_id=1, source_target_pairs={{0,12},{1,49},{2,14},{3,51},{4,0},{5,53},{6,2},{7,55},{8,4},{9,57}... | collective-permute-start | bytes 1572872 | tf_op jit(solution)/shard_map/ppermute | solution.py:37
  43.9 1.4 %shard_map.96 = (f32[128,128]{1,0:T(8,128)S(1)}, f32[128,128]{1,0:T(8,128)S(1)}, bf16[16,128]{1,0:T(8,128)(2,1)S(1)}) custom-call(bf16[4,128,4096]{2,1,0:T(8,128)(2,1)S(1)} %get-tuple-element.43.own, bf16[4,128,4096]{2,1,0:T(8,128)(2,1)S(1)} %collective-permute-done.10.got, bf16[2048,128]{1,0:T(8,128)(2,1)S(1)} %pad_maximum_fusion.refs_0_, ...), custom_call_target="tpu_custom_call" | custom-call | flops 1024 | bytes 1024 | tf_op jit(solution)/shard_map/pallas_call | solution.py:172
  45.4 1.5 %collective-permute-done.13.refs_0_ = bf16[2048,128]{1,0:T(8,128)(2,1)S(1)} collective-permute-done((bf16[2048,128]{1,0:T(8,128)(2,1)S(1)}, bf16[2048,128]{1,0:T(8,128)(2,1)S(1)}, u32[]{:S(2)}, u32[]{:S(2)}) %collective-permute-start.13) | collective-permute-done | bytes 524320 | tf_op jit(solution)/shard_map/ppermute | solution.py:37
  47.6 4.8 %collective-permute-done.11.refs_0_ = bf16[2048,128]{1,0:T(8,128)(2,1)S(1)} collective-permute-done((bf16[2048,128]{1,0:T(8,128)(2,1)S(1)}, bf16[2048,128]{1,0:T(8,128)(2,1)S(1)}, u32[]{:S(2)}, u32[]{:S(2)}) %collective-permute-start.11) | collective-permute-done | bytes 524320 | tf_op jit(solution)/shard_map/ppermute | solution.py:37
  53.3 1.4 %collective-permute-start.15 = (f32[136,128]{1,0:T(8,128)S(1)}, f32[136,128]{1,0:T(8,128)S(1)}, u32[]{:S(2)}, u32[]{:S(2)}) collective-permute-start(f32[136,128]{1,0:T(8,128)S(1)} %get-tuple-element.57), channel_id=1, source_target_pairs={{0,1},{1,0},{2,3},{3,2},{4,5},{5,4},{6,7},{7,6},{8,9},{9,8},{10,11... | collective-permute-start | bytes 208904 | tf_op jit(solution)/shard_map/ppermute | solution.py:37
  55.6 1.1 %shard_map.99 = (bf16[128,256]{1,0:T(8,128)(2,1)}, f32[136,128]{1,0:T(8,128)S(1)}, f32[136,128]{1,0:T(8,128)S(1)}) custom-call(s32[1]{0:T(128)} %bitcast.core, f32[128,128]{1,0:T(8,128)S(1)} %get-tuple-element.56.ours, f32[136,128]{1,0:T(8,128)S(1)} %collective-permute-done.15.partial, bf16[16,128]{1,0:T(8,128)(2,1)S(1)} %get-tuple-element.58.largest_in, ...), custom_call_target="tpu_custom_call" | custom-call | flops 1024 | bytes 1024 | tf_op jit(solution)/shard_map/pallas_call | solution.py:218
  57.1 0.9 collective-permute-done.16
  58.0 2.4 %collective-permute-start.17 = (f32[136,128]{1,0:T(8,128)S(1)}, f32[136,128]{1,0:T(8,128)S(1)}, u32[]{:S(2)}, u32[]{:S(2)}) collective-permute-start(f32[136,128]{1,0:T(8,128)S(1)} %add.57), channel_id=1, source_target_pairs={{0,32},{1,9},{2,34},{3,11},{4,36},{5,13},{6,38},{7,15},{8,40},{9,1... | collective-permute-start | bytes 208904 | tf_op jit(solution)/shard_map/ppermute | solution.py:37
  60.4 1.2 %collective-permute-start.18 = (f32[136,128]{1,0:T(8,128)S(1)}, f32[136,128]{1,0:T(8,128)S(1)}, u32[]{:S(2)}, u32[]{:S(2)}) collective-permute-start(f32[136,128]{1,0:T(8,128)S(1)} %add.57), channel_id=1, source_target_pairs={{0,16},{1,5},{2,18},{3,7},{4,20},{5,9},{6,22},{7,11},{8,24},{9,13}... | collective-permute-start | bytes 208904 | tf_op jit(solution)/shard_map/ppermute | solution.py:37
  61.6 1.5 %collective-permute-start.19 = (f32[136,128]{1,0:T(8,128)S(1)}, f32[136,128]{1,0:T(8,128)S(1)}, u32[]{:S(2)}, u32[]{:S(2)}) collective-permute-start(f32[136,128]{1,0:T(8,128)S(1)} %add.57), channel_id=1, source_target_pairs={{0,48},{1,13},{2,50},{3,15},{4,52},{5,1},{6,54},{7,3},{8,56},{9,5}... | collective-permute-start | bytes 208904 | tf_op jit(solution)/shard_map/ppermute | solution.py:37
  63.1 1.7 %collective-permute-done.18 = f32[136,128]{1,0:T(8,128)S(1)} collective-permute-done((f32[136,128]{1,0:T(8,128)S(1)}, f32[136,128]{1,0:T(8,128)S(1)}, u32[]{:S(2)}, u32[]{:S(2)}) %collective-permute-start.18) | collective-permute-done | bytes 69664 | tf_op jit(solution)/shard_map/ppermute | solution.py:37
  64.8 3.0 %collective-permute-start.20 = (f32[136,128]{1,0:T(8,128)S(1)}, f32[136,128]{1,0:T(8,128)S(1)}, u32[]{:S(2)}, u32[]{:S(2)}) collective-permute-start(f32[136,128]{1,0:T(8,128)S(1)} %add_add_fusion.2), channel_id=1, source_target_pairs={{0,8},{1,33},{2,10},{3,35},{4,12},{5,37},{6,14},{7,39},{8,0},{9,41... | collective-permute-start | bytes 208904 | tf_op jit(solution)/shard_map/ppermute | solution.py:37
  68.0 2.6 %collective-permute-start.22 = (f32[136,128]{1,0:T(8,128)S(1)}, f32[136,128]{1,0:T(8,128)S(1)}, u32[]{:S(2)}, u32[]{:S(2)}) collective-permute-start(f32[136,128]{1,0:T(8,128)S(1)} %add_add_fusion.2), channel_id=1, source_target_pairs={{0,12},{1,49},{2,14},{3,51},{4,0},{5,53},{6,2},{7,55},{8,4},{9,57}... | collective-permute-start | bytes 208904 | tf_op jit(solution)/shard_map/ppermute | solution.py:37
  70.5 2.0 %collective-permute-done.21 = f32[136,128]{1,0:T(8,128)S(1)} collective-permute-done((f32[136,128]{1,0:T(8,128)S(1)}, f32[136,128]{1,0:T(8,128)S(1)}, u32[]{:S(2)}, u32[]{:S(2)}) %collective-permute-start.21) | collective-permute-done | bytes 69664 | tf_op jit(solution)/shard_map/ppermute | solution.py:37
  73.3 2.4 %collective-permute-done.23 = f32[136,128]{1,0:T(8,128)S(1)} collective-permute-done((f32[136,128]{1,0:T(8,128)S(1)}, f32[136,128]{1,0:T(8,128)S(1)}, u32[]{:S(2)}, u32[]{:S(2)}) %collective-permute-start.23) | collective-permute-done | bytes 69664 | tf_op jit(solution)/shard_map/ppermute | solution.py:37
  75.8 3.6 %collective-permute-start.24 = (bf16[136,128]{1,0:T(8,128)(2,1)S(1)}, bf16[136,128]{1,0:T(8,128)(2,1)S(1)}, u32[]{:S(2)}, u32[]{:S(2)}) collective-permute-start(bf16[136,128]{1,0:T(8,128)(2,1)S(1)} %add_convert_fusion), channel_id=1, source_target_pairs={{0,128},{1,129},{2,130},{3,131},{4,132},{5,133},{6,134},{7,135},{8... | collective-permute-start | bytes 104456 | tf_op jit(solution)/shard_map/ppermute | solution.py:37
  79.3 3.6 %collective-permute-start.26 = (bf16[136,128]{1,0:T(8,128)(2,1)S(1)}, bf16[136,128]{1,0:T(8,128)(2,1)S(1)}, u32[]{:S(2)}, u32[]{:S(2)}) collective-permute-start(bf16[136,128]{1,0:T(8,128)(2,1)S(1)} %add_convert_fusion), channel_id=1, source_target_pairs={{0,192},{1,193},{2,194},{3,195},{4,196},{5,197},{6,198},{7,199},{8... | collective-permute-start | bytes 104456 | tf_op jit(solution)/shard_map/ppermute | solution.py:37
  82.9 1.4 %collective-permute-done.25 = bf16[136,128]{1,0:T(8,128)(2,1)S(1)} collective-permute-done((bf16[136,128]{1,0:T(8,128)(2,1)S(1)}, bf16[136,128]{1,0:T(8,128)(2,1)S(1)}, u32[]{:S(2)}, u32[]{:S(2)}) %collective-permute-start.25) | collective-permute-done | bytes 34848 | tf_op jit(solution)/shard_map/ppermute | solution.py:37
  84.4 5.5 %collective-permute-start.27 = (f32[136,128]{1,0:T(8,128)S(1)}, f32[136,128]{1,0:T(8,128)S(1)}, u32[]{:S(2)}, u32[]{:S(2)}) collective-permute-start(f32[136,128]{1,0:T(8,128)S(1)} %add_add_fusion), channel_id=1, source_target_pairs={{0,1},{1,0},{2,3},{3,2},{4,5},{5,4},{6,7},{7,6},{8,9},{9,8},{10,11... | collective-permute-start | bytes 208904 | tf_op jit(solution)/shard_map/ppermute | solution.py:37
  (56 shorter events, 9.1 us)
Async XLA Ops:
  0.6 4.8 %collective-permute-start = (bf16[128,128]{1,0:T(8,128)(2,1)}, bf16[128,128]{1,0:T(8,128)(2,1)S(1)}, u32[]{:S(2)}, u32[]{:S(2)}) collective-permute-start(bf16[128,128]{1,0:T(8,128)(2,1)} %own.1), channel_id=1, source_target_pairs={{0,1},{1,0},{2,3},{3,2},{4,5},{5,4},{6,7},{7,6},{8,9},{9,8},{10,11... | collective-permute-start | bytes 98312 | tf_op jit(solution)/shard_map/ppermute | solution.py:37
  5.4 15.4 %collective-permute-start.1 = (bf16[256,128]{1,0:T(8,128)(2,1)S(1)}, bf16[256,128]{1,0:T(8,128)(2,1)S(1)}, u32[]{:S(2)}, u32[]{:S(2)}) collective-permute-start(bf16[256,128]{1,0:T(8,128)(2,1)S(1)} %constant_dynamic-update-slice_fusion), channel_id=1, source_target_pairs={{0,66},{1,131},{2,128},{3,193},{4,70},{5,135},{6,132},{7,197},{8,7... | collective-permute-start | bytes 196616 | tf_op jit(solution)/shard_map/ppermute | solution.py:37
  10.2 10.6 %collective-permute-start.2 = (bf16[256,128]{1,0:T(8,128)(2,1)S(1)}, bf16[256,128]{1,0:T(8,128)(2,1)S(1)}, u32[]{:S(2)}, u32[]{:S(2)}) collective-permute-start(bf16[256,128]{1,0:T(8,128)(2,1)S(1)} %constant_dynamic-update-slice_fusion), channel_id=1, source_target_pairs={{0,64},{1,193},{2,66},{3,195},{4,68},{5,197},{6,70},{7,199},{8,72}... | collective-permute-start | bytes 196616 | tf_op jit(solution)/shard_map/ppermute | solution.py:37
  10.5 10.4 %collective-permute-start.3 = (bf16[256,128]{1,0:T(8,128)(2,1)S(1)}, bf16[256,128]{1,0:T(8,128)(2,1)S(1)}, u32[]{:S(2)}, u32[]{:S(2)}) collective-permute-start(bf16[256,128]{1,0:T(8,128)(2,1)S(1)} %constant_dynamic-update-slice_fusion), channel_id=1, source_target_pairs={{0,2},{1,195},{2,64},{3,1},{4,6},{5,199},{6,68},{7,5},{8,10},{9,20... | collective-permute-start | bytes 196616 | tf_op jit(solution)/shard_map/ppermute | solution.py:37
  11.0 9.9 %collective-permute-start.4 = (bf16[256,128]{1,0:T(8,128)(2,1)S(1)}, bf16[256,128]{1,0:T(8,128)(2,1)S(1)}, u32[]{:S(2)}, u32[]{:S(2)}) collective-permute-start(bf16[256,128]{1,0:T(8,128)(2,1)S(1)} %constant_dynamic-update-slice_fusion), channel_id=1, source_target_pairs={{0,0},{1,129},{2,2},{3,131},{4,4},{5,133},{6,6},{7,135},{8,8},{9,1... | collective-permute-start | bytes 196616 | tf_op jit(solution)/shard_map/ppermute | solution.py:37
  20.9 9.8 %collective-permute-start.5 = (bf16[1024,128]{1,0:T(8,128)(2,1)S(1)}, bf16[1024,128]{1,0:T(8,128)(2,1)S(1)}, u32[]{:S(2)}, u32[]{:S(2)}) collective-permute-start(bf16[1024,128]{1,0:T(8,128)(2,1)S(1)} %pad_maximum_fusion.2), channel_id=1, source_target_pairs={{0,16},{1,5},{2,18},{3,7},{4,20},{5,9},{6,22},{7,11},{8,24},{9,13}... | collective-permute-start | bytes 786440 | tf_op jit(solution)/shard_map/ppermute | solution.py:37
  22.3 8.4 %collective-permute-start.6 = (bf16[1024,128]{1,0:T(8,128)(2,1)S(1)}, bf16[1024,128]{1,0:T(8,128)(2,1)S(1)}, u32[]{:S(2)}, u32[]{:S(2)}) collective-permute-start(bf16[1024,128]{1,0:T(8,128)(2,1)S(1)} %pad_maximum_fusion.2), channel_id=1, source_target_pairs={{0,48},{1,13},{2,50},{3,15},{4,52},{5,1},{6,54},{7,3},{8,56},{9,5}... | collective-permute-start | bytes 786440 | tf_op jit(solution)/shard_map/ppermute | solution.py:37
  23.8 7.7 %collective-permute-start.7 = (bf16[1024,128]{1,0:T(8,128)(2,1)S(1)}, bf16[1024,128]{1,0:T(8,128)(2,1)S(1)}, u32[]{:S(2)}, u32[]{:S(2)}) collective-permute-start(bf16[1024,128]{1,0:T(8,128)(2,1)S(1)} %pad_maximum_fusion.2), channel_id=1, source_target_pairs={{0,32},{1,9},{2,34},{3,11},{4,36},{5,13},{6,38},{7,15},{8,40},{9,1... | collective-permute-start | bytes 786440 | tf_op jit(solution)/shard_map/ppermute | solution.py:37
  31.5 9.7 %collective-permute-start.10 = (bf16[4,128,4096]{2,1,0:T(8,128)(2,1)S(1)}, bf16[4,128,4096]{2,1,0:T(8,128)(2,1)S(1)}, u32[]{:S(2)}, u32[]{:S(2)}) collective-permute-start(bf16[4,128,4096]{2,1,0:T(8,128)(2,1)S(1)} %get-tuple-element.46), channel_id=1, source_target_pairs={{0,1},{1,0},{2,3},{3,2},{4,5},{5,4},{6,7},{7,6},{8,9},{9,8},{10,11... | collective-permute-start | bytes 12582920 | tf_op jit(solution)/shard_map/ppermute | solution.py:37
  31.6 9.6 %collective-permute-start.8 = (bf16[2048,128]{1,0:T(8,128)(2,1)S(1)}, bf16[2048,128]{1,0:T(8,128)(2,1)S(1)}, u32[]{:S(2)}, u32[]{:S(2)}) collective-permute-start(bf16[2048,128]{1,0:T(8,128)(2,1)S(1)} %pad_maximum_fusion.refs_0_), channel_id=1, source_target_pairs={{0,4},{1,17},{2,6},{3,19},{4,8},{5,21},{6,10},{7,23},{8,12},{9,25}... | collective-permute-start | bytes 1572872 | tf_op jit(solution)/shard_map/ppermute | solution.py:37
  32.9 8.3 %collective-permute-start.9 = (bf16[2048,128]{1,0:T(8,128)(2,1)S(1)}, bf16[2048,128]{1,0:T(8,128)(2,1)S(1)}, u32[]{:S(2)}, u32[]{:S(2)}) collective-permute-start(bf16[2048,128]{1,0:T(8,128)(2,1)S(1)} %pad_maximum_fusion.1.refs_1_), channel_id=1, source_target_pairs={{0,12},{1,49},{2,14},{3,51},{4,0},{5,53},{6,2},{7,55},{8,4},{9,57}... | collective-permute-start | bytes 1572872 | tf_op jit(solution)/shard_map/ppermute | solution.py:37
  34.4 12.5 %collective-permute-start.13 = (bf16[2048,128]{1,0:T(8,128)(2,1)S(1)}, bf16[2048,128]{1,0:T(8,128)(2,1)S(1)}, u32[]{:S(2)}, u32[]{:S(2)}) collective-permute-start(bf16[2048,128]{1,0:T(8,128)(2,1)S(1)} %pad_maximum_fusion.1.refs_1_), channel_id=1, source_target_pairs={{0,4},{1,17},{2,6},{3,19},{4,8},{5,21},{6,10},{7,23},{8,12},{9,25}... | collective-permute-start | bytes 1572872 | tf_op jit(solution)/shard_map/ppermute | solution.py:37
  34.4 12.5 %collective-permute-start.14 = (bf16[2048,128]{1,0:T(8,128)(2,1)S(1)}, bf16[2048,128]{1,0:T(8,128)(2,1)S(1)}, u32[]{:S(2)}, u32[]{:S(2)}) collective-permute-start(bf16[2048,128]{1,0:T(8,128)(2,1)S(1)} %pad_maximum_fusion.refs_0_), channel_id=1, source_target_pairs={{0,12},{1,49},{2,14},{3,51},{4,0},{5,53},{6,2},{7,55},{8,4},{9,57}... | collective-permute-start | bytes 1572872 | tf_op jit(solution)/shard_map/ppermute | solution.py:37
  41.2 11.2 %collective-permute-start.11 = (bf16[2048,128]{1,0:T(8,128)(2,1)S(1)}, bf16[2048,128]{1,0:T(8,128)(2,1)S(1)}, u32[]{:S(2)}, u32[]{:S(2)}) collective-permute-start(bf16[2048,128]{1,0:T(8,128)(2,1)S(1)} %collective-permute-done.8.refs_2_), channel_id=1, source_target_pairs={{0,4},{1,17},{2,6},{3,19},{4,8},{5,21},{6,10},{7,23},{8,12},{9,25}... | collective-permute-start | bytes 1572872 | tf_op jit(solution)/shard_map/ppermute | solution.py:37
  42.4 10.0 %collective-permute-start.12 = (bf16[2048,128]{1,0:T(8,128)(2,1)S(1)}, bf16[2048,128]{1,0:T(8,128)(2,1)S(1)}, u32[]{:S(2)}, u32[]{:S(2)}) collective-permute-start(bf16[2048,128]{1,0:T(8,128)(2,1)S(1)} %collective-permute-done.9.refs_3_), channel_id=1, source_target_pairs={{0,12},{1,49},{2,14},{3,51},{4,0},{5,53},{6,2},{7,55},{8,4},{9,57}... | collective-permute-start | bytes 1572872 | tf_op jit(solution)/shard_map/ppermute | solution.py:37
  52.5 3.1 %copy-start = (bf16[128,128]{1,0:T(8,128)(2,1)S(1)}, bf16[128,128]{1,0:T(8,128)(2,1)}, u32[]{:S(2)}) copy-start(bf16[128,128]{1,0:T(8,128)(2,1)} %own.1) | copy-start | bytes 98308
  52.5 3.1 %copy-start.1 = (bf16[128,256]{1,0:T(8,128)(2,1)S(1)}, bf16[128,256]{1,0:T(8,128)(2,1)}, u32[]{:S(2)}) copy-start(bf16[128,256]{1,0:T(8,128)(2,1)} %weight.1) | copy-start | bytes 196612
  52.5 3.1 %copy-start.2 = (bf16[128,256]{1,0:T(8,128)(2,1)S(1)}, bf16[128,256]{1,0:T(8,128)(2,1)}, u32[]{:S(2)}) copy-start(bf16[128,256]{1,0:T(8,128)(2,1)} %cotangent.1) | copy-start | bytes 196612
  52.5 3.1 %copy-start.3 = (f32[256]{0:T(256)S(1)}, f32[256]{0:T(256)}, u32[]{:S(2)}) copy-start(f32[256]{0:T(256)} %param.12) | copy-start | bytes 3076
  53.3 2.3 %collective-permute-start.15 = (f32[136,128]{1,0:T(8,128)S(1)}, f32[136,128]{1,0:T(8,128)S(1)}, u32[]{:S(2)}, u32[]{:S(2)}) collective-permute-start(f32[136,128]{1,0:T(8,128)S(1)} %get-tuple-element.57), channel_id=1, source_target_pairs={{0,1},{1,0},{2,3},{3,2},{4,5},{5,4},{6,7},{7,6},{8,9},{9,8},{10,11... | collective-permute-start | bytes 208904 | tf_op jit(solution)/shard_map/ppermute | solution.py:37
  56.7 1.3 %collective-permute-start.16 = (f32[136,128]{1,0:T(8,128)S(1)}, f32[136,128]{1,0:T(8,128)S(1)}, u32[]{:S(2)}, u32[]{:S(2)}) collective-permute-start(f32[136,128]{1,0:T(8,128)S(1)} %get-tuple-element.62), channel_id=1, source_target_pairs={{0,1},{1,0},{2,3},{3,2},{4,5},{5,4},{6,7},{7,6},{8,9},{9,8},{10,11... | collective-permute-start | bytes 208904 | tf_op jit(solution)/shard_map/ppermute | solution.py:37
  58.0 5.1 %collective-permute-start.17 = (f32[136,128]{1,0:T(8,128)S(1)}, f32[136,128]{1,0:T(8,128)S(1)}, u32[]{:S(2)}, u32[]{:S(2)}) collective-permute-start(f32[136,128]{1,0:T(8,128)S(1)} %add.57), channel_id=1, source_target_pairs={{0,32},{1,9},{2,34},{3,11},{4,36},{5,13},{6,38},{7,15},{8,40},{9,1... | collective-permute-start | bytes 208904 | tf_op jit(solution)/shard_map/ppermute | solution.py:37
  60.4 4.4 %collective-permute-start.18 = (f32[136,128]{1,0:T(8,128)S(1)}, f32[136,128]{1,0:T(8,128)S(1)}, u32[]{:S(2)}, u32[]{:S(2)}) collective-permute-start(f32[136,128]{1,0:T(8,128)S(1)} %add.57), channel_id=1, source_target_pairs={{0,16},{1,5},{2,18},{3,7},{4,20},{5,9},{6,22},{7,11},{8,24},{9,13}... | collective-permute-start | bytes 208904 | tf_op jit(solution)/shard_map/ppermute | solution.py:37
  61.6 3.2 %collective-permute-start.19 = (f32[136,128]{1,0:T(8,128)S(1)}, f32[136,128]{1,0:T(8,128)S(1)}, u32[]{:S(2)}, u32[]{:S(2)}) collective-permute-start(f32[136,128]{1,0:T(8,128)S(1)} %add.57), channel_id=1, source_target_pairs={{0,48},{1,13},{2,50},{3,15},{4,52},{5,1},{6,54},{7,3},{8,56},{9,5}... | collective-permute-start | bytes 208904 | tf_op jit(solution)/shard_map/ppermute | solution.py:37
  64.8 5.7 %collective-permute-start.20 = (f32[136,128]{1,0:T(8,128)S(1)}, f32[136,128]{1,0:T(8,128)S(1)}, u32[]{:S(2)}, u32[]{:S(2)}) collective-permute-start(f32[136,128]{1,0:T(8,128)S(1)} %add_add_fusion.2), channel_id=1, source_target_pairs={{0,8},{1,33},{2,10},{3,35},{4,12},{5,37},{6,14},{7,39},{8,0},{9,41... | collective-permute-start | bytes 208904 | tf_op jit(solution)/shard_map/ppermute | solution.py:37
  67.9 4.6 %collective-permute-start.21 = (f32[136,128]{1,0:T(8,128)S(1)}, f32[136,128]{1,0:T(8,128)S(1)}, u32[]{:S(2)}, u32[]{:S(2)}) collective-permute-start(f32[136,128]{1,0:T(8,128)S(1)} %add_add_fusion.2), channel_id=1, source_target_pairs={{0,4},{1,17},{2,6},{3,19},{4,8},{5,21},{6,10},{7,23},{8,12},{9,25}... | collective-permute-start | bytes 208904 | tf_op jit(solution)/shard_map/ppermute | solution.py:37
  68.0 4.5 %collective-permute-start.22 = (f32[136,128]{1,0:T(8,128)S(1)}, f32[136,128]{1,0:T(8,128)S(1)}, u32[]{:S(2)}, u32[]{:S(2)}) collective-permute-start(f32[136,128]{1,0:T(8,128)S(1)} %add_add_fusion.2), channel_id=1, source_target_pairs={{0,12},{1,49},{2,14},{3,51},{4,0},{5,53},{6,2},{7,55},{8,4},{9,57}... | collective-permute-start | bytes 208904 | tf_op jit(solution)/shard_map/ppermute | solution.py:37
  72.5 3.2 %collective-permute-start.23 = (f32[136,128]{1,0:T(8,128)S(1)}, f32[136,128]{1,0:T(8,128)S(1)}, u32[]{:S(2)}, u32[]{:S(2)}) collective-permute-start(f32[136,128]{1,0:T(8,128)S(1)} %add_add_fusion.1), channel_id=1, source_target_pairs={{0,2},{1,3},{2,0},{3,1},{4,6},{5,7},{6,4},{7,5},{8,10},{9,11},{10,... | collective-permute-start | bytes 208904 | tf_op jit(solution)/shard_map/ppermute | solution.py:37
  75.8 7.1 %collective-permute-start.24 = (bf16[136,128]{1,0:T(8,128)(2,1)S(1)}, bf16[136,128]{1,0:T(8,128)(2,1)S(1)}, u32[]{:S(2)}, u32[]{:S(2)}) collective-permute-start(bf16[136,128]{1,0:T(8,128)(2,1)S(1)} %add_convert_fusion), channel_id=1, source_target_pairs={{0,128},{1,129},{2,130},{3,131},{4,132},{5,133},{6,134},{7,135},{8... | collective-permute-start | bytes 104456 | tf_op jit(solution)/shard_map/ppermute | solution.py:37
  79.3 5.0 %collective-permute-start.25 = (bf16[136,128]{1,0:T(8,128)(2,1)S(1)}, bf16[136,128]{1,0:T(8,128)(2,1)S(1)}, u32[]{:S(2)}, u32[]{:S(2)}) collective-permute-start(bf16[136,128]{1,0:T(8,128)(2,1)S(1)} %add_convert_fusion), channel_id=1, source_target_pairs={{0,64},{1,65},{2,66},{3,67},{4,68},{5,69},{6,70},{7,71},{8,72},{9,... | collective-permute-start | bytes 104456 | tf_op jit(solution)/shard_map/ppermute | solution.py:37
  79.3 5.0 %collective-permute-start.26 = (bf16[136,128]{1,0:T(8,128)(2,1)S(1)}, bf16[136,128]{1,0:T(8,128)(2,1)S(1)}, u32[]{:S(2)}, u32[]{:S(2)}) collective-permute-start(bf16[136,128]{1,0:T(8,128)(2,1)S(1)} %add_convert_fusion), channel_id=1, source_target_pairs={{0,192},{1,193},{2,194},{3,195},{4,196},{5,197},{6,198},{7,199},{8... | collective-permute-start | bytes 104456 | tf_op jit(solution)/shard_map/ppermute | solution.py:37
  84.4 6.4 %collective-permute-start.27 = (f32[136,128]{1,0:T(8,128)S(1)}, f32[136,128]{1,0:T(8,128)S(1)}, u32[]{:S(2)}, u32[]{:S(2)}) collective-permute-start(f32[136,128]{1,0:T(8,128)S(1)} %add_add_fusion), channel_id=1, source_target_pairs={{0,1},{1,0},{2,3},{3,2},{4,5},{5,4},{6,7},{7,6},{8,9},{9,8},{10,11... | collective-permute-start | bytes 208904 | tf_op jit(solution)/shard_map/ppermute | solution.py:37
